TPU v7x, 32 devices: a whole 2x2x4 slice. The times are simulated.
32 devices in a mesh: grp: 2 (over y), shard: 16 (over z, x, core).
Axes of the slice: x: 2, y: 2, z: 4, core: 2. Of those that a mesh axis runs over, the one named last changes fastest.
Arguments:
- query_rows: bfloat16 [8192, 1024], P(('grp', 'shard')), may hold values from -6 to 6
- key_rows: bfloat16 [8192, 1024], P(('grp', 'shard')), may hold values from -6 to 6
- value_rows: bfloat16 [8192, 1024], P(('grp', 'shard')), may hold values from -6 to 6
- grad_out: bfloat16 [8192, 1024], P(('grp', 'shard')), may hold values from -6 to 6
Outputs:
- attended: bfloat16 [8192, 1024], P(('grp', 'shard'))
- grad_query: bfloat16 [8192, 1024], P(('grp', 'shard'))
- grad_key: bfloat16 [8192, 1024], P(('grp', 'shard'))
- grad_value: bfloat16 [8192, 1024], P(('grp', 'shard'))
All inputs are finite; a program needn't handle non-finite values.
Results may differ from a plain program's by a relative error of at most 0.012.
Values may be sent and summed in bfloat16 or wider, within the bound.
No kernel may reach another device: no remote copies, remote signals or barrier semaphores. Data moves between devices by JAX's collectives and lax.ppermute only.
A program may use at most 256 MiB of HBM per device.

v0:
```python
import jax
import jax.numpy as jnp
from jax import lax
from jax.sharding import PartitionSpec as P

HD = 128


def entering(array, axis, join, neutral, backward):
    count = lax.axis_size(axis)
    place = lax.axis_index(axis)
    ahead = count - 1 - place if backward else place
    gathered = lax.all_gather(array.astype(jnp.bfloat16), axis)
    state = jnp.zeros_like(array) + jnp.asarray(neutral, array.dtype)

    def one(step, state):
        source = count - 1 - step if backward else step
        return join(state, lax.dynamic_index_in_dim(gathered, source, 0, False).astype(array.dtype))

    return lax.fori_loop(0, ahead, one, state)


def add_states(earlier, later_part):
    return earlier + later_part


def prefix_states(local_state, backward):
    empty_state = jnp.zeros_like(local_state)
    inside = entering(local_state, "shard", add_states, empty_state, backward)
    group_sum = lax.psum(local_state, "shard")
    outside = entering(group_sum, "grp", add_states, empty_state, backward)
    return inside + outside


def body(query_rows, key_rows, value_rows, grad_out):
    row_count = query_rows.shape[0]
    head_size = HD
    head_count = query_rows.shape[1] // head_size
    query_heads = query_rows.reshape(row_count, head_count, head_size)
    key_heads = key_rows.reshape(row_count, head_count, head_size)
    value_heads = value_rows.reshape(row_count, head_count, head_size)
    rows_at = lax.broadcasted_iota(jnp.int32, (row_count, row_count), 0)
    cols_at = lax.broadcasted_iota(jnp.int32, (row_count, row_count), 1)
    causal = (rows_at >= cols_at)[None]
    block_state = jnp.einsum(
        "thd,the->hde", key_heads, value_heads, preferred_element_type=jnp.float32
    )
    earlier = prefix_states(block_state, False)
    scores = jnp.einsum("thd,shd->hts", query_heads, key_heads, preferred_element_type=jnp.float32)
    local_scores = jnp.where(causal, scores, 0.0).astype(jnp.bfloat16)
    local_mixed = jnp.einsum(
        "hts,she->the", local_scores, value_heads, preferred_element_type=jnp.float32
    )
    earlier_rounded = earlier.astype(jnp.bfloat16)
    mixed_rows = local_mixed + jnp.einsum(
        "thd,hde->the", query_heads, earlier_rounded, preferred_element_type=jnp.float32
    )
    inv_rms = lax.rsqrt(jnp.mean(mixed_rows * mixed_rows, axis=-1, keepdims=True) + 1.0)
    normed = mixed_rows * inv_rms
    attended = normed.astype(jnp.bfloat16).reshape(row_count, head_count * head_size)
    grad_heads = grad_out.reshape(row_count, head_count, head_size).astype(jnp.float32)
    grad_mixed = (
        (grad_heads - normed * jnp.mean(grad_heads * normed, axis=-1, keepdims=True)) * inv_rms
    ).astype(jnp.bfloat16)
    block_reverse = jnp.einsum(
        "thd,the->hde", query_heads, grad_mixed, preferred_element_type=jnp.float32
    )
    later_sum = prefix_states(block_reverse, True)
    grad_raw = jnp.einsum(
        "the,she->hts", grad_mixed, value_heads, preferred_element_type=jnp.float32
    )
    grad_scores = jnp.where(causal, grad_raw, 0.0).astype(jnp.bfloat16)
    grad_query = jnp.einsum(
        "hts,shd->thd", grad_scores, key_heads, preferred_element_type=jnp.float32
    )
    grad_query = grad_query + jnp.einsum(
        "the,hde->thd", grad_mixed, earlier_rounded, preferred_element_type=jnp.float32
    )
    key_local = jnp.einsum(
        "hts,thd->shd", grad_scores, query_heads, preferred_element_type=jnp.float32
    )
    value_local = jnp.einsum(
        "hts,the->she", local_scores, grad_mixed, preferred_element_type=jnp.float32
    )
    later_rounded = later_sum.astype(jnp.bfloat16)
    grad_key = key_local + jnp.einsum(
        "she,hde->shd", value_heads, later_rounded, preferred_element_type=jnp.float32
    )
    grad_value = value_local + jnp.einsum(
        "shd,hde->she", key_heads, later_rounded, preferred_element_type=jnp.float32
    )
    flat_width = head_count * head_size
    return (
        attended,
        grad_query.astype(jnp.bfloat16).reshape(row_count, flat_width),
        grad_key.astype(jnp.bfloat16).reshape(row_count, flat_width),
        grad_value.astype(jnp.bfloat16).reshape(row_count, flat_width),
    )


def solution(mesh):
    in_specs = (
        P(("grp", "shard"), None),
        P(("grp", "shard"), None),
        P(("grp", "shard"), None),
        P(("grp", "shard"), None),
    )
    out_specs = (
        P(("grp", "shard"), None),
        P(("grp", "shard"), None),
        P(("grp", "shard"), None),
        P(("grp", "shard"), None),
    )
    return jax.shard_map(body, mesh=mesh, in_specs=in_specs, out_specs=out_specs, check_vma=False)
```

profile of v0, /device:TPU:0, one launch (start us, length us, event | category | flops | bytes accessed | tf_op | source)
XLA Modules:
  0.0 227.0 jit_solution(15674418484396753839)
XLA Ops:
  7.2 0.0 copy-start
  7.2 0.0 copy-start.3
  7.2 0.0 all-gather.7.cloned.1.call-start
  7.2 1.2 copy.61
  8.5 0.3 copy.34
  8.8 0.0 copy-done.3
  8.8 0.0 copy-start.1
  8.8 1.0 fusion.27
  9.8 0.0 all-gather.7.cloned.1.call-update
  9.8 0.0 all-gather.9.cloned.1.call-start
  9.9 1.2 copy.38
  11.2 72.2 %all-reduce.2 = bf16[8,128,128]{2,1,0:T(8,128)(2,1)S(1)} all-reduce(f32[8,128,128]{2,1,0:T(8,128)S(1)} %get-tuple-element.217), channel_id=1, replica_groups=mesh['grp'=2,'shard'=16] {'shard'}, use_global_device_ids=true, to_apply=%region_2.3 | all-reduce | flops 131072 | bytes 786432 | tf_op jit(solution)/shard_map/psum | solution.py:30
  83.4 0.0 copy-done.1
  83.4 7.0 %all-gather.1 = bf16[16,128,128]{2,1,0:T(8,128)(2,1)S(1)} all-gather(bf16[8,128,128]{2,1,0:T(8,128)(2,1)S(1)} %all-reduce.2), channel_id=3, replica_groups=mesh['grp'=2,'shard'=16] {'grp'}, dimensions={0}, use_global_device_ids=true | all-gather | bytes 786432 | tf_op jit(solution)/shard_map/all_gather | solution.py:13
  90.5 0.0 copy-done
  90.5 1.5 select_convert_fusion.1
  92.0 0.0 copy-start.5
  92.0 1.5 convolution_bitcast_fusion.5
  93.4 0.0 copy-done.5
  93.5 0.0 all-gather.7.cloned.1.call-done
  93.6 0.1 add_convert_fusion.1
  93.7 1.6 multiply_reduce_fusion.1
  95.3 0.2 multiply_reduce_fusion
  95.4 0.2 multiply_convert_fusion
  95.7 0.0 copy-start.4
  95.7 1.0 fusion.28
  96.7 1.8 copy.45
  98.5 0.0 all-gather.9.cloned.1.call-update
  98.6 85.0 %all-reduce.3 = bf16[8,128,128]{1,2,0:T(8,128)(2,1)} all-reduce(f32[8,128,128]{1,2,0:T(8,128)S(1)} %get-tuple-element.221), channel_id=1, replica_groups=mesh['grp'=2,'shard'=16] {'shard'}, use_global_device_ids=true, to_apply=%region_9.10 | all-reduce | flops 131072 | bytes 786432 | tf_op jit(solution)/shard_map/psum | solution.py:30
  183.6 1.1 copy.46
  184.7 0.0 copy-done.4
  184.7 0.5 select_convert_fusion
  185.2 0.5 convolution_bitcast_fusion.4
  185.7 0.3 fusion.3
  186.0 0.2 copy-done.7
  186.2 1.0 copy.51
  187.2 1.0 copy.50
  188.2 7.2 %all-gather.3 = bf16[16,128,128]{2,1,0:T(8,128)(2,1)S(1)} all-gather(bf16[8,128,128]{2,1,0:T(8,128)(2,1)S(1)} %copy.46), channel_id=5, replica_groups=mesh['grp'=2,'shard'=16] {'grp'}, dimensions={0}, use_global_device_ids=true | all-gather | bytes 786432 | tf_op jit(solution)/shard_map/all_gather | solution.py:13
  195.4 2.5 %fusion.29 = f32[8,128,256]{2,1,0:T(8,128)} fusion(bf16[256,8,128]{0,2,1:T(8,128)(2,1)S(1)} %get-tuple-element.214, bf16[8,256,256]{2,1,0:T(8,128)(2,1)} %copy-done.5), kind=kOutput, calls=%fused_computation.52 | convolution fusion | flops 134217728 | bytes 2621440 | tf_op jit(solution)/shard_map/hts,the->she/dot_general | solution.py:82
  197.9 1.3 convolution_bitcast_fusion.3
  199.3 0.2 while.47
  199.3 0.1 convert_add_fusion.11
  199.4 0.0 all-gather.9.cloned.1.call-done
  199.5 16.5 %while.46 = (s32[]{:T(128)}, f32[8,128,128]{2,1,0:T(8,128)S(1)}, s32[]{:T(128)}, bf16[16,8,128,128]{3,2,1,0:T(8,128)(2,1)}, s32[]{:T(128)}, /*index=5*/s32[]{:T(128)}, s32[]{:T(128)}, s32[]{:T(128)}) while((s32[]{:T(128)}, f32[8,128,128]{2,1,0:T(8,128)S(1)}, s32[]{:T(128)}, bf16[16,8,128,128]{3,2,1,0:T(8,128)(2,1)}, s32[]{:T(128)}, ...), condition=%wide.region_8.9_spmd, body=%wide.region_7.8_spmd.sunk | while | flops 262150 | bytes 1310855 | solution.py:20
  199.5 1.1 convert_add_fusion.10
  200.6 1.1 convert_add_fusion.10
  201.7 1.1 convert_add_fusion.10
  202.8 1.1 convert_add_fusion.10
  203.9 1.1 convert_add_fusion.10
  205.0 1.1 convert_add_fusion.10
  206.1 1.1 convert_add_fusion.10
  207.2 1.1 convert_add_fusion.10
  208.3 1.1 convert_add_fusion.10
  209.4 1.1 convert_add_fusion.10
  210.5 1.1 convert_add_fusion.10
  211.6 1.1 convert_add_fusion.10
  212.7 1.1 convert_add_fusion.10
  213.8 1.1 convert_add_fusion.10
  214.9 1.1 convert_add_fusion.10
  216.0 0.1 add_convert_fusion
  216.0 1.8 fusion.5
  217.8 1.0 copy.53
  218.9 0.3 fusion.4
  219.2 1.0 copy.52
  (16 shorter events, 0.2 us)
Async XLA Ops:
  7.2 83.3 %copy-start = (bf16[256,1024]{1,0:T(8,128)(2,1)S(1)}, bf16[256,1024]{1,0:T(8,128)(2,1)}, u32[]{:S(2)}) copy-start(bf16[256,1024]{1,0:T(8,128)(2,1)} %param.12) | copy-start | bytes 1572868
  7.2 1.6 copy-start.3
  7.2 86.3 %all-gather.7.cloned.1.call-start = ((), (), s32[]{:S(2)}) async-start(), calls=%async_computation | async-start | bytes 4456448 | tf_op jit(solution)/shard_map/all_gather | solution.py:13
  8.8 74.6 %copy-start.1 = (bf16[256,8,128]{0,2,1:T(8,128)(2,1)}, bf16[256,8,128]{0,2,1:T(8,128)(2,1)S(1)}, u32[]{:S(2)}) copy-start(bf16[256,8,128]{0,2,1:T(8,128)(2,1)S(1)} %copy.34) | copy-start | bytes 1572868
  9.8 189.6 %all-gather.9.cloned.1.call-start = ((), (), s32[]{:S(2)}) async-start(), calls=%async_computation.1 | async-start | bytes 4456448 | tf_op jit(solution)/shard_map/all_gather | solution.py:13
  92.0 1.5 copy-start.5
  95.7 89.0 %copy-start.4 = (bf16[256,1024]{1,0:T(8,128)(2,1)S(1)}, bf16[256,1024]{1,0:T(8,128)(2,1)}, u32[]{:S(2)}) copy-start(bf16[256,1024]{1,0:T(8,128)(2,1)} %param.14) | copy-start | bytes 1572868
  96.7 88.5 %copy-start.2 = (bf16[256,8,128]{0,2,1:T(8,128)(2,1)S(1)}, bf16[256,8,128]{0,2,1:T(8,128)(2,1)}, u32[]{:S(2)}) copy-start(bf16[256,8,128]{0,2,1:T(8,128)(2,1)} %copy-done.1) | copy-start | bytes 1572868
  185.2 1.0 copy-start.7
  188.2 9.7 %copy-start.8 = (bf16[8,256,256]{2,1,0:T(8,128)(2,1)S(1)}, bf16[8,256,256]{2,1,0:T(8,128)(2,1)}, u32[]{:S(2)}) copy-start(bf16[8,256,256]{2,1,0:T(8,128)(2,1)} %copy-done.7) | copy-start | bytes 3145732
  216.0 2.9 %copy-start.6 = (f32[256,8,128]{0,2,1:T(8,128)S(1)}, f32[256,8,128]{0,2,1:T(8,128)}, u32[]{:S(2)}) copy-start(f32[256,8,128]{0,2,1:T(8,128)} %convolution_bitcast_fusion.3) | copy-start | bytes 3145732
Sparse Core Ops, SparseCore 0:
  10.8 56.6 all-gather.6
  98.7 67.9 all-gather.8
where the time goes:
time: 228 us; the launch traced here: 227 us
  blocking collectives  171 us (75%)
  other arithmetic  16.7 us (7%)
  between operations  14.3 us (6%)
  matrix products  13.7 us (6%)
  local copies, waits for them, and re-layouts  10.2 us (4%)
    psum x2, blocking collectives, prefix_states(): group_sum = lax.psum(local_state, 'shard')  157 us
    add x16, other arithmetic, add_states(): return earlier + later_part  16.2 us
    all_gather x2, blocking collectives, entering(): gathered = lax.all_gather(array.astype(jnp.bfloat16), axis)  14.2 us
    unnamed x23, local copies, waits for them, and re-layouts  5.49 us
  transfers between devices with their start and end apart: 2, of which 0 were waited for; matrix products, arithmetic and copies ran while one was open for 6% of the time, Pallas kernels for 0%

commit v1 on v0

v1 whole, which is shorter than its diff:
```python
import functools

import jax
import jax.numpy as jnp
from jax import lax
from jax.experimental import pallas as pl
from jax.experimental.pallas import tpu as pltpu
from jax.sharding import PartitionSpec as P

HD = 128
AXES = ("grp", "shard")
F32 = jnp.float32
BF16 = jnp.bfloat16


def dot_nn(a, b):
    return lax.dot_general(a, b, (((1,), (0,)), ((), ())), preferred_element_type=F32)


def dot_nt(a, b):
    return lax.dot_general(a, b, (((1,), (1,)), ((), ())), preferred_element_type=F32)


def dot_tn(a, b):
    return lax.dot_general(a, b, (((0,), (0,)), ((), ())), preferred_element_type=F32)


def columns(head):
    start = head * HD
    if not isinstance(head, int):
        start = pl.multiple_of(start, HD)
    return pl.ds(start, HD)


def call(kernel, out_shapes, flops, *args):
    smem = pl.BlockSpec(memory_space=pltpu.SMEM)
    vmem = pl.BlockSpec(memory_space=pltpu.VMEM)
    size = sum(a.size * a.dtype.itemsize for a in (*args, *out_shapes))
    return pl.pallas_call(
        kernel,
        out_shape=out_shapes,
        in_specs=[smem if a.dtype == jnp.int32 else vmem for a in args],
        out_specs=[vmem] * len(out_shapes),
        compiler_params=pltpu.CompilerParams(vmem_limit_bytes=32 * 1024 * 1024),
        cost_estimate=pl.CostEstimate(flops=flops, bytes_accessed=size, transcendentals=0),
    )(*args)


def state_kernel(half, core_ref, k_ref, v_ref, own_ref, send_ref):
    core = core_ref[0]
    for j in range(half):
        cols = columns((1 - core) * half + j)
        send_ref[j] = dot_tn(k_ref[:, cols], v_ref[:, cols]).astype(BF16)
    for j in range(half):
        cols = columns(core * half + j)
        own_ref[j] = dot_tn(k_ref[:, cols], v_ref[:, cols])


def lower(rows):
    return lax.broadcasted_iota(jnp.int32, (rows, rows), 0) >= lax.broadcasted_iota(
        jnp.int32, (rows, rows), 1
    )


def upper(rows):
    return lax.broadcasted_iota(jnp.int32, (rows, rows), 0) <= lax.broadcasted_iota(
        jnp.int32, (rows, rows), 1
    )


def local_kernel(heads, q_ref, k_ref, v_ref, mixed_ref, qt_ref):
    mask = lower(q_ref.shape[0])
    for h in range(heads):
        cols = columns(h)
        q = q_ref[:, cols]
        scores = jnp.where(mask, dot_nt(q, k_ref[:, cols]), 0.0).astype(BF16)
        mixed_ref[:, cols] = dot_nn(scores, v_ref[:, cols])
        qt_ref[h] = q.T


def norm_kernel(half, core_ref, q_ref, g_ref, qt_ref, mixed_ref, eown_ref, eother_ref, att_ref, gm_ref, own_ref, send_ref):
    core = core_ref[0]
    for mine, state_ref in ((0, eother_ref), (1, eown_ref)):
        for j in range(half):
            head = (core if mine else 1 - core) * half + j
            cols = columns(head)
            mixed = mixed_ref[:, cols] + dot_nn(q_ref[:, cols], state_ref[j])
            inv_rms = lax.rsqrt(jnp.mean(mixed * mixed, axis=-1, keepdims=True) + 1.0)
            normed = mixed * inv_rms
            att_ref[:, cols] = normed.astype(BF16)
            g = g_ref[:, cols].astype(F32)
            gm = ((g - normed * jnp.mean(g * normed, axis=-1, keepdims=True)) * inv_rms).astype(BF16)
            gm_ref[:, cols] = gm
            state = dot_nn(qt_ref[head], gm)
            if mine:
                own_ref[j] = state
            else:
                send_ref[j] = state.astype(BF16)


def grads_kernel(half, core_ref, q_ref, k_ref, v_ref, gm_ref, eown_ref, eother_ref, gq_ref, kl_ref, vl_ref):
    core = core_ref[0]
    rows = q_ref.shape[0]
    low = lower(rows)
    upp = upper(rows)
    for mine, state_ref in ((0, eother_ref), (1, eown_ref)):
        for j in range(half):
            cols = columns((core if mine else 1 - core) * half + j)
            q = q_ref[:, cols]
            k = k_ref[:, cols]
            v = v_ref[:, cols]
            gm = gm_ref[:, cols]
            gs = jnp.where(low, dot_nt(gm, v), 0.0).astype(BF16)
            gq_ref[:, cols] = (dot_nn(gs, k) + dot_nt(gm, state_ref[j])).astype(BF16)
            gst = jnp.where(upp, dot_nt(v, gm), 0.0).astype(BF16)
            kl_ref[:, cols] = dot_nn(gst, q)
            lst = jnp.where(upp, dot_nt(k, q), 0.0).astype(BF16)
            vl_ref[:, cols] = dot_nn(lst, gm)


def last_kernel(half, core_ref, k_ref, v_ref, kl_ref, vl_ref, lown_ref, lother_ref, gk_ref, gv_ref):
    core = core_ref[0]
    for mine, state_ref in ((0, lother_ref), (1, lown_ref)):
        for j in range(half):
            cols = columns((core if mine else 1 - core) * half + j)
            later = state_ref[j]
            gk_ref[:, cols] = (kl_ref[:, cols] + dot_nt(v_ref[:, cols], later)).astype(BF16)
            gv_ref[:, cols] = (vl_ref[:, cols] + dot_nn(k_ref[:, cols], later)).astype(BF16)


def swap(array, bit, count):
    return lax.ppermute(array, AXES, [(i, i ^ bit) for i in range(count)])


def scan_states(own, send, place, count, backward):
    def before(bit):
        is_set = (place & bit) != 0
        return ~is_set if backward else is_set

    from_core = swap(send, 1, count).astype(F32)
    total = own + from_core
    entering = jnp.zeros_like(own)
    bit = 2
    while bit < count:
        arrived = swap(total.astype(BF16), bit, count).astype(F32)
        entering = entering + jnp.where(before(bit), arrived, 0.0)
        total = total + arrived
        bit *= 2
    mine = entering + jnp.where(before(1), from_core, 0.0)
    theirs = entering + jnp.where(before(1), 0.0, own)
    return mine.astype(BF16), swap(theirs.astype(BF16), 1, count)


def body(query_rows, key_rows, value_rows, grad_out):
    rows, width = query_rows.shape
    heads = width // HD
    half = heads // 2
    count = lax.axis_size("grp") * lax.axis_size("shard")
    place = lax.axis_index(AXES)
    core = (place & 1).astype(jnp.int32).reshape(1)
    part = jax.ShapeDtypeStruct((half, HD, HD), F32)
    part16 = jax.ShapeDtypeStruct((half, HD, HD), BF16)
    full = jax.ShapeDtypeStruct((rows, width), F32)
    full16 = jax.ShapeDtypeStruct((rows, width), BF16)
    turned = jax.ShapeDtypeStruct((heads, HD, rows), BF16)
    work = 2 * rows * width * HD
    scores = 2 * rows * width * rows

    own, send = call(
        functools.partial(state_kernel, half), (part, part16), work, core, key_rows, value_rows
    )
    e_own, e_other = scan_states(own, send, place, count, False)
    mixed, q_turned = call(
        functools.partial(local_kernel, heads), (full, turned), 2 * scores, query_rows, key_rows, value_rows
    )
    attended, grad_mixed, own, send = call(
        functools.partial(norm_kernel, half),
        (full16, full16, part, part16),
        2 * work,
        core, query_rows, grad_out, q_turned, mixed, e_own, e_other,
    )
    l_own, l_other = scan_states(own, send, place, count, True)
    grad_query, key_local, value_local = call(
        functools.partial(grads_kernel, half),
        (full16, full, full),
        6 * scores + work,
        core, query_rows, key_rows, value_rows, grad_mixed, e_own, e_other,
    )
    grad_key, grad_value = call(
        functools.partial(last_kernel, half),
        (full16, full16),
        2 * work,
        core, key_rows, value_rows, key_local, value_local, l_own, l_other,
    )
    return attended, grad_query, grad_key, grad_value


def solution(mesh):
    spec = P(AXES, None)
    return jax.shard_map(
        body, mesh=mesh, in_specs=(spec,) * 4, out_specs=(spec,) * 4, check_vma=False
    )
```

time: 228 us -> 62.8 us (0.28)
  blocking collectives: 171 us -> 0 us
  waiting for transfers between devices: 0.07 us -> 37.1 us
  other arithmetic: 16.7 us -> 0.77 us
  starting transfers between devices: 0.08 us -> 14.1 us
  matrix products: 13.7 us -> 0 us
  between operations: 14.3 us -> 0.75 us
  local copies, waits for them, and re-layouts: 10.2 us -> 2.1 us
  Pallas kernels: 0 us -> 7.74 us
    psum x2 -> x0, blocking collectives: 157 us -> none  [prefix_states(): group_sum = lax.psum(local_state, 'shard')]
    ppermute x0 -> x12, waiting for transfers between devices: none -> 37.1 us  [swap(): return lax.ppermute(array, AXES, [(i, i ^ bit) for i in range(count)])]
    add x16 -> x0, other arithmetic: 16.2 us -> none  [add_states(): return earlier + later_part]
    all_gather x2 -> x0, blocking collectives: 14.2 us -> none  [entering(): gathered = lax.all_gather(array.astype(jnp.bfloat16), axis)]
    ppermute x0 -> x12, starting transfers between devices: none -> 14.1 us  [swap(): return lax.ppermute(array, AXES, [(i, i ^ bit) for i in range(count)])]
    dot_general x12 -> x0, matrix products: 13.7 us -> none  [the longest x1 2.5 us: body(): jnp.einsum('hts,the->she', local_scores, grad_mixed, preferred_element_ty...]
    pallas_call x0 -> x5, Pallas kernels: none -> 7.74 us  [call(): pl.pallas_call(kernel, out_shape=out_shapes, in_specs=[smem if a.dtype ==...]
    convert_element_type x3 -> x0, local copies, waits for them, and re-layouts: 4.2 us -> none  [the longest x2 2.95 us: entering(): gathered = lax.all_gather(array.astype(jnp.bfloat16), axis)]
  transfers between devices with their start and end apart: 2 -> 12, of which waited for: 0 -> 11; matrix products, arithmetic and copies ran while one was open for 6% -> 0% of each run, Pallas kernels for 0% -> 7%
where the time goes in v1:
time: 62.8 us; the launch traced here: 62.5 us
  waiting for transfers between devices  37.1 us (59%)
  starting transfers between devices  14.1 us (22%)
  Pallas kernels  7.74 us (12%)
  local copies, waits for them, and re-layouts  2.1 us (3%)
  other arithmetic  0.77 us (1%)
  between operations  0.75 us (1%)
    ppermute x12, waiting for transfers between devices, swap(): return lax.ppermute(array, AXES, [(i, i ^ bit) for i in range(count)])  37.1 us
    ppermute x12, starting transfers between devices, swap(): return lax.ppermute(array, AXES, [(i, i ^ bit) for i in range(count)])  14.1 us
    pallas_call x5, Pallas kernels, call(): pl.pallas_call(kernel, out_shape=out_shapes, in_specs=[smem if a.dtype ==...  7.74 us
    unnamed x12, local copies, waits for them, and re-layouts  2.1 us
  transfers between devices with their start and end apart: 12, of which 11 were waited for; matrix products, arithmetic and copies ran while one was open for 0% of the time, Pallas kernels for 7%

profile of v1, /device:TPU:0, one launch (start us, length us, event | category | flops | bytes accessed | tf_op | source)
XLA Modules:
  0.0 62.5 jit_solution(4370081457720008063)
XLA Ops:
  0.6 0.0 copy-start
  0.6 1.0 %copy-done = bf16[256,1024]{1,0:T(8,128)(2,1)S(1)} copy-done((bf16[256,1024]{1,0:T(8,128)(2,1)S(1)}, bf16[256,1024]{1,0:T(8,128)(2,1)}, u32[]{:S(2)}) %copy-start) | copy-done | bytes 524312
  1.7 0.0 copy-start.2
  1.7 1.0 %copy-done.2 = bf16[256,1024]{1,0:T(8,128)(2,1)S(1)} copy-done((bf16[256,1024]{1,0:T(8,128)(2,1)S(1)}, bf16[256,1024]{1,0:T(8,128)(2,1)}, u32[]{:S(2)}) %copy-start.2) | copy-done | bytes 524312
  2.7 0.5 shard_map.76
  3.2 0.5 collective-permute-start
  3.7 1.0 %collective-permute-done = bf16[4,128,128]{2,1,0:T(8,128)(2,1)S(1)} collective-permute-done((bf16[4,128,128]{2,1,0:T(8,128)(2,1)S(1)}, bf16[4,128,128]{2,1,0:T(8,128)(2,1)S(1)}, u32[]{:S(2)}, u32[]{:S(2)}) %collective-permute-start) | collective-permute-done | bytes 131104 | tf_op jit(solution)/shard_map/ppermute | solution.py:132
  4.7 2.9 %collective-permute-start.1 = (bf16[4,128,128]{2,1,0:T(8,128)(2,1)S(1)}, bf16[4,128,128]{2,1,0:T(8,128)(2,1)S(1)}, u32[]{:S(2)}, u32[]{:S(2)}) collective-permute-start(bf16[4,128,128]{2,1,0:T(8,128)(2,1)S(1)} %fusion.12), channel_id=1, source_target_pairs={{0,2},{1,3},{2,0},{3,1},{4,6},{5,7},{6,4},{7,5},{8,10},{9,11},{10,... | collective-permute-start | bytes 393224 | tf_op jit(solution)/shard_map/ppermute | solution.py:132
  7.7 3.8 %collective-permute-done.1 = bf16[4,128,128]{2,1,0:T(8,128)(2,1)S(1)} collective-permute-done((bf16[4,128,128]{2,1,0:T(8,128)(2,1)S(1)}, bf16[4,128,128]{2,1,0:T(8,128)(2,1)S(1)}, u32[]{:S(2)}, u32[]{:S(2)}) %collective-permute-start.1) | collective-permute-done | bytes 131104 | tf_op jit(solution)/shard_map/ppermute | solution.py:132
  11.5 1.9 %collective-permute-start.2 = (bf16[4,128,128]{2,1,0:T(8,128)(2,1)S(1)}, bf16[4,128,128]{2,1,0:T(8,128)(2,1)S(1)}, u32[]{:S(2)}, u32[]{:S(2)}) collective-permute-start(bf16[4,128,128]{2,1,0:T(8,128)(2,1)S(1)} %fusion.16), channel_id=1, source_target_pairs={{0,4},{1,5},{2,6},{3,7},{4,0},{5,1},{6,2},{7,3},{8,12},{9,13},{10,... | collective-permute-start | bytes 393224 | tf_op jit(solution)/shard_map/ppermute | solution.py:132
  13.4 3.2 %collective-permute-done.2 = bf16[4,128,128]{2,1,0:T(8,128)(2,1)S(1)} collective-permute-done((bf16[4,128,128]{2,1,0:T(8,128)(2,1)S(1)}, bf16[4,128,128]{2,1,0:T(8,128)(2,1)S(1)}, u32[]{:S(2)}, u32[]{:S(2)}) %collective-permute-start.2) | collective-permute-done | bytes 131104 | tf_op jit(solution)/shard_map/ppermute | solution.py:132
  16.6 0.1 fusion.13
  16.7 2.8 %collective-permute-start.3 = (bf16[4,128,128]{2,1,0:T(8,128)(2,1)S(1)}, bf16[4,128,128]{2,1,0:T(8,128)(2,1)S(1)}, u32[]{:S(2)}, u32[]{:S(2)}) collective-permute-start(bf16[4,128,128]{2,1,0:T(8,128)(2,1)S(1)} %fusion.13), channel_id=1, source_target_pairs={{0,8},{1,9},{2,10},{3,11},{4,12},{5,13},{6,14},{7,15},{8,0},{9,1},... | collective-permute-start | bytes 393224 | tf_op jit(solution)/shard_map/ppermute | solution.py:132
  19.5 5.1 %collective-permute-done.3 = bf16[4,128,128]{2,1,0:T(8,128)(2,1)S(1)} collective-permute-done((bf16[4,128,128]{2,1,0:T(8,128)(2,1)S(1)}, bf16[4,128,128]{2,1,0:T(8,128)(2,1)S(1)}, u32[]{:S(2)}, u32[]{:S(2)}) %collective-permute-start.3) | collective-permute-done | bytes 131104 | tf_op jit(solution)/shard_map/ppermute | solution.py:132
  24.6 0.0 copy-start.4
  24.6 0.1 fusion.5
  24.7 1.2 %collective-permute-start.4 = (bf16[4,128,128]{2,1,0:T(8,128)(2,1)S(1)}, bf16[4,128,128]{2,1,0:T(8,128)(2,1)S(1)}, u32[]{:S(2)}, u32[]{:S(2)}) collective-permute-start(bf16[4,128,128]{2,1,0:T(8,128)(2,1)S(1)} %fusion.5), channel_id=1, source_target_pairs={{0,16},{1,17},{2,18},{3,19},{4,20},{5,21},{6,22},{7,23},{8,24},{9,... | collective-permute-start | bytes 393224 | tf_op jit(solution)/shard_map/ppermute | solution.py:132
  25.9 0.0 copy-start.1
  25.9 0.0 copy-start.3
  25.9 3.8 %collective-permute-done.4 = bf16[4,128,128]{2,1,0:T(8,128)(2,1)S(1)} collective-permute-done((bf16[4,128,128]{2,1,0:T(8,128)(2,1)S(1)}, bf16[4,128,128]{2,1,0:T(8,128)(2,1)S(1)}, u32[]{:S(2)}, u32[]{:S(2)}) %collective-permute-start.4) | collective-permute-done | bytes 131104 | tf_op jit(solution)/shard_map/ppermute | solution.py:132
  29.7 0.2 add_convert_fusion.1
  29.9 0.0 copy-start.5
  29.9 0.1 collective-permute-start.5
  30.0 0.0 copy-done.4
  30.0 0.0 copy-done.1
  30.0 0.0 copy-done.3
  30.0 0.9 %shard_map.75 = (f32[256,1024]{1,0:T(8,128)S(1)}, bf16[8,128,256]{2,1,0:T(8,128)(2,1)S(1)}) custom-call(bf16[256,1024]{1,0:T(8,128)(2,1)S(1)} %copy-done.4, bf16[256,1024]{1,0:T(8,128)(2,1)S(1)} %copy-done.1, bf16[256,1024]{1,0:T(8,128)(2,1)S(1)} %copy-done.3), custom_call_target="tpu_custom_call" | custom-call | flops 268435456 | bytes 3145728 | tf_op jit(solution)/shard_map/pallas_call | solution.py:39
  30.9 0.4 collective-permute-done.5.eother_ref
  31.3 0.0 copy-done.5
  31.3 1.6 %shard_map.77 = (bf16[256,1024]{1,0:T(8,128)(2,1)}, bf16[256,1024]{1,0:T(8,128)(2,1)S(1)}, f32[4,128,128]{2,1,0:T(8,128)S(1)}, bf16[4,128,128]{2,1,0:T(8,128)(2,1)S(1)}) custom-call(s32[1]{0:T(128)} %bitcast.core_ref, bf16[256,1024]{1,0:T(8,128)(2,1)S(1)} %copy-done.4, bf16[256,1024]{1,0:T(8,128)(2,1)S(1)} %copy-done.5, ...), custom_call_target="tpu_custom_call" | custom-call | flops 134217728 | bytes 4325380 | tf_op jit(solution)/shard_map/pallas_call | solution.py:39
  32.9 0.2 collective-permute-start.6
  33.1 1.2 %collective-permute-done.6 = bf16[4,128,128]{2,1,0:T(8,128)(2,1)S(1)} collective-permute-done((bf16[4,128,128]{2,1,0:T(8,128)(2,1)S(1)}, bf16[4,128,128]{2,1,0:T(8,128)(2,1)S(1)}, u32[]{:S(2)}, u32[]{:S(2)}) %collective-permute-start.6) | collective-permute-done | bytes 131104 | tf_op jit(solution)/shard_map/ppermute | solution.py:132
  34.3 1.2 %collective-permute-start.7 = (bf16[4,128,128]{2,1,0:T(8,128)(2,1)S(1)}, bf16[4,128,128]{2,1,0:T(8,128)(2,1)S(1)}, u32[]{:S(2)}, u32[]{:S(2)}) collective-permute-start(bf16[4,128,128]{2,1,0:T(8,128)(2,1)S(1)} %fusion.14), channel_id=1, source_target_pairs={{0,2},{1,3},{2,0},{3,1},{4,6},{5,7},{6,4},{7,5},{8,10},{9,11},{10,... | collective-permute-start | bytes 393224 | tf_op jit(solution)/shard_map/ppermute | solution.py:132
  35.5 4.5 %collective-permute-done.7 = bf16[4,128,128]{2,1,0:T(8,128)(2,1)S(1)} collective-permute-done((bf16[4,128,128]{2,1,0:T(8,128)(2,1)S(1)}, bf16[4,128,128]{2,1,0:T(8,128)(2,1)S(1)}, u32[]{:S(2)}, u32[]{:S(2)}) %collective-permute-start.7) | collective-permute-done | bytes 131104 | tf_op jit(solution)/shard_map/ppermute | solution.py:132
  40.0 0.3 collective-permute-start.8
  40.3 4.7 %collective-permute-done.8 = bf16[4,128,128]{2,1,0:T(8,128)(2,1)S(1)} collective-permute-done((bf16[4,128,128]{2,1,0:T(8,128)(2,1)S(1)}, bf16[4,128,128]{2,1,0:T(8,128)(2,1)S(1)}, u32[]{:S(2)}, u32[]{:S(2)}) %collective-permute-start.8) | collective-permute-done | bytes 131104 | tf_op jit(solution)/shard_map/ppermute | solution.py:132
  45.0 0.1 fusion.15
  45.1 1.7 %collective-permute-start.9 = (bf16[4,128,128]{2,1,0:T(8,128)(2,1)S(1)}, bf16[4,128,128]{2,1,0:T(8,128)(2,1)S(1)}, u32[]{:S(2)}, u32[]{:S(2)}) collective-permute-start(bf16[4,128,128]{2,1,0:T(8,128)(2,1)S(1)} %fusion.15), channel_id=1, source_target_pairs={{0,8},{1,9},{2,10},{3,11},{4,12},{5,13},{6,14},{7,15},{8,0},{9,1},... | collective-permute-start | bytes 393224 | tf_op jit(solution)/shard_map/ppermute | solution.py:132
  46.8 5.6 %collective-permute-done.9 = bf16[4,128,128]{2,1,0:T(8,128)(2,1)S(1)} collective-permute-done((bf16[4,128,128]{2,1,0:T(8,128)(2,1)S(1)}, bf16[4,128,128]{2,1,0:T(8,128)(2,1)S(1)}, u32[]{:S(2)}, u32[]{:S(2)}) %collective-permute-start.9) | collective-permute-done | bytes 131104 | tf_op jit(solution)/shard_map/ppermute | solution.py:132
  52.4 0.1 fusion.11
  52.5 1.2 %collective-permute-start.10 = (bf16[4,128,128]{2,1,0:T(8,128)(2,1)S(1)}, bf16[4,128,128]{2,1,0:T(8,128)(2,1)S(1)}, u32[]{:S(2)}, u32[]{:S(2)}) collective-permute-start(bf16[4,128,128]{2,1,0:T(8,128)(2,1)S(1)} %fusion.11), channel_id=1, source_target_pairs={{0,16},{1,17},{2,18},{3,19},{4,20},{5,21},{6,22},{7,23},{8,24},{9,... | collective-permute-start | bytes 393224 | tf_op jit(solution)/shard_map/ppermute | solution.py:132
  53.7 3.8 %collective-permute-done.10 = bf16[4,128,128]{2,1,0:T(8,128)(2,1)S(1)} collective-permute-done((bf16[4,128,128]{2,1,0:T(8,128)(2,1)S(1)}, bf16[4,128,128]{2,1,0:T(8,128)(2,1)S(1)}, u32[]{:S(2)}, u32[]{:S(2)}) %collective-permute-start.10) | collective-permute-done | bytes 131104 | tf_op jit(solution)/shard_map/ppermute | solution.py:132
  57.6 0.2 add_convert_fusion
  57.7 0.1 collective-permute-start.11
  57.8 3.2 %shard_map.78 = (bf16[256,1024]{1,0:T(8,128)(2,1)}, f32[256,1024]{1,0:T(8,128)S(1)}, f32[256,1024]{1,0:T(8,128)S(1)}) custom-call(s32[1]{0:T(128)} %bitcast.core_ref, bf16[256,1024]{1,0:T(8,128)(2,1)S(1)} %copy-done.4, bf16[256,1024]{1,0:T(8,128)(2,1)S(1)} %copy-done.1, bf16[256,1024]{1,0:T(8,128)(2,1)S(1)} %copy-done.3, ...), custom_call_target="tpu_custom_call" | custom-call | flops 872415232 | bytes 4980740 | tf_op jit(solution)/shard_map/pallas_call | solution.py:39
  61.0 0.0 collective-permute-done.11.lother_ref
  61.0 1.5 %shard_map.79 = (bf16[256,1024]{1,0:T(8,128)(2,1)}, bf16[256,1024]{1,0:T(8,128)(2,1)}) custom-call(s32[1]{0:T(128)} %bitcast.core_ref, bf16[256,1024]{1,0:T(8,128)(2,1)S(1)} %copy-done.1, bf16[256,1024]{1,0:T(8,128)(2,1)S(1)} %copy-done.3, f32[256,1024]{1,0:T(8,128)S(1)} %get-tuple-element.24.kl_ref, f32[256,1024]{1,0:T(8,128)S(1)} %get-tuple-element.25.vl_ref, ...), custom_call_target="tpu_custom_call" | custom-call | flops 134217728 | bytes 4456452 | tf_op jit(solution)/shard_map/pallas_call | solution.py:39
  (4 shorter events, 0.2 us)
Async XLA Ops:
  0.6 1.0 %copy-start = (bf16[256,1024]{1,0:T(8,128)(2,1)S(1)}, bf16[256,1024]{1,0:T(8,128)(2,1)}, u32[]{:S(2)}) copy-start(bf16[256,1024]{1,0:T(8,128)(2,1)} %k_ref.7) | copy-start | bytes 1572868
  1.7 1.0 %copy-start.2 = (bf16[256,1024]{1,0:T(8,128)(2,1)S(1)}, bf16[256,1024]{1,0:T(8,128)(2,1)}, u32[]{:S(2)}) copy-start(bf16[256,1024]{1,0:T(8,128)(2,1)} %v_ref.7) | copy-start | bytes 1572868
  3.2 1.5 %collective-permute-start = (bf16[4,128,128]{2,1,0:T(8,128)(2,1)S(1)}, bf16[4,128,128]{2,1,0:T(8,128)(2,1)S(1)}, u32[]{:S(2)}, u32[]{:S(2)}) collective-permute-start(bf16[4,128,128]{2,1,0:T(8,128)(2,1)S(1)} %get-tuple-element.20), channel_id=1, source_target_pairs={{0,1},{1,0},{2,3},{3,2},{4,5},{5,4},{6,7},{7,6},{8,9},{9,8},{10,11... | collective-permute-start | bytes 393224 | tf_op jit(solution)/shard_map/ppermute | solution.py:132
  4.7 6.7 %collective-permute-start.1 = (bf16[4,128,128]{2,1,0:T(8,128)(2,1)S(1)}, bf16[4,128,128]{2,1,0:T(8,128)(2,1)S(1)}, u32[]{:S(2)}, u32[]{:S(2)}) collective-permute-start(bf16[4,128,128]{2,1,0:T(8,128)(2,1)S(1)} %fusion.12), channel_id=1, source_target_pairs={{0,2},{1,3},{2,0},{3,1},{4,6},{5,7},{6,4},{7,5},{8,10},{9,11},{10,... | collective-permute-start | bytes 393224 | tf_op jit(solution)/shard_map/ppermute | solution.py:132
  11.5 5.1 %collective-permute-start.2 = (bf16[4,128,128]{2,1,0:T(8,128)(2,1)S(1)}, bf16[4,128,128]{2,1,0:T(8,128)(2,1)S(1)}, u32[]{:S(2)}, u32[]{:S(2)}) collective-permute-start(bf16[4,128,128]{2,1,0:T(8,128)(2,1)S(1)} %fusion.16), channel_id=1, source_target_pairs={{0,4},{1,5},{2,6},{3,7},{4,0},{5,1},{6,2},{7,3},{8,12},{9,13},{10,... | collective-permute-start | bytes 393224 | tf_op jit(solution)/shard_map/ppermute | solution.py:132
  16.7 7.9 %collective-permute-start.3 = (bf16[4,128,128]{2,1,0:T(8,128)(2,1)S(1)}, bf16[4,128,128]{2,1,0:T(8,128)(2,1)S(1)}, u32[]{:S(2)}, u32[]{:S(2)}) collective-permute-start(bf16[4,128,128]{2,1,0:T(8,128)(2,1)S(1)} %fusion.13), channel_id=1, source_target_pairs={{0,8},{1,9},{2,10},{3,11},{4,12},{5,13},{6,14},{7,15},{8,0},{9,1},... | collective-permute-start | bytes 393224 | tf_op jit(solution)/shard_map/ppermute | solution.py:132
  24.6 5.4 %copy-start.4 = (bf16[256,1024]{1,0:T(8,128)(2,1)S(1)}, bf16[256,1024]{1,0:T(8,128)(2,1)}, u32[]{:S(2)}) copy-start(bf16[256,1024]{1,0:T(8,128)(2,1)} %q_ref.5) | copy-start | bytes 1572868
  24.7 5.0 %collective-permute-start.4 = (bf16[4,128,128]{2,1,0:T(8,128)(2,1)S(1)}, bf16[4,128,128]{2,1,0:T(8,128)(2,1)S(1)}, u32[]{:S(2)}, u32[]{:S(2)}) collective-permute-start(bf16[4,128,128]{2,1,0:T(8,128)(2,1)S(1)} %fusion.5), channel_id=1, source_target_pairs={{0,16},{1,17},{2,18},{3,19},{4,20},{5,21},{6,22},{7,23},{8,24},{9,... | collective-permute-start | bytes 393224 | tf_op jit(solution)/shard_map/ppermute | solution.py:132
  25.9 4.1 %copy-start.1 = (bf16[256,1024]{1,0:T(8,128)(2,1)S(1)}, bf16[256,1024]{1,0:T(8,128)(2,1)}, u32[]{:S(2)}) copy-start(bf16[256,1024]{1,0:T(8,128)(2,1)} %k_ref.7) | copy-start | bytes 1572868
  25.9 4.1 %copy-start.3 = (bf16[256,1024]{1,0:T(8,128)(2,1)S(1)}, bf16[256,1024]{1,0:T(8,128)(2,1)}, u32[]{:S(2)}) copy-start(bf16[256,1024]{1,0:T(8,128)(2,1)} %v_ref.7) | copy-start | bytes 1572868
  29.9 1.4 %copy-start.5 = (bf16[256,1024]{1,0:T(8,128)(2,1)S(1)}, bf16[256,1024]{1,0:T(8,128)(2,1)}, u32[]{:S(2)}) copy-start(bf16[256,1024]{1,0:T(8,128)(2,1)} %g_ref.1) | copy-start | bytes 1572868
  29.9 1.4 %collective-permute-start.5 = (bf16[4,128,128]{2,1,0:T(8,128)(2,1)S(1)}, bf16[4,128,128]{2,1,0:T(8,128)(2,1)S(1)}, u32[]{:S(2)}, u32[]{:S(2)}) collective-permute-start(bf16[4,128,128]{2,1,0:T(8,128)(2,1)S(1)} %get-tuple-element.32), channel_id=1, source_target_pairs={{0,1},{1,0},{2,3},{3,2},{4,5},{5,4},{6,7},{7,6},{8,9},{9,8},{10,11... | collective-permute-start | bytes 393224 | tf_op jit(solution)/shard_map/ppermute | solution.py:132
  32.9 1.3 %collective-permute-start.6 = (bf16[4,128,128]{2,1,0:T(8,128)(2,1)S(1)}, bf16[4,128,128]{2,1,0:T(8,128)(2,1)S(1)}, u32[]{:S(2)}, u32[]{:S(2)}) collective-permute-start(bf16[4,128,128]{2,1,0:T(8,128)(2,1)S(1)} %get-tuple-element.27), channel_id=1, source_target_pairs={{0,1},{1,0},{2,3},{3,2},{4,5},{5,4},{6,7},{7,6},{8,9},{9,8},{10,11... | collective-permute-start | bytes 393224 | tf_op jit(solution)/shard_map/ppermute | solution.py:132
  34.3 5.6 %collective-permute-start.7 = (bf16[4,128,128]{2,1,0:T(8,128)(2,1)S(1)}, bf16[4,128,128]{2,1,0:T(8,128)(2,1)S(1)}, u32[]{:S(2)}, u32[]{:S(2)}) collective-permute-start(bf16[4,128,128]{2,1,0:T(8,128)(2,1)S(1)} %fusion.14), channel_id=1, source_target_pairs={{0,2},{1,3},{2,0},{3,1},{4,6},{5,7},{6,4},{7,5},{8,10},{9,11},{10,... | collective-permute-start | bytes 393224 | tf_op jit(solution)/shard_map/ppermute | solution.py:132
  40.0 5.0 %collective-permute-start.8 = (bf16[4,128,128]{2,1,0:T(8,128)(2,1)S(1)}, bf16[4,128,128]{2,1,0:T(8,128)(2,1)S(1)}, u32[]{:S(2)}, u32[]{:S(2)}) collective-permute-start(bf16[4,128,128]{2,1,0:T(8,128)(2,1)S(1)} %fusion.17), channel_id=1, source_target_pairs={{0,4},{1,5},{2,6},{3,7},{4,0},{5,1},{6,2},{7,3},{8,12},{9,13},{10,... | collective-permute-start | bytes 393224 | tf_op jit(solution)/shard_map/ppermute | solution.py:132
  45.1 7.4 %collective-permute-start.9 = (bf16[4,128,128]{2,1,0:T(8,128)(2,1)S(1)}, bf16[4,128,128]{2,1,0:T(8,128)(2,1)S(1)}, u32[]{:S(2)}, u32[]{:S(2)}) collective-permute-start(bf16[4,128,128]{2,1,0:T(8,128)(2,1)S(1)} %fusion.15), channel_id=1, source_target_pairs={{0,8},{1,9},{2,10},{3,11},{4,12},{5,13},{6,14},{7,15},{8,0},{9,1},... | collective-permute-start | bytes 393224 | tf_op jit(solution)/shard_map/ppermute | solution.py:132
  52.5 5.0 %collective-permute-start.10 = (bf16[4,128,128]{2,1,0:T(8,128)(2,1)S(1)}, bf16[4,128,128]{2,1,0:T(8,128)(2,1)S(1)}, u32[]{:S(2)}, u32[]{:S(2)}) collective-permute-start(bf16[4,128,128]{2,1,0:T(8,128)(2,1)S(1)} %fusion.11), channel_id=1, source_target_pairs={{0,16},{1,17},{2,18},{3,19},{4,20},{5,21},{6,22},{7,23},{8,24},{9,... | collective-permute-start | bytes 393224 | tf_op jit(solution)/shard_map/ppermute | solution.py:132
  57.7 3.2 %collective-permute-start.11 = (bf16[4,128,128]{2,1,0:T(8,128)(2,1)S(1)}, bf16[4,128,128]{2,1,0:T(8,128)(2,1)S(1)}, u32[]{:S(2)}, u32[]{:S(2)}) collective-permute-start(bf16[4,128,128]{2,1,0:T(8,128)(2,1)S(1)} %get-tuple-element.30), channel_id=1, source_target_pairs={{0,1},{1,0},{2,3},{3,2},{4,5},{5,4},{6,7},{7,6},{8,9},{9,8},{10,11... | collective-permute-start | bytes 393224 | tf_op jit(solution)/shard_map/ppermute | solution.py:132

commit v2 on v0

v2 whole, which is shorter than its diff:
```python
import functools

import jax
import jax.numpy as jnp
from jax import lax
from jax.experimental import pallas as pl
from jax.experimental.pallas import tpu as pltpu
from jax.sharding import PartitionSpec as P

HD = 128
AXES = ("grp", "shard")
F32 = jnp.float32
BF16 = jnp.bfloat16


def dot(a, b, a_dim, b_dim):
    return lax.dot_general(a, b, (((a_dim,), (b_dim,)), ((), ())), preferred_element_type=F32)


def columns(slot, key):
    return pl.ds(pl.multiple_of((slot ^ key) * HD, HD), HD)


def triangle(rows, keep_lower):
    at_row = lax.broadcasted_iota(jnp.int32, (rows, rows), 0)
    at_col = lax.broadcasted_iota(jnp.int32, (rows, rows), 1)
    return at_row >= at_col if keep_lower else at_row <= at_col


def call(kernel, outs, args, flops, out_hbm=0, in_hbm=(), scratch=(), aliases=None):
    smem = pl.BlockSpec(memory_space=pltpu.SMEM)
    vmem = pl.BlockSpec(memory_space=pltpu.VMEM)
    hbm = pl.BlockSpec(memory_space=pltpu.HBM)
    shapes = [jax.ShapeDtypeStruct(shape, dtype) for shape, dtype in outs]
    size = sum(a.size * a.dtype.itemsize for a in (*args, *shapes))
    specs = [smem if a.dtype == jnp.int32 else hbm if i in in_hbm else vmem for i, a in enumerate(args)]
    return pl.pallas_call(
        kernel,
        out_shape=shapes,
        in_specs=specs,
        out_specs=[hbm if i < out_hbm else vmem for i in range(len(shapes))],
        scratch_shapes=list(scratch),
        input_output_aliases=aliases or {},
        compiler_params=pltpu.CompilerParams(vmem_limit_bytes=32 * 1024 * 1024),
        cost_estimate=pl.CostEstimate(flops=flops, bytes_accessed=size, transcendentals=0),
    )(*args)


def state_kernel(base, key_ref, k_hbm, v_hbm, out_ref, k_buf, v_buf, sems):
    key = key_ref[0]
    copies = []
    for j in range(out_ref.shape[0]):
        cols = columns(base + j, key)
        pair = (
            pltpu.make_async_copy(k_hbm.at[:, cols], k_buf.at[j], sems.at[0, j]),
            pltpu.make_async_copy(v_hbm.at[:, cols], v_buf.at[j], sems.at[1, j]),
        )
        for copy in pair:
            copy.start()
        copies.append(pair)
    for j, pair in enumerate(copies):
        for copy in pair:
            copy.wait()
        out_ref[j] = dot(k_buf[j], v_buf[j], 0, 0).astype(out_ref.dtype)


def local_kernel(key_ref, q_ref, k_ref, v_ref, mixed_ref, turned_ref, scores_ref):
    key = key_ref[0]
    rows = q_ref.shape[0]
    low = triangle(rows, True)
    high = triangle(rows, False)
    for s in range(mixed_ref.shape[0]):
        cols = columns(s, key)
        q = q_ref[:, cols]
        k = k_ref[:, cols]
        scores = jnp.where(low, dot(q, k, 1, 1), 0.0).astype(BF16)
        mixed_ref[s] = dot(scores, v_ref[:, cols], 1, 0)
        turned_ref[s] = q.T
        scores_ref[s] = jnp.where(high, dot(k, q, 1, 1), 0.0).astype(BF16)


def norm_kernel(base, key_ref, q_ref, g_ref, turned_ref, mixed_ref, e_ref, att_ref, gm_ref, state_ref):
    key = key_ref[0]
    for j in range(e_ref.shape[0]):
        cols = columns(base + j, key)
        mixed = mixed_ref[base + j] + dot(q_ref[:, cols], e_ref[j], 1, 0)
        inv_rms = lax.rsqrt(jnp.mean(mixed * mixed, axis=-1, keepdims=True) + 1.0)
        normed = mixed * inv_rms
        att_ref[j] = normed.astype(BF16)
        g = g_ref[:, cols].astype(F32)
        gm = ((g - normed * jnp.mean(g * normed, axis=-1, keepdims=True)) * inv_rms).astype(BF16)
        gm_ref[j] = gm
        state_ref[j] = dot(turned_ref[base + j], gm, 1, 0).astype(state_ref.dtype)


def grads_kernel(base, key_ref, q_ref, k_ref, v_ref, att_ref, gm_ref, e_ref, scores_ref, *refs):
    att_hbm, gq_hbm, kl_ref, vl_ref, gq_buf, sems = refs[-6:]
    key = key_ref[0]
    rows = q_ref.shape[0]
    low = triangle(rows, True)
    high = triangle(rows, False)
    copies = []
    for j in range(e_ref.shape[0]):
        cols = columns(base + j, key)
        copies.append(pltpu.make_async_copy(att_ref.at[j], att_hbm.at[:, cols], sems.at[0, j]))
        copies[-1].start()
        v = v_ref[:, cols]
        gm = gm_ref[j]
        gs = jnp.where(low, dot(gm, v, 1, 1), 0.0).astype(BF16)
        gq_buf[j] = (dot(gs, k_ref[:, cols], 1, 0) + dot(gm, e_ref[j], 1, 1)).astype(BF16)
        copies.append(pltpu.make_async_copy(gq_buf.at[j], gq_hbm.at[:, cols], sems.at[1, j]))
        copies[-1].start()
        gs_turned = jnp.where(high, dot(v, gm, 1, 1), 0.0).astype(BF16)
        kl_ref[j] = dot(gs_turned, q_ref[:, cols], 1, 0)
        vl_ref[j] = dot(scores_ref[base + j], gm, 1, 0)
    for copy in copies:
        copy.wait()


def last_kernel(base, key_ref, k_ref, v_ref, kl_ref, vl_ref, l_ref, *refs):
    gk_hbm, gv_hbm, gk_buf, gv_buf, sems = refs[-5:]
    key = key_ref[0]
    copies = []
    for j in range(l_ref.shape[0]):
        cols = columns(base + j, key)
        later = l_ref[j]
        gk_buf[j] = (kl_ref[j] + dot(v_ref[:, cols], later, 1, 1)).astype(BF16)
        copies.append(pltpu.make_async_copy(gk_buf.at[j], gk_hbm.at[:, cols], sems.at[0, j]))
        copies[-1].start()
        gv_buf[j] = (vl_ref[j] + dot(k_ref[:, cols], later, 1, 0)).astype(BF16)
        copies.append(pltpu.make_async_copy(gv_buf.at[j], gv_hbm.at[:, cols], sems.at[1, j]))
        copies[-1].start()
    for copy in copies:
        copy.wait()


def swap(array, mask, count):
    return lax.ppermute(array, AXES, [(i, i ^ mask) for i in range(count)])


def exchange_levels(count):
    bits = count.bit_length() - 1
    levels = []
    bit = 3
    while bit < bits:
        first = (1 << bit) | 1
        if bit + 1 < bits:
            second = 1 << (bit + 1)
            levels.append((first | second, second, first))
        else:
            levels.append((first,))
        bit += 2
    return levels


SCATTER = (3, 4, 7)


def slot_key(place, count):
    bits = count.bit_length() - 1
    half = (place ^ (place >> 1)) & 1
    for bit in range(3, bits, 2):
        half = half ^ ((place >> bit) & 1)
    return (half << 2) | ((place >> 1) & 3)


def beside(arrays, work, tie):
    if work is None:
        return arrays, None
    done = work(tie)
    return lax.optimization_barrier((arrays, done))


def scan_states(own, from_core, place, count, backward, works):
    def before(a, b):
        return (a > b) if backward else (a < b)

    def pick(condition, array):
        return jnp.where(condition, array, 0.0)

    chip = place >> 1
    total = own + from_core
    rounded = total.astype(BF16)
    arrived = [swap(rounded[j], SCATTER[j - 1], count) for j in (1, 2, 3)]
    arrived, first = beside(arrived, works[0], rounded)
    parts = [total[0], *(a.astype(F32) for a in arrived)]
    cluster = parts[0] + parts[1] + parts[2] + parts[3]
    entering = jnp.zeros_like(cluster)
    second = None
    for at, masks in enumerate(exchange_levels(count)):
        rounded = cluster.astype(BF16)
        arrived = [swap(rounded, mask, count) for mask in masks]
        if at == 0:
            arrived, second = beside(arrived, works[1], rounded)
        for mask, array in zip(masks, arrived):
            array = array.astype(F32)
            entering = entering + pick(before(chip ^ (mask >> 1), chip), array)
            cluster = cluster + array
    low = chip & 3
    sums = []
    for j in range(4):
        value = entering
        for i in range(4):
            if i != j:
                value = value + pick(before(low ^ i, low ^ j), parts[i])
        sums.append(value)
    rounded = [value.astype(BF16) for value in sums[1:]]
    arrived = [swap(rounded[j - 1], SCATTER[j - 1], count) for j in (1, 2, 3)]
    arrived, third = beside(arrived, works[2], rounded[0])
    entering = jnp.stack([sums[0], *(a.astype(F32) for a in arrived)])
    core = place & 1
    mine = entering + pick(before(core ^ 1, core), from_core)
    theirs = entering + pick(before(core, core ^ 1), own)
    return mine.astype(BF16), theirs.astype(BF16), (first, second, third)


def body(query_rows, key_rows, value_rows, grad_out):
    rows, width = query_rows.shape
    heads = width // HD
    half = heads // 2
    count = lax.axis_size("grp") * lax.axis_size("shard")
    place = lax.axis_index(AXES)
    key = slot_key(place, count).astype(jnp.int32).reshape(1)
    work = rows * width * HD
    scores = rows * width * rows
    block = (half, rows, HD)
    flat = (rows, width)
    dma = pltpu.SemaphoreType.DMA((2, half))
    buffer = pltpu.VMEM(block, BF16)

    def state(base, dtype, key):
        return call(
            functools.partial(state_kernel, base), [((half, HD, HD), dtype)], (key, key_rows, value_rows),
            work, in_hbm=(1, 2), scratch=(buffer, buffer, dma),
        )[0]

    def tied(tie):
        return lax.optimization_barrier((key, tie))[0]

    def local(tie):
        return call(
            local_kernel,
            [((heads, rows, HD), F32), ((heads, HD, rows), BF16), ((heads, rows, rows), BF16)],
            (tied(tie), query_rows, key_rows, value_rows), 6 * scores,
        )

    send = state(half, BF16, key)
    own = state(0, F32, tied(send))
    from_core = swap(send, 1, count).astype(F32)
    mine, theirs, (_, (mixed, turned, turned_scores), _) = scan_states(
        own, from_core, place, count, False, (None, local, None)
    )
    e_other = swap(theirs, 1, count)

    def norm(base, key, e, dtype):
        return call(
            functools.partial(norm_kernel, base),
            [(block, BF16), (block, BF16), ((half, HD, HD), dtype)],
            (key, query_rows, grad_out, turned, mixed, e), 2 * work,
        )

    att_mine, gm_mine, send = norm(0, key, mine, BF16)
    from_core = swap(send, 1, count).astype(F32)
    att_other, gm_other, own = norm(half, tied(send), e_other, F32)

    def grads(base, key, att, gm, e, outs):
        n = 8
        return call(
            functools.partial(grads_kernel, base),
            [(flat, BF16), (flat, BF16), (block, F32), (block, F32)],
            (key, query_rows, key_rows, value_rows, att, gm, e, turned_scores, *outs),
            4 * scores + work, out_hbm=2, in_hbm=(n, n + 1), scratch=(buffer, dma),
            aliases={n: 0, n + 1: 1} if outs else None,
        )

    def grads_mine(tie):
        return grads(0, tied(tie), att_mine, gm_mine, mine, ())

    made = []

    def grads_first(tie):
        made.append(grads_mine(tie))
        return made[0]

    def grads_second(tie):
        return grads(half, tied(tie), att_other, gm_other, e_other, made[0][:2])

    l_other, theirs, ((_, _, kl_mine, vl_mine), (attended, grad_query, kl_other, vl_other), _) = scan_states(
        own, from_core, place, count, True, (grads_first, grads_second, None)
    )
    l_mine = swap(theirs, 1, count)

    def last(base, key, kl, vl, later, outs):
        n = 6
        return call(
            functools.partial(last_kernel, base),
            [(flat, BF16), (flat, BF16)],
            (key, key_rows, value_rows, kl, vl, later, *outs),
            2 * work, out_hbm=2, in_hbm=(n, n + 1), scratch=(buffer, buffer, dma),
            aliases={n: 0, n + 1: 1} if outs else None,
        )

    outs = last(half, key, kl_other, vl_other, l_other, ())
    grad_key, grad_value = last(0, key, kl_mine, vl_mine, l_mine, outs)
    return attended, grad_query, grad_key, grad_value


def solution(mesh):
    spec = P(AXES, None)
    return jax.shard_map(
        body, mesh=mesh, in_specs=(spec,) * 4, out_specs=(spec,) * 4, check_vma=False
    )
```

time: 228 us -> 57.9 us (0.25)
  blocking collectives: 171 us -> 0 us
  starting transfers between devices: 0.08 us -> 23.3 us
  waiting for transfers between devices: 0.07 us -> 14.3 us
  other arithmetic: 16.7 us -> 2.74 us
  matrix products: 13.7 us -> 0 us
  between operations: 14.3 us -> 0.97 us
  Pallas kernels: 0 us -> 10.8 us
  local copies, waits for them, and re-layouts: 10.2 us -> 5.47 us
    psum x2 -> x0, blocking collectives: 157 us -> none  [prefix_states(): group_sum = lax.psum(local_state, 'shard')]
    ppermute x0 -> x22, starting transfers between devices: none -> 23.3 us  [swap(): return lax.ppermute(array, AXES, [(i, i ^ mask) for i in range(count)])]
    add x16 -> x0, other arithmetic: 16.2 us -> none  [add_states(): return earlier + later_part]
    ppermute x0 -> x22, waiting for transfers between devices: none -> 14.3 us  [swap(): return lax.ppermute(array, AXES, [(i, i ^ mask) for i in range(count)])]
    all_gather x2 -> x0, blocking collectives: 14.2 us -> none  [entering(): gathered = lax.all_gather(array.astype(jnp.bfloat16), axis)]
    dot_general x12 -> x0, matrix products: 13.7 us -> none  [the longest x1 2.5 us: body(): jnp.einsum('hts,the->she', local_scores, grad_mixed, preferred_element_ty...]
    pallas_call x0 -> x9, Pallas kernels: none -> 10.8 us  [call(): pl.pallas_call(kernel, out_shape=shapes, in_specs=specs, out_specs=[hbm i...]
    convert_element_type x3 -> x0, local copies, waits for them, and re-layouts: 4.2 us -> none  [the longest x2 2.95 us: entering(): gathered = lax.all_gather(array.astype(jnp.bfloat16), axis)]
  transfers between devices with their start and end apart: 2 -> 22, of which waited for: 0 -> 12; matrix products, arithmetic and copies ran while one was open for 6% -> 2% of each run, Pallas kernels for 0% -> 15%
where the time goes in v2:
time: 57.9 us; the launch traced here: 57.5 us
  starting transfers between devices  23.3 us (40%)
  waiting for transfers between devices  14.3 us (25%)
  Pallas kernels  10.8 us (19%)
  local copies, waits for them, and re-layouts  5.47 us (9%)
  other arithmetic  2.74 us (5%)
  between operations  0.97 us (2%)
    ppermute x22, starting transfers between devices, swap(): return lax.ppermute(array, AXES, [(i, i ^ mask) for i in range(count)])  23.3 us
    ppermute x22, waiting for transfers between devices, swap(): return lax.ppermute(array, AXES, [(i, i ^ mask) for i in range(count)])  14.3 us
    pallas_call x9, Pallas kernels, call(): pl.pallas_call(kernel, out_shape=shapes, in_specs=specs, out_specs=[hbm i...  10.8 us
    unnamed x44, local copies, waits for them, and re-layouts  5.45 us
  transfers between devices with their start and end apart: 22, of which 12 were waited for; matrix products, arithmetic and copies ran while one was open for 2% of the time, Pallas kernels for 15%

profile of v2, /device:TPU:0, one launch (start us, length us, event | category | flops | bytes accessed | tf_op | source)
XLA Modules:
  0.0 57.5 jit_solution(15814341757743209701)
XLA Ops:
  0.6 0.0 copy-start
  0.7 1.0 %copy-done = bf16[256,1024]{1,0:T(8,128)(2,1)S(1)} copy-done((bf16[256,1024]{1,0:T(8,128)(2,1)S(1)}, bf16[256,1024]{1,0:T(8,128)(2,1)}, u32[]{:S(2)}) %copy-start) | copy-done | bytes 524312
  1.7 1.0 %copy-done.2 = bf16[256,1024]{1,0:T(8,128)(2,1)S(1)} copy-done((bf16[256,1024]{1,0:T(8,128)(2,1)S(1)}, bf16[256,1024]{1,0:T(8,128)(2,1)}, u32[]{:S(2)}) %copy-start.2) | copy-done | bytes 524312
  2.7 1.0 %shard_map.75 = bf16[4,128,128]{2,1,0:T(8,128)(2,1)S(1)} custom-call(s32[1]{0:T(128)} %bitcast.key_ref, bf16[256,1024]{1,0:T(8,128)(2,1)S(1)} %copy-done, bf16[256,1024]{1,0:T(8,128)(2,1)S(1)} %copy-done.2), custom_call_target="tpu_custom_call" | custom-call | flops 33554432 | bytes 1179652 | tf_op jit(solution)/shard_map/pallas_call | solution.py:37
  3.8 0.5 collective-permute-start
  4.3 1.0 %shard_map.76 = f32[4,128,128]{2,1,0:T(8,128)S(1)} custom-call(s32[1]{0:T(128)} %bitcast.key_ref, bf16[256,1024]{1,0:T(8,128)(2,1)S(1)} %copy-done, bf16[256,1024]{1,0:T(8,128)(2,1)S(1)} %copy-done.2), custom_call_target="tpu_custom_call" | custom-call | flops 33554432 | bytes 1310724 | tf_op jit(solution)/shard_map/pallas_call | solution.py:37
  5.3 0.0 copy-start.1
  5.4 0.0 copy-start.3
  5.4 0.0 collective-permute-done
  5.4 2.7 %collective-permute-start.1 = (bf16[128,128]{1,0:T(8,128)(2,1)S(1)}, bf16[128,128]{1,0:T(8,128)(2,1)S(1)}, u32[]{:S(2)}, u32[]{:S(2)}) collective-permute-start(bf16[128,128]{1,0:T(8,128)(2,1)S(1)} %get-tuple-element.111), channel_id=1, source_target_pairs={{0,3},{1,2},{2,1},{3,0},{4,7},{5,6},{6,5},{7,4},{8,11},{9,10},{10,... | collective-permute-start | bytes 98312 | tf_op jit(solution)/shard_map/ppermute | solution.py:138
  8.1 1.6 %collective-permute-start.2 = (bf16[128,128]{1,0:T(8,128)(2,1)S(1)}, bf16[128,128]{1,0:T(8,128)(2,1)S(1)}, u32[]{:S(2)}, u32[]{:S(2)}) collective-permute-start(bf16[128,128]{1,0:T(8,128)(2,1)S(1)} %get-tuple-element.113), channel_id=1, source_target_pairs={{0,4},{1,5},{2,6},{3,7},{4,0},{5,1},{6,2},{7,3},{8,12},{9,13},{10,... | collective-permute-start | bytes 98312 | tf_op jit(solution)/shard_map/ppermute | solution.py:138
  9.7 0.0 collective-permute-done.1
  9.7 2.3 %collective-permute-done.2 = bf16[128,128]{1,0:T(8,128)(2,1)S(1)} collective-permute-done((bf16[128,128]{1,0:T(8,128)(2,1)S(1)}, bf16[128,128]{1,0:T(8,128)(2,1)S(1)}, u32[]{:S(2)}, u32[]{:S(2)}) %collective-permute-start.2) | collective-permute-done | bytes 32800 | tf_op jit(solution)/shard_map/ppermute | solution.py:138
  12.0 2.1 %collective-permute-done.3 = bf16[128,128]{1,0:T(8,128)(2,1)S(1)} collective-permute-done((bf16[128,128]{1,0:T(8,128)(2,1)S(1)}, bf16[128,128]{1,0:T(8,128)(2,1)S(1)}, u32[]{:S(2)}, u32[]{:S(2)}) %collective-permute-start.3) | collective-permute-done | bytes 32800 | tf_op jit(solution)/shard_map/ppermute | solution.py:138
  14.1 3.3 %collective-permute-start.4 = (bf16[128,128]{1,0:T(8,128)(2,1)S(1)}, bf16[128,128]{1,0:T(8,128)(2,1)S(1)}, u32[]{:S(2)}, u32[]{:S(2)}) collective-permute-start(bf16[128,128]{1,0:T(8,128)(2,1)S(1)} %fusion.17), channel_id=1, source_target_pairs={{0,25},{1,24},{2,27},{3,26},{4,29},{5,28},{6,31},{7,30},{8,17},{9,... | collective-permute-start | bytes 98312 | tf_op jit(solution)/shard_map/ppermute | solution.py:138
  17.5 0.5 collective-permute-start.5
  18.0 0.1 collective-permute-start.6
  18.0 1.6 %shard_map.77 = (f32[8,256,128]{2,1,0:T(8,128)S(1)}, bf16[8,128,256]{2,1,0:T(8,128)(2,1)S(1)}, bf16[8,256,256]{2,1,0:T(8,128)(2,1)S(1)}) custom-call(s32[1]{0:T(128)} %bitcast.key_ref, bf16[256,1024]{1,0:T(8,128)(2,1)S(1)} %copy-done.4, bf16[256,1024]{1,0:T(8,128)(2,1)S(1)} %copy-done.1, bf16[256,1024]{1,0:T(8,128)(2,1)S(1)} %copy-done.3), custom_call_target="tpu_custom_call" | custom-call | flops 402653184 | bytes 4194308 | tf_op jit(solution)/shard_map/pallas_call | solution.py:37
  19.7 0.6 %collective-permute-done.4 = bf16[128,128]{1,0:T(8,128)(2,1)S(1)} collective-permute-done((bf16[128,128]{1,0:T(8,128)(2,1)S(1)}, bf16[128,128]{1,0:T(8,128)(2,1)S(1)}, u32[]{:S(2)}, u32[]{:S(2)}) %collective-permute-start.4) | collective-permute-done | bytes 32800 | tf_op jit(solution)/shard_map/ppermute | solution.py:138
  20.3 1.1 %collective-permute-done.5 = bf16[128,128]{1,0:T(8,128)(2,1)S(1)} collective-permute-done((bf16[128,128]{1,0:T(8,128)(2,1)S(1)}, bf16[128,128]{1,0:T(8,128)(2,1)S(1)}, u32[]{:S(2)}, u32[]{:S(2)}) %collective-permute-start.5) | collective-permute-done | bytes 32800 | tf_op jit(solution)/shard_map/ppermute | solution.py:138
  21.4 1.7 %collective-permute-done.6 = bf16[128,128]{1,0:T(8,128)(2,1)S(1)} collective-permute-done((bf16[128,128]{1,0:T(8,128)(2,1)S(1)}, bf16[128,128]{1,0:T(8,128)(2,1)S(1)}, u32[]{:S(2)}, u32[]{:S(2)}) %collective-permute-start.6) | collective-permute-done | bytes 32800 | tf_op jit(solution)/shard_map/ppermute | solution.py:138
  23.1 0.1 fusion.16
  23.2 0.1 collective-permute-start.8
  23.3 0.2 collective-permute-start.7
  23.5 0.1 fusion.7
  23.6 3.0 %collective-permute-start.9 = (bf16[128,128]{1,0:T(8,128)(2,1)S(1)}, bf16[128,128]{1,0:T(8,128)(2,1)S(1)}, u32[]{:S(2)}, u32[]{:S(2)}) collective-permute-start(bf16[128,128]{1,0:T(8,128)(2,1)S(1)} %get-tuple-element.107), channel_id=1, source_target_pairs={{0,7},{1,6},{2,5},{3,4},{4,3},{5,2},{6,1},{7,0},{8,15},{9,14},{10,... | collective-permute-start | bytes 98312 | tf_op jit(solution)/shard_map/ppermute | solution.py:138
  26.6 0.6 %collective-permute-done.8 = bf16[128,128]{1,0:T(8,128)(2,1)S(1)} collective-permute-done((bf16[128,128]{1,0:T(8,128)(2,1)S(1)}, bf16[128,128]{1,0:T(8,128)(2,1)S(1)}, u32[]{:S(2)}, u32[]{:S(2)}) %collective-permute-start.8) | collective-permute-done | bytes 32800 | tf_op jit(solution)/shard_map/ppermute | solution.py:138
  27.2 0.0 copy-start.5
  27.2 1.0 %collective-permute-done.9 = bf16[128,128]{1,0:T(8,128)(2,1)S(1)} collective-permute-done((bf16[128,128]{1,0:T(8,128)(2,1)S(1)}, bf16[128,128]{1,0:T(8,128)(2,1)S(1)}, u32[]{:S(2)}, u32[]{:S(2)}) %collective-permute-start.9) | collective-permute-done | bytes 32800 | tf_op jit(solution)/shard_map/ppermute | solution.py:138
  28.2 0.1 add_convert_fusion.1
  28.3 0.3 collective-permute-start.10
  28.5 0.7 %shard_map.78 = (bf16[4,256,128]{2,1,0:T(8,128)(2,1)S(1)}, bf16[4,256,128]{2,1,0:T(8,128)(2,1)S(1)}, bf16[4,128,128]{2,1,0:T(8,128)(2,1)S(1)}) custom-call(s32[1]{0:T(128)} %bitcast.key_ref, bf16[256,1024]{1,0:T(8,128)(2,1)S(1)} %copy-done.4, bf16[256,1024]{1,0:T(8,128)(2,1)S(1)} %copy-done.5, bf16[8,128,256]{2,1,0:T(8,128)(2,1)S(1)} %get-tuple-element.53.turned_ref, ...), custom_call_target="tpu_custom_call" | custom-call | flops 67108864 | bytes 3407876 | tf_op jit(solution)/shard_map/pallas_call | solution.py:37
  29.2 0.4 collective-permute-start.11
  29.6 0.1 collective-permute-done.10.e_ref
  29.7 0.7 %shard_map.79 = (bf16[4,256,128]{2,1,0:T(8,128)(2,1)S(1)}, bf16[4,256,128]{2,1,0:T(8,128)(2,1)S(1)}, f32[4,128,128]{2,1,0:T(8,128)S(1)}) custom-call(s32[1]{0:T(128)} %bitcast.key_ref, bf16[256,1024]{1,0:T(8,128)(2,1)S(1)} %copy-done.4, bf16[256,1024]{1,0:T(8,128)(2,1)S(1)} %copy-done.5, bf16[8,128,256]{2,1,0:T(8,128)(2,1)S(1)} %get-tuple-element.53.turned_ref, ...), custom_call_target="tpu_custom_call" | custom-call | flops 67108864 | bytes 3538948 | tf_op jit(solution)/shard_map/pallas_call | solution.py:37
  30.4 0.0 copy-start.8
  30.4 0.0 copy-start.10
  30.4 0.3 collective-permute-done.11
  30.7 0.4 copy-done.8
  31.1 0.1 copy-done.10
  31.1 0.1 copy-done.14
  31.3 1.3 %collective-permute-start.12 = (bf16[128,128]{1,0:T(8,128)(2,1)S(1)}, bf16[128,128]{1,0:T(8,128)(2,1)S(1)}, u32[]{:S(2)}, u32[]{:S(2)}) collective-permute-start(bf16[128,128]{1,0:T(8,128)(2,1)S(1)} %get-tuple-element.110), channel_id=1, source_target_pairs={{0,3},{1,2},{2,1},{3,0},{4,7},{5,6},{6,5},{7,4},{8,11},{9,10},{10,... | collective-permute-start | bytes 98312 | tf_op jit(solution)/shard_map/ppermute | solution.py:138
  32.6 1.9 %collective-permute-start.13 = (bf16[128,128]{1,0:T(8,128)(2,1)S(1)}, bf16[128,128]{1,0:T(8,128)(2,1)S(1)}, u32[]{:S(2)}, u32[]{:S(2)}) collective-permute-start(bf16[128,128]{1,0:T(8,128)(2,1)S(1)} %get-tuple-element.109), channel_id=1, source_target_pairs={{0,4},{1,5},{2,6},{3,7},{4,0},{5,1},{6,2},{7,3},{8,12},{9,13},{10,... | collective-permute-start | bytes 98312 | tf_op jit(solution)/shard_map/ppermute | solution.py:138
  34.5 1.8 %shard_map.80 = (bf16[256,1024]{1,0:T(8,128)(2,1)}, bf16[256,1024]{1,0:T(8,128)(2,1)}, f32[4,256,128]{2,1,0:T(8,128)S(1)}, f32[4,256,128]{2,1,0:T(8,128)S(1)}) custom-call(s32[1]{0:T(128)} %bitcast.key_ref, bf16[256,1024]{1,0:T(8,128)(2,1)S(1)} %copy-done.4, bf16[256,1024]{1,0:T(8,128)(2,1)S(1)} %copy-done.1, bf16[256,1024]{1,0:T(8,128)(2,1)S(1)} %copy-done.3, ...), custom_call_target="tpu_custom_call" | custom-call | flops 301989888 | bytes 5373956 | tf_op jit(solution)/shard_map/pallas_call | solution.py:37
  36.4 0.8 %copy-done.6 = f32[4,256,128]{2,1,0:T(8,128)} copy-done((f32[4,256,128]{2,1,0:T(8,128)}, f32[4,256,128]{2,1,0:T(8,128)S(1)}, u32[]{:S(2)}) %copy-start.6) | copy-done | bytes 524312
  37.2 1.7 %collective-permute-done.14 = bf16[128,128]{1,0:T(8,128)(2,1)S(1)} collective-permute-done((bf16[128,128]{1,0:T(8,128)(2,1)S(1)}, bf16[128,128]{1,0:T(8,128)(2,1)S(1)}, u32[]{:S(2)}, u32[]{:S(2)}) %collective-permute-start.14) | collective-permute-done | bytes 32800 | tf_op jit(solution)/shard_map/ppermute | solution.py:138
  38.9 0.6 %fusion.31 = bf16[128,128]{1,0:T(8,128)(2,1)} fusion(bf16[128,128]{1,0:T(8,128)(2,1)S(1)} %collective-permute-done.14, bf16[128,128]{1,0:T(8,128)(2,1)S(1)} %collective-permute-done.13, bf16[128,128]{1,0:T(8,128)(2,1)S(1)} %collective-permute-done.12, f32[4,128,128]{2,1,0:T(8,128)S(1)} %get-tuple-element.93), kind=kLoop, calls=%fused_computation.63 | loop fusion | flops 114688 | bytes 196608 | tf_op jit(solution)/shard_map/convert_element_type | solution.py:191
  39.5 0.3 collective-permute-start.15
  39.8 1.3 %collective-permute-start.16 = (bf16[128,128]{1,0:T(8,128)(2,1)}, bf16[128,128]{1,0:T(8,128)(2,1)}, u32[]{:S(2)}, u32[]{:S(2)}) collective-permute-start(bf16[128,128]{1,0:T(8,128)(2,1)} %fusion.31), channel_id=1, source_target_pairs={{0,16},{1,17},{2,18},{3,19},{4,20},{5,21},{6,22},{7,23},{8,24},{9,... | collective-permute-start | bytes 98312 | tf_op jit(solution)/shard_map/ppermute | solution.py:138
  41.2 2.3 %collective-permute-start.17 = (bf16[128,128]{1,0:T(8,128)(2,1)}, bf16[128,128]{1,0:T(8,128)(2,1)}, u32[]{:S(2)}, u32[]{:S(2)}) collective-permute-start(bf16[128,128]{1,0:T(8,128)(2,1)} %fusion.31), channel_id=1, source_target_pairs={{0,9},{1,8},{2,11},{3,10},{4,13},{5,12},{6,15},{7,14},{8,1},{9,0},... | collective-permute-start | bytes 98312 | tf_op jit(solution)/shard_map/ppermute | solution.py:138
  43.4 0.9 %copy-done.9 = bf16[4,256,128]{2,1,0:T(8,128)(2,1)S(1)} copy-done((bf16[4,256,128]{2,1,0:T(8,128)(2,1)S(1)}, bf16[4,256,128]{2,1,0:T(8,128)(2,1)}, u32[]{:S(2)}) %copy-start.9) | copy-done | bytes 262168
  44.4 0.9 %copy-done.11 = bf16[4,256,128]{2,1,0:T(8,128)(2,1)S(1)} copy-done((bf16[4,256,128]{2,1,0:T(8,128)(2,1)S(1)}, bf16[4,256,128]{2,1,0:T(8,128)(2,1)}, u32[]{:S(2)}) %copy-start.11) | copy-done | bytes 262168
  45.3 1.8 %shard_map.81 = (bf16[256,1024]{1,0:T(8,128)(2,1)}, bf16[256,1024]{1,0:T(8,128)(2,1)}, f32[4,256,128]{2,1,0:T(8,128)S(1)}, f32[4,256,128]{2,1,0:T(8,128)S(1)}) custom-call(s32[1]{0:T(128)} %bitcast.key_ref, bf16[256,1024]{1,0:T(8,128)(2,1)S(1)} %copy-done.4, bf16[256,1024]{1,0:T(8,128)(2,1)S(1)} %copy-done.1, ...), custom_call_target="tpu_custom_call", output_to_operand_aliasing={{0}: (8, {}), {1}: (9, {})} | custom-call | flops 301989888 | bytes 6422532 | tf_op jit(solution)/shard_map/pallas_call | solution.py:37
  47.3 0.9 %fusion.30 = (bf16[128,128]{1,0:T(8,128)(2,1)S(1)}, bf16[128,128]{1,0:T(8,128)(2,1)S(1)}) fusion(bf16[128,128]{1,0:T(8,128)(2,1)S(1)} %copy-done.19, bf16[128,128]{1,0:T(8,128)(2,1)S(1)} %copy-done.21, f32[4,128,128]{2,1,0:T(8,128)S(1)} %copy-done.13, pred[]{:T(512)S(6)} %gt.59, pred[]{:T(512)S(6)} %gt.58, pred[]{:T(512)S(6)} %gt.57, ...), kind=kLoop, calls=%fused_computation.62 | loop fusion | flops 409600 | bytes 327689 | tf_op jit(solution)/shard_map/convert_element_type | solution.py:207
  48.1 0.1 collective-permute-start.19
  48.2 1.5 %collective-permute-start.18 = (bf16[128,128]{1,0:T(8,128)(2,1)S(1)}, bf16[128,128]{1,0:T(8,128)(2,1)S(1)}, u32[]{:S(2)}, u32[]{:S(2)}) collective-permute-start(bf16[128,128]{1,0:T(8,128)(2,1)S(1)} %get-tuple-element.96), channel_id=1, source_target_pairs={{0,3},{1,2},{2,1},{3,0},{4,7},{5,6},{6,5},{7,4},{8,11},{9,10},{10,... | collective-permute-start | bytes 98312 | tf_op jit(solution)/shard_map/ppermute | solution.py:138
  49.7 0.9 %fusion.21 = (f32[1,128,128]{2,1,0:T(8,128)S(1)}, bf16[128,128]{1,0:T(8,128)(2,1)S(1)}) fusion(bf16[128,128]{1,0:T(8,128)(2,1)S(1)} %copy-done.17, bf16[128,128]{1,0:T(8,128)(2,1)S(1)} %copy-done.19, bf16[128,128]{1,0:T(8,128)(2,1)S(1)} %copy-done.21, pred[]{:T(512)S(6)} %gt.56, pred[]{:T(512)S(6)} %gt.55, pred[]{:T(512)S(6)} %gt.54, ...), kind=kLoop, calls=%fused_computation.53 | loop fusion | flops 393216 | bytes 360457 | tf_op jit(solution)/shard_map/stack | solution.py:210
  50.6 1.8 %collective-permute-start.20 = (bf16[128,128]{1,0:T(8,128)(2,1)S(1)}, bf16[128,128]{1,0:T(8,128)(2,1)S(1)}, u32[]{:S(2)}, u32[]{:S(2)}) collective-permute-start(bf16[128,128]{1,0:T(8,128)(2,1)S(1)} %get-tuple-element.105), channel_id=1, source_target_pairs={{0,7},{1,6},{2,5},{3,4},{4,3},{5,2},{6,1},{7,0},{8,15},{9,14},{10,... | collective-permute-start | bytes 98312 | tf_op jit(solution)/shard_map/ppermute | solution.py:138
  52.4 2.6 %collective-permute-done.20 = bf16[128,128]{1,0:T(8,128)(2,1)S(1)} collective-permute-done((bf16[128,128]{1,0:T(8,128)(2,1)S(1)}, bf16[128,128]{1,0:T(8,128)(2,1)S(1)}, u32[]{:S(2)}, u32[]{:S(2)}) %collective-permute-start.20) | collective-permute-done | bytes 32800 | tf_op jit(solution)/shard_map/ppermute | solution.py:138
  55.0 0.1 fusion.3
  55.1 0.2 collective-permute-start.21
  55.2 1.0 %shard_map.82 = (bf16[256,1024]{1,0:T(8,128)(2,1)}, bf16[256,1024]{1,0:T(8,128)(2,1)}) custom-call(s32[1]{0:T(128)} %bitcast.key_ref, bf16[256,1024]{1,0:T(8,128)(2,1)S(1)} %copy-done.1, bf16[256,1024]{1,0:T(8,128)(2,1)S(1)} %copy-done.3, f32[4,256,128]{2,1,0:T(8,128)S(1)} %get-tuple-element.86.kl_ref, f32[4,256,128]{2,1,0:T(8,128)S(1)} %get-tuple-element.87.vl_ref, ...), custom_call_target="tpu_custom_call" | custom-call | flops 67108864 | bytes 3276804 | tf_op jit(solution)/shard_map/pallas_call | solution.py:37
  56.3 0.2 collective-permute-done.21.l_ref
  56.5 1.0 %shard_map.83 = (bf16[256,1024]{1,0:T(8,128)(2,1)}, bf16[256,1024]{1,0:T(8,128)(2,1)}) custom-call(s32[1]{0:T(128)} %bitcast.key_ref, bf16[256,1024]{1,0:T(8,128)(2,1)S(1)} %copy-done.1, bf16[256,1024]{1,0:T(8,128)(2,1)S(1)} %copy-done.3, f32[4,256,128]{2,1,0:T(8,128)S(1)} %get-tuple-element.81.kl_ref, ...), custom_call_target="tpu_custom_call", output_to_operand_aliasing={{0}: (6, {}), {1}: (7, {})} | custom-call | flops 67108864 | bytes 4325380 | tf_op jit(solution)/shard_map/pallas_call | solution.py:37
  (51 shorter events, 0.2 us)
Async XLA Ops:
  0.6 1.0 %copy-start = (bf16[256,1024]{1,0:T(8,128)(2,1)S(1)}, bf16[256,1024]{1,0:T(8,128)(2,1)}, u32[]{:S(2)}) copy-start(bf16[256,1024]{1,0:T(8,128)(2,1)} %k_ref.9) | copy-start | bytes 1572868
  1.7 1.0 %copy-start.2 = (bf16[256,1024]{1,0:T(8,128)(2,1)S(1)}, bf16[256,1024]{1,0:T(8,128)(2,1)}, u32[]{:S(2)}) copy-start(bf16[256,1024]{1,0:T(8,128)(2,1)} %v_ref.9) | copy-start | bytes 1572868
  3.8 1.6 %collective-permute-start = (bf16[4,128,128]{2,1,0:T(8,128)(2,1)S(1)}, bf16[4,128,128]{2,1,0:T(8,128)(2,1)S(1)}, u32[]{:S(2)}, u32[]{:S(2)}) collective-permute-start(bf16[4,128,128]{2,1,0:T(8,128)(2,1)S(1)} %shard_map.75), channel_id=1, source_target_pairs={{0,1},{1,0},{2,3},{3,2},{4,5},{5,4},{6,7},{7,6},{8,9},{9,8},{10,11... | collective-permute-start | bytes 393224 | tf_op jit(solution)/shard_map/ppermute | solution.py:138
  4.3 13.7 %copy-start.4 = (bf16[256,1024]{1,0:T(8,128)(2,1)S(1)}, bf16[256,1024]{1,0:T(8,128)(2,1)}, u32[]{:S(2)}) copy-start(bf16[256,1024]{1,0:T(8,128)(2,1)} %q_ref.9) | copy-start | bytes 1572868
  5.3 12.7 %copy-start.1 = (bf16[256,1024]{1,0:T(8,128)(2,1)S(1)}, bf16[256,1024]{1,0:T(8,128)(2,1)}, u32[]{:S(2)}) copy-start(bf16[256,1024]{1,0:T(8,128)(2,1)} %k_ref.9) | copy-start | bytes 1572868
  5.4 12.7 %copy-start.3 = (bf16[256,1024]{1,0:T(8,128)(2,1)S(1)}, bf16[256,1024]{1,0:T(8,128)(2,1)}, u32[]{:S(2)}) copy-start(bf16[256,1024]{1,0:T(8,128)(2,1)} %v_ref.9) | copy-start | bytes 1572868
  5.4 4.3 %collective-permute-start.1 = (bf16[128,128]{1,0:T(8,128)(2,1)S(1)}, bf16[128,128]{1,0:T(8,128)(2,1)S(1)}, u32[]{:S(2)}, u32[]{:S(2)}) collective-permute-start(bf16[128,128]{1,0:T(8,128)(2,1)S(1)} %get-tuple-element.111), channel_id=1, source_target_pairs={{0,3},{1,2},{2,1},{3,0},{4,7},{5,6},{6,5},{7,4},{8,11},{9,10},{10,... | collective-permute-start | bytes 98312 | tf_op jit(solution)/shard_map/ppermute | solution.py:138
  8.1 3.9 %collective-permute-start.2 = (bf16[128,128]{1,0:T(8,128)(2,1)S(1)}, bf16[128,128]{1,0:T(8,128)(2,1)S(1)}, u32[]{:S(2)}, u32[]{:S(2)}) collective-permute-start(bf16[128,128]{1,0:T(8,128)(2,1)S(1)} %get-tuple-element.113), channel_id=1, source_target_pairs={{0,4},{1,5},{2,6},{3,7},{4,0},{5,1},{6,2},{7,3},{8,12},{9,13},{10,... | collective-permute-start | bytes 98312 | tf_op jit(solution)/shard_map/ppermute | solution.py:138
  9.7 4.4 %collective-permute-start.3 = (bf16[128,128]{1,0:T(8,128)(2,1)S(1)}, bf16[128,128]{1,0:T(8,128)(2,1)S(1)}, u32[]{:S(2)}, u32[]{:S(2)}) collective-permute-start(bf16[128,128]{1,0:T(8,128)(2,1)S(1)} %get-tuple-element.112), channel_id=1, source_target_pairs={{0,7},{1,6},{2,5},{3,4},{4,3},{5,2},{6,1},{7,0},{8,15},{9,14},{10,... | collective-permute-start | bytes 98312 | tf_op jit(solution)/shard_map/ppermute | solution.py:138
  14.1 6.1 %collective-permute-start.4 = (bf16[128,128]{1,0:T(8,128)(2,1)S(1)}, bf16[128,128]{1,0:T(8,128)(2,1)S(1)}, u32[]{:S(2)}, u32[]{:S(2)}) collective-permute-start(bf16[128,128]{1,0:T(8,128)(2,1)S(1)} %fusion.17), channel_id=1, source_target_pairs={{0,25},{1,24},{2,27},{3,26},{4,29},{5,28},{6,31},{7,30},{8,17},{9,... | collective-permute-start | bytes 98312 | tf_op jit(solution)/shard_map/ppermute | solution.py:138
  17.5 3.9 %collective-permute-start.5 = (bf16[128,128]{1,0:T(8,128)(2,1)S(1)}, bf16[128,128]{1,0:T(8,128)(2,1)S(1)}, u32[]{:S(2)}, u32[]{:S(2)}) collective-permute-start(bf16[128,128]{1,0:T(8,128)(2,1)S(1)} %fusion.17), channel_id=1, source_target_pairs={{0,16},{1,17},{2,18},{3,19},{4,20},{5,21},{6,22},{7,23},{8,24},{9,... | collective-permute-start | bytes 98312 | tf_op jit(solution)/shard_map/ppermute | solution.py:138
  18.0 5.1 %collective-permute-start.6 = (bf16[128,128]{1,0:T(8,128)(2,1)S(1)}, bf16[128,128]{1,0:T(8,128)(2,1)S(1)}, u32[]{:S(2)}, u32[]{:S(2)}) collective-permute-start(bf16[128,128]{1,0:T(8,128)(2,1)S(1)} %fusion.17), channel_id=1, source_target_pairs={{0,9},{1,8},{2,11},{3,10},{4,13},{5,12},{6,15},{7,14},{8,1},{9,0},... | collective-permute-start | bytes 98312 | tf_op jit(solution)/shard_map/ppermute | solution.py:138
  23.2 4.0 %collective-permute-start.8 = (bf16[128,128]{1,0:T(8,128)(2,1)S(1)}, bf16[128,128]{1,0:T(8,128)(2,1)S(1)}, u32[]{:S(2)}, u32[]{:S(2)}) collective-permute-start(bf16[128,128]{1,0:T(8,128)(2,1)S(1)} %get-tuple-element.99), channel_id=1, source_target_pairs={{0,4},{1,5},{2,6},{3,7},{4,0},{5,1},{6,2},{7,3},{8,12},{9,13},{10,... | collective-permute-start | bytes 98312 | tf_op jit(solution)/shard_map/ppermute | solution.py:138
  23.3 3.9 %collective-permute-start.7 = (bf16[128,128]{1,0:T(8,128)(2,1)S(1)}, bf16[128,128]{1,0:T(8,128)(2,1)S(1)}, u32[]{:S(2)}, u32[]{:S(2)}) collective-permute-start(bf16[128,128]{1,0:T(8,128)(2,1)S(1)} %get-tuple-element.98), channel_id=1, source_target_pairs={{0,3},{1,2},{2,1},{3,0},{4,7},{5,6},{6,5},{7,4},{8,11},{9,10},{10,... | collective-permute-start | bytes 98312 | tf_op jit(solution)/shard_map/ppermute | solution.py:138
  23.6 4.6 %collective-permute-start.9 = (bf16[128,128]{1,0:T(8,128)(2,1)S(1)}, bf16[128,128]{1,0:T(8,128)(2,1)S(1)}, u32[]{:S(2)}, u32[]{:S(2)}) collective-permute-start(bf16[128,128]{1,0:T(8,128)(2,1)S(1)} %get-tuple-element.107), channel_id=1, source_target_pairs={{0,7},{1,6},{2,5},{3,4},{4,3},{5,2},{6,1},{7,0},{8,15},{9,14},{10,... | collective-permute-start | bytes 98312 | tf_op jit(solution)/shard_map/ppermute | solution.py:138
  27.2 1.3 %copy-start.5 = (bf16[256,1024]{1,0:T(8,128)(2,1)S(1)}, bf16[256,1024]{1,0:T(8,128)(2,1)}, u32[]{:S(2)}) copy-start(bf16[256,1024]{1,0:T(8,128)(2,1)} %g_ref.3) | copy-start | bytes 1572868
  28.3 1.4 %collective-permute-start.10 = (bf16[4,128,128]{2,1,0:T(8,128)(2,1)S(1)}, bf16[4,128,128]{2,1,0:T(8,128)(2,1)S(1)}, u32[]{:S(2)}, u32[]{:S(2)}) collective-permute-start(bf16[4,128,128]{2,1,0:T(8,128)(2,1)S(1)} %get-tuple-element.102), channel_id=1, source_target_pairs={{0,1},{1,0},{2,3},{3,2},{4,5},{5,4},{6,7},{7,6},{8,9},{9,8},{10,11... | collective-permute-start | bytes 393224 | tf_op jit(solution)/shard_map/ppermute | solution.py:138
  29.2 1.4 %collective-permute-start.11 = (bf16[4,128,128]{2,1,0:T(8,128)(2,1)S(1)}, bf16[4,128,128]{2,1,0:T(8,128)(2,1)S(1)}, u32[]{:S(2)}, u32[]{:S(2)}) collective-permute-start(bf16[4,128,128]{2,1,0:T(8,128)(2,1)S(1)} %get-tuple-element.58), channel_id=1, source_target_pairs={{0,1},{1,0},{2,3},{3,2},{4,5},{5,4},{6,7},{7,6},{8,9},{9,8},{10,11... | collective-permute-start | bytes 393224 | tf_op jit(solution)/shard_map/ppermute | solution.py:138
  30.4 0.7 %copy-start.8 = (bf16[4,256,128]{2,1,0:T(8,128)(2,1)}, bf16[4,256,128]{2,1,0:T(8,128)(2,1)S(1)}, u32[]{:S(2)}) copy-start(bf16[4,256,128]{2,1,0:T(8,128)(2,1)S(1)} %get-tuple-element.73.att_ref) | copy-start | bytes 786436
  30.4 0.8 %copy-start.10 = (bf16[4,256,128]{2,1,0:T(8,128)(2,1)}, bf16[4,256,128]{2,1,0:T(8,128)(2,1)S(1)}, u32[]{:S(2)}) copy-start(bf16[4,256,128]{2,1,0:T(8,128)(2,1)S(1)} %get-tuple-element.74.gm_ref) | copy-start | bytes 786436
  30.6 0.6 %copy-start.14 = (bf16[4,128,128]{2,1,0:T(8,128)(2,1)}, bf16[4,128,128]{2,1,0:T(8,128)(2,1)S(1)}, u32[]{:S(2)}) copy-start(bf16[4,128,128]{2,1,0:T(8,128)(2,1)S(1)} %collective-permute-done.11) | copy-start | bytes 393220
  31.3 7.6 %copy-start.12 = (f32[4,128,128]{2,1,0:T(8,128)}, f32[4,128,128]{2,1,0:T(8,128)S(1)}, u32[]{:S(2)}) copy-start(f32[4,128,128]{2,1,0:T(8,128)S(1)} %get-tuple-element.93) | copy-start | bytes 786436
  31.3 5.9 %collective-permute-start.12 = (bf16[128,128]{1,0:T(8,128)(2,1)S(1)}, bf16[128,128]{1,0:T(8,128)(2,1)S(1)}, u32[]{:S(2)}, u32[]{:S(2)}) collective-permute-start(bf16[128,128]{1,0:T(8,128)(2,1)S(1)} %get-tuple-element.110), channel_id=1, source_target_pairs={{0,3},{1,2},{2,1},{3,0},{4,7},{5,6},{6,5},{7,4},{8,11},{9,10},{10,... | collective-permute-start | bytes 98312 | tf_op jit(solution)/shard_map/ppermute | solution.py:138
  32.6 4.6 %collective-permute-start.13 = (bf16[128,128]{1,0:T(8,128)(2,1)S(1)}, bf16[128,128]{1,0:T(8,128)(2,1)S(1)}, u32[]{:S(2)}, u32[]{:S(2)}) collective-permute-start(bf16[128,128]{1,0:T(8,128)(2,1)S(1)} %get-tuple-element.109), channel_id=1, source_target_pairs={{0,4},{1,5},{2,6},{3,7},{4,0},{5,1},{6,2},{7,3},{8,12},{9,13},{10,... | collective-permute-start | bytes 98312 | tf_op jit(solution)/shard_map/ppermute | solution.py:138
  34.5 4.3 %collective-permute-start.14 = (bf16[128,128]{1,0:T(8,128)(2,1)S(1)}, bf16[128,128]{1,0:T(8,128)(2,1)S(1)}, u32[]{:S(2)}, u32[]{:S(2)}) collective-permute-start(bf16[128,128]{1,0:T(8,128)(2,1)S(1)} %get-tuple-element.108), channel_id=1, source_target_pairs={{0,7},{1,6},{2,5},{3,4},{4,3},{5,2},{6,1},{7,0},{8,15},{9,14},{10,... | collective-permute-start | bytes 98312 | tf_op jit(solution)/shard_map/ppermute | solution.py:138
  36.4 0.8 %copy-start.6 = (f32[4,256,128]{2,1,0:T(8,128)}, f32[4,256,128]{2,1,0:T(8,128)S(1)}, u32[]{:S(2)}) copy-start(f32[4,256,128]{2,1,0:T(8,128)S(1)} %get-tuple-element.82.vl_ref) | copy-start | bytes 1572868
  37.2 2.3 %copy-start.16 = (bf16[128,128]{1,0:T(8,128)(2,1)}, bf16[128,128]{1,0:T(8,128)(2,1)S(1)}, u32[]{:S(2)}) copy-start(bf16[128,128]{1,0:T(8,128)(2,1)S(1)} %collective-permute-done.12) | copy-start | bytes 98308
  37.2 2.3 %copy-start.18 = (bf16[128,128]{1,0:T(8,128)(2,1)}, bf16[128,128]{1,0:T(8,128)(2,1)S(1)}, u32[]{:S(2)}) copy-start(bf16[128,128]{1,0:T(8,128)(2,1)S(1)} %collective-permute-done.13) | copy-start | bytes 98308
  38.9 0.6 %copy-start.20 = (bf16[128,128]{1,0:T(8,128)(2,1)}, bf16[128,128]{1,0:T(8,128)(2,1)S(1)}, u32[]{:S(2)}) copy-start(bf16[128,128]{1,0:T(8,128)(2,1)S(1)} %collective-permute-done.14) | copy-start | bytes 98308
  39.5 7.7 %collective-permute-start.15 = (bf16[128,128]{1,0:T(8,128)(2,1)}, bf16[128,128]{1,0:T(8,128)(2,1)}, u32[]{:S(2)}, u32[]{:S(2)}) collective-permute-start(bf16[128,128]{1,0:T(8,128)(2,1)} %fusion.31), channel_id=1, source_target_pairs={{0,25},{1,24},{2,27},{3,26},{4,29},{5,28},{6,31},{7,30},{8,17},{9,... | collective-permute-start | bytes 98312 | tf_op jit(solution)/shard_map/ppermute | solution.py:138
  39.8 7.4 %collective-permute-start.16 = (bf16[128,128]{1,0:T(8,128)(2,1)}, bf16[128,128]{1,0:T(8,128)(2,1)}, u32[]{:S(2)}, u32[]{:S(2)}) collective-permute-start(bf16[128,128]{1,0:T(8,128)(2,1)} %fusion.31), channel_id=1, source_target_pairs={{0,16},{1,17},{2,18},{3,19},{4,20},{5,21},{6,22},{7,23},{8,24},{9,... | collective-permute-start | bytes 98312 | tf_op jit(solution)/shard_map/ppermute | solution.py:138
  41.2 6.0 %collective-permute-start.17 = (bf16[128,128]{1,0:T(8,128)(2,1)}, bf16[128,128]{1,0:T(8,128)(2,1)}, u32[]{:S(2)}, u32[]{:S(2)}) collective-permute-start(bf16[128,128]{1,0:T(8,128)(2,1)} %fusion.31), channel_id=1, source_target_pairs={{0,9},{1,8},{2,11},{3,10},{4,13},{5,12},{6,15},{7,14},{8,1},{9,0},... | collective-permute-start | bytes 98312 | tf_op jit(solution)/shard_map/ppermute | solution.py:138
  43.4 0.9 %copy-start.9 = (bf16[4,256,128]{2,1,0:T(8,128)(2,1)S(1)}, bf16[4,256,128]{2,1,0:T(8,128)(2,1)}, u32[]{:S(2)}) copy-start(bf16[4,256,128]{2,1,0:T(8,128)(2,1)} %copy-done.8) | copy-start | bytes 786436
  44.4 0.9 %copy-start.11 = (bf16[4,256,128]{2,1,0:T(8,128)(2,1)S(1)}, bf16[4,256,128]{2,1,0:T(8,128)(2,1)}, u32[]{:S(2)}) copy-start(bf16[4,256,128]{2,1,0:T(8,128)(2,1)} %copy-done.10) | copy-start | bytes 786436
  45.3 1.9 %copy-start.13 = (f32[4,128,128]{2,1,0:T(8,128)S(1)}, f32[4,128,128]{2,1,0:T(8,128)}, u32[]{:S(2)}) copy-start(f32[4,128,128]{2,1,0:T(8,128)} %copy-done.12) | copy-start | bytes 786436
  45.3 1.9 %copy-start.17 = (bf16[128,128]{1,0:T(8,128)(2,1)S(1)}, bf16[128,128]{1,0:T(8,128)(2,1)}, u32[]{:S(2)}) copy-start(bf16[128,128]{1,0:T(8,128)(2,1)} %copy-done.16) | copy-start | bytes 98308
  45.3 1.9 %copy-start.19 = (bf16[128,128]{1,0:T(8,128)(2,1)S(1)}, bf16[128,128]{1,0:T(8,128)(2,1)}, u32[]{:S(2)}) copy-start(bf16[128,128]{1,0:T(8,128)(2,1)} %copy-done.18) | copy-start | bytes 98308
  45.3 1.9 %copy-start.21 = (bf16[128,128]{1,0:T(8,128)(2,1)S(1)}, bf16[128,128]{1,0:T(8,128)(2,1)}, u32[]{:S(2)}) copy-start(bf16[128,128]{1,0:T(8,128)(2,1)} %copy-done.20) | copy-start | bytes 98308
  48.1 4.2 %collective-permute-start.19 = (bf16[128,128]{1,0:T(8,128)(2,1)S(1)}, bf16[128,128]{1,0:T(8,128)(2,1)S(1)}, u32[]{:S(2)}, u32[]{:S(2)}) collective-permute-start(bf16[128,128]{1,0:T(8,128)(2,1)S(1)} %get-tuple-element.97), channel_id=1, source_target_pairs={{0,4},{1,5},{2,6},{3,7},{4,0},{5,1},{6,2},{7,3},{8,12},{9,13},{10,... | collective-permute-start | bytes 98312 | tf_op jit(solution)/shard_map/ppermute | solution.py:138
  48.2 4.2 %collective-permute-start.18 = (bf16[128,128]{1,0:T(8,128)(2,1)S(1)}, bf16[128,128]{1,0:T(8,128)(2,1)S(1)}, u32[]{:S(2)}, u32[]{:S(2)}) collective-permute-start(bf16[128,128]{1,0:T(8,128)(2,1)S(1)} %get-tuple-element.96), channel_id=1, source_target_pairs={{0,3},{1,2},{2,1},{3,0},{4,7},{5,6},{6,5},{7,4},{8,11},{9,10},{10,... | collective-permute-start | bytes 98312 | tf_op jit(solution)/shard_map/ppermute | solution.py:138
  50.6 4.4 %copy-start.15 = (bf16[4,128,128]{2,1,0:T(8,128)(2,1)S(1)}, bf16[4,128,128]{2,1,0:T(8,128)(2,1)}, u32[]{:S(2)}) copy-start(bf16[4,128,128]{2,1,0:T(8,128)(2,1)} %copy-done.14) | copy-start | bytes 393220
  50.6 4.4 %collective-permute-start.20 = (bf16[128,128]{1,0:T(8,128)(2,1)S(1)}, bf16[128,128]{1,0:T(8,128)(2,1)S(1)}, u32[]{:S(2)}, u32[]{:S(2)}) collective-permute-start(bf16[128,128]{1,0:T(8,128)(2,1)S(1)} %get-tuple-element.105), channel_id=1, source_target_pairs={{0,7},{1,6},{2,5},{3,4},{4,3},{5,2},{6,1},{7,0},{8,15},{9,14},{10,... | collective-permute-start | bytes 98312 | tf_op jit(solution)/shard_map/ppermute | solution.py:138
  55.1 1.4 %collective-permute-start.21 = (bf16[4,128,128]{2,1,0:T(8,128)(2,1)S(1)}, bf16[4,128,128]{2,1,0:T(8,128)(2,1)S(1)}, u32[]{:S(2)}, u32[]{:S(2)}) collective-permute-start(bf16[4,128,128]{2,1,0:T(8,128)(2,1)S(1)} %get-tuple-element.101), channel_id=1, source_target_pairs={{0,1},{1,0},{2,3},{3,2},{4,5},{5,4},{6,7},{7,6},{8,9},{9,8},{10,11... | collective-permute-start | bytes 393224 | tf_op jit(solution)/shard_map/ppermute | solution.py:138
  55.2 1.2 %copy-start.7 = (f32[4,256,128]{2,1,0:T(8,128)S(1)}, f32[4,256,128]{2,1,0:T(8,128)}, u32[]{:S(2)}) copy-start(f32[4,256,128]{2,1,0:T(8,128)} %copy-done.6) | copy-start | bytes 1572868

commit v3 on v2

--- a/solution.py
+++ b/solution.py
@@ -1,4 +1,5 @@
 import functools
+import math
 
 import jax
 import jax.numpy as jnp
@@ -31,8 +32,12 @@
     smem = pl.BlockSpec(memory_space=pltpu.SMEM)
     vmem = pl.BlockSpec(memory_space=pltpu.VMEM)
     hbm = pl.BlockSpec(memory_space=pltpu.HBM)
-    shapes = [jax.ShapeDtypeStruct(shape, dtype) for shape, dtype in outs]
-    size = sum(a.size * a.dtype.itemsize for a in (*args, *shapes))
+    shapes = [
+        jax.ShapeDtypeStruct(shape, dtype) if i < out_hbm else pltpu.VMEM(shape, dtype)
+        for i, (shape, dtype) in enumerate(outs)
+    ]
+    size = sum(math.prod(a.shape) * jnp.dtype(a.dtype).itemsize for a in (*args, *shapes))
+    args = [pltpu.with_memory_space_constraint(a, pltpu.HBM) if i in in_hbm else a for i, a in enumerate(args)]
     specs = [smem if a.dtype == jnp.int32 else hbm if i in in_hbm else vmem for i, a in enumerate(args)]
     return pl.pallas_call(
         kernel,
@@ -41,34 +46,41 @@
         out_specs=[hbm if i < out_hbm else vmem for i in range(len(shapes))],
         scratch_shapes=list(scratch),
         input_output_aliases=aliases or {},
-        compiler_params=pltpu.CompilerParams(vmem_limit_bytes=32 * 1024 * 1024),
+        compiler_params=pltpu.CompilerParams(vmem_limit_bytes=12 * 1024 * 1024),
         cost_estimate=pl.CostEstimate(flops=flops, bytes_accessed=size, transcendentals=0),
     )(*args)
 
 
-def state_kernel(base, key_ref, k_hbm, v_hbm, out_ref, k_buf, v_buf, sems):
-    key = key_ref[0]
+def send_kernel(key_ref, k_hbm, v_hbm, out_ref, k_ref, v_ref, sems):
+    key = key_ref[0]
+    half = out_ref.shape[0]
     copies = []
+    for part in range(2):
+        start = pl.multiple_of(((1 - part) * half ^ (key & half)) * HD, half * HD)
+        cols = pl.ds(start, half * HD)
+        for at, (hbm, ref) in enumerate(((k_hbm, k_ref), (v_hbm, v_ref))):
+            copies.append(pltpu.make_async_copy(hbm.at[:, cols], ref.at[:, cols], sems.at[part, at]))
+            copies[-1].start()
+    for copy in copies[:2]:
+        copy.wait()
+    for j in range(half):
+        cols = columns(half + j, key)
+        out_ref[j] = dot(k_ref[:, cols], v_ref[:, cols], 0, 0).astype(BF16)
+    for copy in copies[2:]:
+        copy.wait()
+
+
+def own_kernel(key_ref, k_ref, v_ref, out_ref):
+    key = key_ref[0]
     for j in range(out_ref.shape[0]):
-        cols = columns(base + j, key)
-        pair = (
-            pltpu.make_async_copy(k_hbm.at[:, cols], k_buf.at[j], sems.at[0, j]),
-            pltpu.make_async_copy(v_hbm.at[:, cols], v_buf.at[j], sems.at[1, j]),
-        )
-        for copy in pair:
-            copy.start()
-        copies.append(pair)
-    for j, pair in enumerate(copies):
-        for copy in pair:
-            copy.wait()
-        out_ref[j] = dot(k_buf[j], v_buf[j], 0, 0).astype(out_ref.dtype)
-
-
-def local_kernel(key_ref, q_ref, k_ref, v_ref, mixed_ref, turned_ref, scores_ref):
+        cols = columns(j, key)
+        out_ref[j] = dot(k_ref[:, cols], v_ref[:, cols], 0, 0).astype(BF16)
+
+
+def local_kernel(key_ref, q_ref, k_ref, v_ref, mixed_ref, turned_ref):
     key = key_ref[0]
     rows = q_ref.shape[0]
     low = triangle(rows, True)
-    high = triangle(rows, False)
     for s in range(mixed_ref.shape[0]):
         cols = columns(s, key)
         q = q_ref[:, cols]
@@ -76,7 +88,6 @@
         scores = jnp.where(low, dot(q, k, 1, 1), 0.0).astype(BF16)
         mixed_ref[s] = dot(scores, v_ref[:, cols], 1, 0)
         turned_ref[s] = q.T
-        scores_ref[s] = jnp.where(high, dot(k, q, 1, 1), 0.0).astype(BF16)
 
 
 def norm_kernel(base, key_ref, q_ref, g_ref, turned_ref, mixed_ref, e_ref, att_ref, gm_ref, state_ref):
@@ -93,7 +104,7 @@
         state_ref[j] = dot(turned_ref[base + j], gm, 1, 0).astype(state_ref.dtype)
 
 
-def grads_kernel(base, key_ref, q_ref, k_ref, v_ref, att_ref, gm_ref, e_ref, scores_ref, *refs):
+def grads_kernel(base, key_ref, q_ref, k_ref, v_ref, att_ref, gm_ref, e_ref, *refs):
     att_hbm, gq_hbm, kl_ref, vl_ref, gq_buf, sems = refs[-6:]
     key = key_ref[0]
     rows = q_ref.shape[0]
@@ -104,15 +115,18 @@
         cols = columns(base + j, key)
         copies.append(pltpu.make_async_copy(att_ref.at[j], att_hbm.at[:, cols], sems.at[0, j]))
         copies[-1].start()
+        q = q_ref[:, cols]
+        k = k_ref[:, cols]
         v = v_ref[:, cols]
         gm = gm_ref[j]
         gs = jnp.where(low, dot(gm, v, 1, 1), 0.0).astype(BF16)
-        gq_buf[j] = (dot(gs, k_ref[:, cols], 1, 0) + dot(gm, e_ref[j], 1, 1)).astype(BF16)
+        gq_buf[j] = (dot(gs, k, 1, 0) + dot(gm, e_ref[j], 1, 1)).astype(BF16)
         copies.append(pltpu.make_async_copy(gq_buf.at[j], gq_hbm.at[:, cols], sems.at[1, j]))
         copies[-1].start()
         gs_turned = jnp.where(high, dot(v, gm, 1, 1), 0.0).astype(BF16)
-        kl_ref[j] = dot(gs_turned, q_ref[:, cols], 1, 0)
-        vl_ref[j] = dot(scores_ref[base + j], gm, 1, 0)
+        kl_ref[j] = dot(gs_turned, q, 1, 0).astype(BF16)
+        scores = jnp.where(high, dot(k, q, 1, 1), 0.0).astype(BF16)
+        vl_ref[j] = dot(scores, gm, 1, 0).astype(BF16)
     for copy in copies:
         copy.wait()
 
@@ -179,6 +193,7 @@
         return jnp.where(condition, array, 0.0)
 
     chip = place >> 1
+    own = own.astype(F32)
     total = own + from_core
     rounded = total.astype(BF16)
     arrived = [swap(rounded[j], SCATTER[j - 1], count) for j in (1, 2, 3)]
@@ -228,26 +243,23 @@
     dma = pltpu.SemaphoreType.DMA((2, half))
     buffer = pltpu.VMEM(block, BF16)
 
-    def state(base, dtype, key):
-        return call(
-            functools.partial(state_kernel, base), [((half, HD, HD), dtype)], (key, key_rows, value_rows),
-            work, in_hbm=(1, 2), scratch=(buffer, buffer, dma),
-        )[0]
-
     def tied(tie):
         return lax.optimization_barrier((key, tie))[0]
 
     def local(tie):
         return call(
             local_kernel,
-            [((heads, rows, HD), F32), ((heads, HD, rows), BF16), ((heads, rows, rows), BF16)],
-            (tied(tie), query_rows, key_rows, value_rows), 6 * scores,
+            [((heads, rows, HD), F32), ((heads, HD, rows), BF16)],
+            (tied(tie), query_rows, keys, values), 4 * scores,
         )
 
-    send = state(half, BF16, key)
-    own = state(0, F32, tied(send))
+    send, keys, values = call(
+        send_kernel, [((half, HD, HD), BF16), (flat, BF16), (flat, BF16)], (key, key_rows, value_rows),
+        work, in_hbm=(1, 2), scratch=(pltpu.SemaphoreType.DMA((2, 2)),),
+    )
+    (own,) = call(own_kernel, [((half, HD, HD), BF16)], (tied(send), keys, values), work)
     from_core = swap(send, 1, count).astype(F32)
-    mine, theirs, (_, (mixed, turned, turned_scores), _) = scan_states(
+    mine, theirs, (_, (mixed, turned), _) = scan_states(
         own, from_core, place, count, False, (None, local, None)
     )
     e_other = swap(theirs, 1, count)
@@ -261,14 +273,14 @@
 
     att_mine, gm_mine, send = norm(0, key, mine, BF16)
     from_core = swap(send, 1, count).astype(F32)
-    att_other, gm_other, own = norm(half, tied(send), e_other, F32)
+    att_other, gm_other, own = norm(half, tied(send), e_other, BF16)
 
     def grads(base, key, att, gm, e, outs):
-        n = 8
+        n = 7
         return call(
             functools.partial(grads_kernel, base),
-            [(flat, BF16), (flat, BF16), (block, F32), (block, F32)],
-            (key, query_rows, key_rows, value_rows, att, gm, e, turned_scores, *outs),
+            [(flat, BF16), (flat, BF16), (block, BF16), (block, BF16)],
+            (key, query_rows, keys, values, att, gm, e, *outs),
             4 * scores + work, out_hbm=2, in_hbm=(n, n + 1), scratch=(buffer, dma),
             aliases={n: 0, n + 1: 1} if outs else None,
         )
@@ -295,7 +307,7 @@
         return call(
             functools.partial(last_kernel, base),
             [(flat, BF16), (flat, BF16)],
-            (key, key_rows, value_rows, kl, vl, later, *outs),
+            (key, keys, values, kl, vl, later, *outs),
             2 * work, out_hbm=2, in_hbm=(n, n + 1), scratch=(buffer, buffer, dma),
             aliases={n: 0, n + 1: 1} if outs else None,
         )

time: 57.9 us -> 51.6 us (0.89)
  local copies, waits for them, and re-layouts: 5.47 us -> 0.03 us
  waiting for transfers between devices: 14.3 us -> 16.7 us
  other arithmetic: 2.74 us -> 0.54 us
  Pallas kernels: 10.8 us -> 9.81 us
    unnamed x44 -> x4, local copies, waits for them, and re-layouts: 5.45 us -> 0.01 us
    ppermute x22, waiting for transfers between devices: 14.3 us -> 16.7 us  [swap(): return lax.ppermute(array, AXES, [(i, i ^ mask) for i in range(count)])]
    pallas_call x9, Pallas kernels: 10.8 us -> 9.81 us  [call(): pl.pallas_call(kernel, out_shape=shapes, in_specs=specs, out_specs=[hbm i...]
    convert_element_type x2, other arithmetic: 0.92 us -> 0.12 us  [scan_states(): rounded = [value.astype(BF16) for value in sums[1:]]]
    another operation x8, other arithmetic: 0.95 us -> 0.16 us  [scan_states(): entering = jnp.stack([sums[0], *(a.astype(F32) for a in arrived)])]
    convert_element_type x2, other arithmetic: 0.65 us -> 0.04 us  [scan_states(): rounded = cluster.astype(BF16)]
  transfers between devices with their start and end apart: 22 -> 22, of which waited for: 12 -> 15; matrix products, arithmetic and copies ran while one was open for 2% -> 0% of each run, Pallas kernels for 15% -> 14%
where the time goes in v3:
time: 51.6 us; the launch traced here: 51.4 us
  starting transfers between devices  23.5 us (46%)
  waiting for transfers between devices  16.7 us (32%)
  Pallas kernels  9.81 us (19%)
  between operations  0.85 us (2%)
  other arithmetic  0.54 us (1%)
    ppermute x22, starting transfers between devices, swap(): return lax.ppermute(array, AXES, [(i, i ^ mask) for i in range(count)])  23.5 us
    ppermute x22, waiting for transfers between devices, swap(): return lax.ppermute(array, AXES, [(i, i ^ mask) for i in range(count)])  16.7 us
    pallas_call x9, Pallas kernels, call(): pl.pallas_call(kernel, out_shape=shapes, in_specs=specs, out_specs=[hbm i...  9.81 us
  transfers between devices with their start and end apart: 22, of which 15 were waited for; matrix products, arithmetic and copies ran while one was open for 0% of the time, Pallas kernels for 14%

profile of v3, /device:TPU:0, one launch (start us, length us, event | category | flops | bytes accessed | tf_op | source)
XLA Modules:
  0.0 51.4 jit_solution(12111972607670773350)
XLA Ops:
  0.6 1.4 %shard_map.75 = (bf16[4,128,128]{2,1,0:T(8,128)(2,1)S(1)}, bf16[256,1024]{1,0:T(8,128)(2,1)S(1)}, bf16[256,1024]{1,0:T(8,128)(2,1)S(1)}) custom-call(s32[1]{0:T(128)} %bitcast.key_ref, bf16[256,1024]{1,0:T(8,128)(2,1)} %k_hbm.1, bf16[256,1024]{1,0:T(8,128)(2,1)} %v_hbm.1), custom_call_target="tpu_custom_call" | custom-call | flops 33554432 | bytes 2228228 | tf_op jit(solution)/shard_map/pallas_call | solution.py:42
  2.0 0.5 %collective-permute-start = (bf16[4,128,128]{2,1,0:T(8,128)(2,1)S(1)}, bf16[4,128,128]{2,1,0:T(8,128)(2,1)S(1)}, u32[]{:S(2)}, u32[]{:S(2)}) collective-permute-start(bf16[4,128,128]{2,1,0:T(8,128)(2,1)S(1)} %get-tuple-element.49), channel_id=1, source_target_pairs={{0,1},{1,0},{2,3},{3,2},{4,5},{5,4},{6,7},{7,6},{8,9},{9,8},{10,11... | collective-permute-start | bytes 393224 | tf_op jit(solution)/shard_map/ppermute | solution.py:152
  2.6 0.3 shard_map.76
  2.9 0.0 copy-start
  2.9 0.7 %collective-permute-done = bf16[4,128,128]{2,1,0:T(8,128)(2,1)S(1)} collective-permute-done((bf16[4,128,128]{2,1,0:T(8,128)(2,1)S(1)}, bf16[4,128,128]{2,1,0:T(8,128)(2,1)S(1)}, u32[]{:S(2)}, u32[]{:S(2)}) %collective-permute-start) | collective-permute-done | bytes 131104 | tf_op jit(solution)/shard_map/ppermute | solution.py:152
  3.6 2.7 %collective-permute-start.1 = (bf16[128,128]{1,0:T(8,128)(2,1)S(1)}, bf16[128,128]{1,0:T(8,128)(2,1)S(1)}, u32[]{:S(2)}, u32[]{:S(2)}) collective-permute-start(bf16[128,128]{1,0:T(8,128)(2,1)S(1)} %get-tuple-element.113), channel_id=1, source_target_pairs={{0,3},{1,2},{2,1},{3,0},{4,7},{5,6},{6,5},{7,4},{8,11},{9,10},{10,... | collective-permute-start | bytes 98312 | tf_op jit(solution)/shard_map/ppermute | solution.py:152
  6.3 1.6 %collective-permute-start.2 = (bf16[128,128]{1,0:T(8,128)(2,1)S(1)}, bf16[128,128]{1,0:T(8,128)(2,1)S(1)}, u32[]{:S(2)}, u32[]{:S(2)}) collective-permute-start(bf16[128,128]{1,0:T(8,128)(2,1)S(1)} %get-tuple-element.115), channel_id=1, source_target_pairs={{0,4},{1,5},{2,6},{3,7},{4,0},{5,1},{6,2},{7,3},{8,12},{9,13},{10,... | collective-permute-start | bytes 98312 | tf_op jit(solution)/shard_map/ppermute | solution.py:152
  7.9 0.0 collective-permute-start.3
  7.9 0.0 collective-permute-done.1
  7.9 2.3 %collective-permute-done.2 = bf16[128,128]{1,0:T(8,128)(2,1)S(1)} collective-permute-done((bf16[128,128]{1,0:T(8,128)(2,1)S(1)}, bf16[128,128]{1,0:T(8,128)(2,1)S(1)}, u32[]{:S(2)}, u32[]{:S(2)}) %collective-permute-start.2) | collective-permute-done | bytes 32800 | tf_op jit(solution)/shard_map/ppermute | solution.py:152
  10.2 2.0 %collective-permute-done.3 = bf16[128,128]{1,0:T(8,128)(2,1)S(1)} collective-permute-done((bf16[128,128]{1,0:T(8,128)(2,1)S(1)}, bf16[128,128]{1,0:T(8,128)(2,1)S(1)}, u32[]{:S(2)}, u32[]{:S(2)}) %collective-permute-start.3) | collective-permute-done | bytes 32800 | tf_op jit(solution)/shard_map/ppermute | solution.py:152
  12.2 3.3 %collective-permute-start.4 = (bf16[128,128]{1,0:T(8,128)(2,1)S(1)}, bf16[128,128]{1,0:T(8,128)(2,1)S(1)}, u32[]{:S(2)}, u32[]{:S(2)}) collective-permute-start(bf16[128,128]{1,0:T(8,128)(2,1)S(1)} %fusion.21), channel_id=1, source_target_pairs={{0,25},{1,24},{2,27},{3,26},{4,29},{5,28},{6,31},{7,30},{8,17},{9,... | collective-permute-start | bytes 98312 | tf_op jit(solution)/shard_map/ppermute | solution.py:152
  15.6 0.5 collective-permute-start.5
  16.1 0.1 collective-permute-start.6
  16.1 0.0 copy-done
  16.1 0.9 %shard_map.77 = (f32[8,256,128]{2,1,0:T(8,128)S(1)}, bf16[8,128,256]{2,1,0:T(8,128)(2,1)S(1)}) custom-call(s32[1]{0:T(128)} %bitcast.key_ref, bf16[256,1024]{1,0:T(8,128)(2,1)S(1)} %copy-done, bf16[256,1024]{1,0:T(8,128)(2,1)S(1)} %get-tuple-element.51.k_ref, bf16[256,1024]{1,0:T(8,128)(2,1)S(1)} %get-tuple-element.52.v_ref), custom_call_target="tpu_custom_call" | custom-call | flops 268435456 | bytes 3145732 | tf_op jit(solution)/shard_map/pallas_call | solution.py:42
  17.1 1.3 %collective-permute-done.4 = bf16[128,128]{1,0:T(8,128)(2,1)S(1)} collective-permute-done((bf16[128,128]{1,0:T(8,128)(2,1)S(1)}, bf16[128,128]{1,0:T(8,128)(2,1)S(1)}, u32[]{:S(2)}, u32[]{:S(2)}) %collective-permute-start.4) | collective-permute-done | bytes 32800 | tf_op jit(solution)/shard_map/ppermute | solution.py:152
  18.3 1.1 %collective-permute-done.5 = bf16[128,128]{1,0:T(8,128)(2,1)S(1)} collective-permute-done((bf16[128,128]{1,0:T(8,128)(2,1)S(1)}, bf16[128,128]{1,0:T(8,128)(2,1)S(1)}, u32[]{:S(2)}, u32[]{:S(2)}) %collective-permute-start.5) | collective-permute-done | bytes 32800 | tf_op jit(solution)/shard_map/ppermute | solution.py:152
  19.5 1.7 %collective-permute-done.6 = bf16[128,128]{1,0:T(8,128)(2,1)S(1)} collective-permute-done((bf16[128,128]{1,0:T(8,128)(2,1)S(1)}, bf16[128,128]{1,0:T(8,128)(2,1)S(1)}, u32[]{:S(2)}, u32[]{:S(2)}) %collective-permute-start.6) | collective-permute-done | bytes 32800 | tf_op jit(solution)/shard_map/ppermute | solution.py:152
  21.2 0.1 fusion.20
  21.3 0.1 collective-permute-start.8
  21.4 0.2 collective-permute-start.7
  21.5 0.1 fusion.11
  21.6 0.0 copy-start.1
  21.6 3.1 %collective-permute-start.9 = (bf16[128,128]{1,0:T(8,128)(2,1)S(1)}, bf16[128,128]{1,0:T(8,128)(2,1)S(1)}, u32[]{:S(2)}, u32[]{:S(2)}) collective-permute-start(bf16[128,128]{1,0:T(8,128)(2,1)S(1)} %get-tuple-element.109), channel_id=1, source_target_pairs={{0,7},{1,6},{2,5},{3,4},{4,3},{5,2},{6,1},{7,0},{8,15},{9,14},{10,... | collective-permute-start | bytes 98312 | tf_op jit(solution)/shard_map/ppermute | solution.py:152
  24.7 0.6 %collective-permute-done.8 = bf16[128,128]{1,0:T(8,128)(2,1)S(1)} collective-permute-done((bf16[128,128]{1,0:T(8,128)(2,1)S(1)}, bf16[128,128]{1,0:T(8,128)(2,1)S(1)}, u32[]{:S(2)}, u32[]{:S(2)}) %collective-permute-start.8) | collective-permute-done | bytes 32800 | tf_op jit(solution)/shard_map/ppermute | solution.py:152
  25.3 0.0 collective-permute-done.7
  25.3 1.0 %collective-permute-done.9 = bf16[128,128]{1,0:T(8,128)(2,1)S(1)} collective-permute-done((bf16[128,128]{1,0:T(8,128)(2,1)S(1)}, bf16[128,128]{1,0:T(8,128)(2,1)S(1)}, u32[]{:S(2)}, u32[]{:S(2)}) %collective-permute-start.9) | collective-permute-done | bytes 32800 | tf_op jit(solution)/shard_map/ppermute | solution.py:152
  26.3 0.1 fusion.1
  26.4 0.4 collective-permute-start.10
  26.7 0.0 copy-done.1
  26.7 0.7 %shard_map.78 = (bf16[4,256,128]{2,1,0:T(8,128)(2,1)S(1)}, bf16[4,256,128]{2,1,0:T(8,128)(2,1)S(1)}, bf16[4,128,128]{2,1,0:T(8,128)(2,1)S(1)}) custom-call(s32[1]{0:T(128)} %bitcast.key_ref, bf16[256,1024]{1,0:T(8,128)(2,1)S(1)} %copy-done, bf16[256,1024]{1,0:T(8,128)(2,1)S(1)} %copy-done.1, bf16[8,128,256]{2,1,0:T(8,128)(2,1)S(1)} %get-tuple-element.56.turned_ref, ...), custom_call_target="tpu_custom_call" | custom-call | flops 67108864 | bytes 3407876 | tf_op jit(solution)/shard_map/pallas_call | solution.py:42
  27.4 0.3 collective-permute-start.11
  27.7 0.1 collective-permute-done.10.e_ref
  27.8 0.7 %shard_map.79 = (bf16[4,256,128]{2,1,0:T(8,128)(2,1)S(1)}, bf16[4,256,128]{2,1,0:T(8,128)(2,1)S(1)}, bf16[4,128,128]{2,1,0:T(8,128)(2,1)S(1)}) custom-call(s32[1]{0:T(128)} %bitcast.key_ref, bf16[256,1024]{1,0:T(8,128)(2,1)S(1)} %copy-done, bf16[256,1024]{1,0:T(8,128)(2,1)S(1)} %copy-done.1, bf16[8,128,256]{2,1,0:T(8,128)(2,1)S(1)} %get-tuple-element.56.turned_ref, ...), custom_call_target="tpu_custom_call" | custom-call | flops 67108864 | bytes 3407876 | tf_op jit(solution)/shard_map/pallas_call | solution.py:42
  28.5 0.4 collective-permute-done.11
  28.9 1.2 %collective-permute-start.12 = (bf16[128,128]{1,0:T(8,128)(2,1)S(1)}, bf16[128,128]{1,0:T(8,128)(2,1)S(1)}, u32[]{:S(2)}, u32[]{:S(2)}) collective-permute-start(bf16[128,128]{1,0:T(8,128)(2,1)S(1)} %get-tuple-element.112), channel_id=1, source_target_pairs={{0,3},{1,2},{2,1},{3,0},{4,7},{5,6},{6,5},{7,4},{8,11},{9,10},{10,... | collective-permute-start | bytes 98312 | tf_op jit(solution)/shard_map/ppermute | solution.py:152
  30.1 1.9 %collective-permute-start.13 = (bf16[128,128]{1,0:T(8,128)(2,1)S(1)}, bf16[128,128]{1,0:T(8,128)(2,1)S(1)}, u32[]{:S(2)}, u32[]{:S(2)}) collective-permute-start(bf16[128,128]{1,0:T(8,128)(2,1)S(1)} %get-tuple-element.111), channel_id=1, source_target_pairs={{0,4},{1,5},{2,6},{3,7},{4,0},{5,1},{6,2},{7,3},{8,12},{9,13},{10,... | collective-permute-start | bytes 98312 | tf_op jit(solution)/shard_map/ppermute | solution.py:152
  32.0 0.0 collective-permute-start.14
  32.0 1.9 %shard_map.80 = (bf16[256,1024]{1,0:T(8,128)(2,1)}, bf16[256,1024]{1,0:T(8,128)(2,1)}, bf16[4,256,128]{2,1,0:T(8,128)(2,1)S(1)}, bf16[4,256,128]{2,1,0:T(8,128)(2,1)S(1)}) custom-call(s32[1]{0:T(128)} %bitcast.key_ref, bf16[256,1024]{1,0:T(8,128)(2,1)S(1)} %copy-done, bf16[256,1024]{1,0:T(8,128)(2,1)S(1)} %get-tuple-element.51.k_ref, ...), custom_call_target="tpu_custom_call" | custom-call | flops 301989888 | bytes 3801092 | tf_op jit(solution)/shard_map/pallas_call | solution.py:42
  33.9 0.0 collective-permute-done.12
  33.9 0.1 collective-permute-done.13
  34.0 2.3 %collective-permute-done.14 = bf16[128,128]{1,0:T(8,128)(2,1)S(1)} collective-permute-done((bf16[128,128]{1,0:T(8,128)(2,1)S(1)}, bf16[128,128]{1,0:T(8,128)(2,1)S(1)}, u32[]{:S(2)}, u32[]{:S(2)}) %collective-permute-start.14) | collective-permute-done | bytes 32800 | tf_op jit(solution)/shard_map/ppermute | solution.py:152
  36.4 0.3 collective-permute-start.15
  36.7 1.3 %collective-permute-start.16 = (bf16[128,128]{1,0:T(8,128)(2,1)S(1)}, bf16[128,128]{1,0:T(8,128)(2,1)S(1)}, u32[]{:S(2)}, u32[]{:S(2)}) collective-permute-start(bf16[128,128]{1,0:T(8,128)(2,1)S(1)} %fusion.35), channel_id=1, source_target_pairs={{0,16},{1,17},{2,18},{3,19},{4,20},{5,21},{6,22},{7,23},{8,24},{9,... | collective-permute-start | bytes 98312 | tf_op jit(solution)/shard_map/ppermute | solution.py:152
  38.1 2.3 %collective-permute-start.17 = (bf16[128,128]{1,0:T(8,128)(2,1)S(1)}, bf16[128,128]{1,0:T(8,128)(2,1)S(1)}, u32[]{:S(2)}, u32[]{:S(2)}) collective-permute-start(bf16[128,128]{1,0:T(8,128)(2,1)S(1)} %fusion.35), channel_id=1, source_target_pairs={{0,9},{1,8},{2,11},{3,10},{4,13},{5,12},{6,15},{7,14},{8,1},{9,0},... | collective-permute-start | bytes 98312 | tf_op jit(solution)/shard_map/ppermute | solution.py:152
  40.3 1.9 %shard_map.81 = (bf16[256,1024]{1,0:T(8,128)(2,1)}, bf16[256,1024]{1,0:T(8,128)(2,1)}, bf16[4,256,128]{2,1,0:T(8,128)(2,1)S(1)}, bf16[4,256,128]{2,1,0:T(8,128)(2,1)S(1)}) custom-call(s32[1]{0:T(128)} %bitcast.key_ref, bf16[256,1024]{1,0:T(8,128)(2,1)S(1)} %copy-done, ...), custom_call_target="tpu_custom_call", output_to_operand_aliasing={{0}: (7, {}), {1}: (8, {})} | custom-call | flops 301989888 | bytes 4849668 | tf_op jit(solution)/shard_map/pallas_call | solution.py:42
  42.2 0.0 collective-permute-done.15
  42.2 0.0 collective-permute-done.16
  42.2 1.3 %collective-permute-done.17 = bf16[128,128]{1,0:T(8,128)(2,1)S(1)} collective-permute-done((bf16[128,128]{1,0:T(8,128)(2,1)S(1)}, bf16[128,128]{1,0:T(8,128)(2,1)S(1)}, u32[]{:S(2)}, u32[]{:S(2)}) %collective-permute-start.17) | collective-permute-done | bytes 32800 | tf_op jit(solution)/shard_map/ppermute | solution.py:152
  43.5 0.1 fusion.34
  43.6 0.1 collective-permute-start.19
  43.7 0.6 %collective-permute-start.18 = (bf16[128,128]{1,0:T(8,128)(2,1)S(1)}, bf16[128,128]{1,0:T(8,128)(2,1)S(1)}, u32[]{:S(2)}, u32[]{:S(2)}) collective-permute-start(bf16[128,128]{1,0:T(8,128)(2,1)S(1)} %get-tuple-element.94), channel_id=1, source_target_pairs={{0,3},{1,2},{2,1},{3,0},{4,7},{5,6},{6,5},{7,4},{8,11},{9,10},{10,... | collective-permute-start | bytes 98312 | tf_op jit(solution)/shard_map/ppermute | solution.py:152
  44.4 0.1 fusion.25
  44.4 2.6 %collective-permute-start.20 = (bf16[128,128]{1,0:T(8,128)(2,1)S(1)}, bf16[128,128]{1,0:T(8,128)(2,1)S(1)}, u32[]{:S(2)}, u32[]{:S(2)}) collective-permute-start(bf16[128,128]{1,0:T(8,128)(2,1)S(1)} %get-tuple-element.107), channel_id=1, source_target_pairs={{0,7},{1,6},{2,5},{3,4},{4,3},{5,2},{6,1},{7,0},{8,15},{9,14},{10,... | collective-permute-start | bytes 98312 | tf_op jit(solution)/shard_map/ppermute | solution.py:152
  47.0 0.6 %collective-permute-done.19 = bf16[128,128]{1,0:T(8,128)(2,1)S(1)} collective-permute-done((bf16[128,128]{1,0:T(8,128)(2,1)S(1)}, bf16[128,128]{1,0:T(8,128)(2,1)S(1)}, u32[]{:S(2)}, u32[]{:S(2)}) %collective-permute-start.19) | collective-permute-done | bytes 32800 | tf_op jit(solution)/shard_map/ppermute | solution.py:152
  47.6 0.0 collective-permute-done.18
  47.6 1.1 %collective-permute-done.20 = bf16[128,128]{1,0:T(8,128)(2,1)S(1)} collective-permute-done((bf16[128,128]{1,0:T(8,128)(2,1)S(1)}, bf16[128,128]{1,0:T(8,128)(2,1)S(1)}, u32[]{:S(2)}, u32[]{:S(2)}) %collective-permute-start.20) | collective-permute-done | bytes 32800 | tf_op jit(solution)/shard_map/ppermute | solution.py:152
  48.7 0.1 fusion.7
  48.8 0.5 collective-permute-start.21
  49.3 1.0 %shard_map.82 = (bf16[256,1024]{1,0:T(8,128)(2,1)}, bf16[256,1024]{1,0:T(8,128)(2,1)}) custom-call(s32[1]{0:T(128)} %bitcast.key_ref, bf16[256,1024]{1,0:T(8,128)(2,1)S(1)} %get-tuple-element.51.k_ref, bf16[256,1024]{1,0:T(8,128)(2,1)S(1)} %get-tuple-element.52.v_ref, bf16[4,256,128]{2,1,0:T(8,128)(2,1)S(1)} %get-tuple-element.88.kl_ref, ...), custom_call_target="tpu_custom_call" | custom-call | flops 67108864 | bytes 2752516 | tf_op jit(solution)/shard_map/pallas_call | solution.py:42
  50.4 0.0 collective-permute-done.21.l_ref
  50.4 1.0 %shard_map.83 = (bf16[256,1024]{1,0:T(8,128)(2,1)}, bf16[256,1024]{1,0:T(8,128)(2,1)}) custom-call(s32[1]{0:T(128)} %bitcast.key_ref, bf16[256,1024]{1,0:T(8,128)(2,1)S(1)} %get-tuple-element.51.k_ref, bf16[256,1024]{1,0:T(8,128)(2,1)S(1)} %get-tuple-element.52.v_ref, ...), custom_call_target="tpu_custom_call", output_to_operand_aliasing={{0}: (6, {}), {1}: (7, {})} | custom-call | flops 67108864 | bytes 3801092 | tf_op jit(solution)/shard_map/pallas_call | solution.py:42
  (12 shorter events, 0.2 us)
Async XLA Ops:
  2.0 1.5 %collective-permute-start = (bf16[4,128,128]{2,1,0:T(8,128)(2,1)S(1)}, bf16[4,128,128]{2,1,0:T(8,128)(2,1)S(1)}, u32[]{:S(2)}, u32[]{:S(2)}) collective-permute-start(bf16[4,128,128]{2,1,0:T(8,128)(2,1)S(1)} %get-tuple-element.49), channel_id=1, source_target_pairs={{0,1},{1,0},{2,3},{3,2},{4,5},{5,4},{6,7},{7,6},{8,9},{9,8},{10,11... | collective-permute-start | bytes 393224 | tf_op jit(solution)/shard_map/ppermute | solution.py:152
  2.9 13.2 %copy-start = (bf16[256,1024]{1,0:T(8,128)(2,1)S(1)}, bf16[256,1024]{1,0:T(8,128)(2,1)}, u32[]{:S(2)}) copy-start(bf16[256,1024]{1,0:T(8,128)(2,1)} %q_ref.9) | copy-start | bytes 1572868
  3.6 4.3 %collective-permute-start.1 = (bf16[128,128]{1,0:T(8,128)(2,1)S(1)}, bf16[128,128]{1,0:T(8,128)(2,1)S(1)}, u32[]{:S(2)}, u32[]{:S(2)}) collective-permute-start(bf16[128,128]{1,0:T(8,128)(2,1)S(1)} %get-tuple-element.113), channel_id=1, source_target_pairs={{0,3},{1,2},{2,1},{3,0},{4,7},{5,6},{6,5},{7,4},{8,11},{9,10},{10,... | collective-permute-start | bytes 98312 | tf_op jit(solution)/shard_map/ppermute | solution.py:152
  6.3 3.9 %collective-permute-start.2 = (bf16[128,128]{1,0:T(8,128)(2,1)S(1)}, bf16[128,128]{1,0:T(8,128)(2,1)S(1)}, u32[]{:S(2)}, u32[]{:S(2)}) collective-permute-start(bf16[128,128]{1,0:T(8,128)(2,1)S(1)} %get-tuple-element.115), channel_id=1, source_target_pairs={{0,4},{1,5},{2,6},{3,7},{4,0},{5,1},{6,2},{7,3},{8,12},{9,13},{10,... | collective-permute-start | bytes 98312 | tf_op jit(solution)/shard_map/ppermute | solution.py:152
  7.9 4.3 %collective-permute-start.3 = (bf16[128,128]{1,0:T(8,128)(2,1)S(1)}, bf16[128,128]{1,0:T(8,128)(2,1)S(1)}, u32[]{:S(2)}, u32[]{:S(2)}) collective-permute-start(bf16[128,128]{1,0:T(8,128)(2,1)S(1)} %get-tuple-element.114), channel_id=1, source_target_pairs={{0,7},{1,6},{2,5},{3,4},{4,3},{5,2},{6,1},{7,0},{8,15},{9,14},{10,... | collective-permute-start | bytes 98312 | tf_op jit(solution)/shard_map/ppermute | solution.py:152
  12.2 6.1 %collective-permute-start.4 = (bf16[128,128]{1,0:T(8,128)(2,1)S(1)}, bf16[128,128]{1,0:T(8,128)(2,1)S(1)}, u32[]{:S(2)}, u32[]{:S(2)}) collective-permute-start(bf16[128,128]{1,0:T(8,128)(2,1)S(1)} %fusion.21), channel_id=1, source_target_pairs={{0,25},{1,24},{2,27},{3,26},{4,29},{5,28},{6,31},{7,30},{8,17},{9,... | collective-permute-start | bytes 98312 | tf_op jit(solution)/shard_map/ppermute | solution.py:152
  15.6 3.9 %collective-permute-start.5 = (bf16[128,128]{1,0:T(8,128)(2,1)S(1)}, bf16[128,128]{1,0:T(8,128)(2,1)S(1)}, u32[]{:S(2)}, u32[]{:S(2)}) collective-permute-start(bf16[128,128]{1,0:T(8,128)(2,1)S(1)} %fusion.21), channel_id=1, source_target_pairs={{0,16},{1,17},{2,18},{3,19},{4,20},{5,21},{6,22},{7,23},{8,24},{9,... | collective-permute-start | bytes 98312 | tf_op jit(solution)/shard_map/ppermute | solution.py:152
  16.1 5.1 %collective-permute-start.6 = (bf16[128,128]{1,0:T(8,128)(2,1)S(1)}, bf16[128,128]{1,0:T(8,128)(2,1)S(1)}, u32[]{:S(2)}, u32[]{:S(2)}) collective-permute-start(bf16[128,128]{1,0:T(8,128)(2,1)S(1)} %fusion.21), channel_id=1, source_target_pairs={{0,9},{1,8},{2,11},{3,10},{4,13},{5,12},{6,15},{7,14},{8,1},{9,0},... | collective-permute-start | bytes 98312 | tf_op jit(solution)/shard_map/ppermute | solution.py:152
  21.3 4.0 %collective-permute-start.8 = (bf16[128,128]{1,0:T(8,128)(2,1)S(1)}, bf16[128,128]{1,0:T(8,128)(2,1)S(1)}, u32[]{:S(2)}, u32[]{:S(2)}) collective-permute-start(bf16[128,128]{1,0:T(8,128)(2,1)S(1)} %get-tuple-element.97), channel_id=1, source_target_pairs={{0,4},{1,5},{2,6},{3,7},{4,0},{5,1},{6,2},{7,3},{8,12},{9,13},{10,... | collective-permute-start | bytes 98312 | tf_op jit(solution)/shard_map/ppermute | solution.py:152
  21.4 3.9 %collective-permute-start.7 = (bf16[128,128]{1,0:T(8,128)(2,1)S(1)}, bf16[128,128]{1,0:T(8,128)(2,1)S(1)}, u32[]{:S(2)}, u32[]{:S(2)}) collective-permute-start(bf16[128,128]{1,0:T(8,128)(2,1)S(1)} %get-tuple-element.96), channel_id=1, source_target_pairs={{0,3},{1,2},{2,1},{3,0},{4,7},{5,6},{6,5},{7,4},{8,11},{9,10},{10,... | collective-permute-start | bytes 98312 | tf_op jit(solution)/shard_map/ppermute | solution.py:152
  21.6 5.2 %copy-start.1 = (bf16[256,1024]{1,0:T(8,128)(2,1)S(1)}, bf16[256,1024]{1,0:T(8,128)(2,1)}, u32[]{:S(2)}) copy-start(bf16[256,1024]{1,0:T(8,128)(2,1)} %g_ref.3) | copy-start | bytes 1572868
  21.6 4.7 %collective-permute-start.9 = (bf16[128,128]{1,0:T(8,128)(2,1)S(1)}, bf16[128,128]{1,0:T(8,128)(2,1)S(1)}, u32[]{:S(2)}, u32[]{:S(2)}) collective-permute-start(bf16[128,128]{1,0:T(8,128)(2,1)S(1)} %get-tuple-element.109), channel_id=1, source_target_pairs={{0,7},{1,6},{2,5},{3,4},{4,3},{5,2},{6,1},{7,0},{8,15},{9,14},{10,... | collective-permute-start | bytes 98312 | tf_op jit(solution)/shard_map/ppermute | solution.py:152
  26.4 1.4 %collective-permute-start.10 = (bf16[4,128,128]{2,1,0:T(8,128)(2,1)S(1)}, bf16[4,128,128]{2,1,0:T(8,128)(2,1)S(1)}, u32[]{:S(2)}, u32[]{:S(2)}) collective-permute-start(bf16[4,128,128]{2,1,0:T(8,128)(2,1)S(1)} %get-tuple-element.102), channel_id=1, source_target_pairs={{0,1},{1,0},{2,3},{3,2},{4,5},{5,4},{6,7},{7,6},{8,9},{9,8},{10,11... | collective-permute-start | bytes 393224 | tf_op jit(solution)/shard_map/ppermute | solution.py:152
  27.4 1.4 %collective-permute-start.11 = (bf16[4,128,128]{2,1,0:T(8,128)(2,1)S(1)}, bf16[4,128,128]{2,1,0:T(8,128)(2,1)S(1)}, u32[]{:S(2)}, u32[]{:S(2)}) collective-permute-start(bf16[4,128,128]{2,1,0:T(8,128)(2,1)S(1)} %get-tuple-element.61), channel_id=1, source_target_pairs={{0,1},{1,0},{2,3},{3,2},{4,5},{5,4},{6,7},{7,6},{8,9},{9,8},{10,11... | collective-permute-start | bytes 393224 | tf_op jit(solution)/shard_map/ppermute | solution.py:152
  28.9 5.0 %collective-permute-start.12 = (bf16[128,128]{1,0:T(8,128)(2,1)S(1)}, bf16[128,128]{1,0:T(8,128)(2,1)S(1)}, u32[]{:S(2)}, u32[]{:S(2)}) collective-permute-start(bf16[128,128]{1,0:T(8,128)(2,1)S(1)} %get-tuple-element.112), channel_id=1, source_target_pairs={{0,3},{1,2},{2,1},{3,0},{4,7},{5,6},{6,5},{7,4},{8,11},{9,10},{10,... | collective-permute-start | bytes 98312 | tf_op jit(solution)/shard_map/ppermute | solution.py:152
  30.1 3.9 %collective-permute-start.13 = (bf16[128,128]{1,0:T(8,128)(2,1)S(1)}, bf16[128,128]{1,0:T(8,128)(2,1)S(1)}, u32[]{:S(2)}, u32[]{:S(2)}) collective-permute-start(bf16[128,128]{1,0:T(8,128)(2,1)S(1)} %get-tuple-element.111), channel_id=1, source_target_pairs={{0,4},{1,5},{2,6},{3,7},{4,0},{5,1},{6,2},{7,3},{8,12},{9,13},{10,... | collective-permute-start | bytes 98312 | tf_op jit(solution)/shard_map/ppermute | solution.py:152
  32.0 4.3 %collective-permute-start.14 = (bf16[128,128]{1,0:T(8,128)(2,1)S(1)}, bf16[128,128]{1,0:T(8,128)(2,1)S(1)}, u32[]{:S(2)}, u32[]{:S(2)}) collective-permute-start(bf16[128,128]{1,0:T(8,128)(2,1)S(1)} %get-tuple-element.110), channel_id=1, source_target_pairs={{0,7},{1,6},{2,5},{3,4},{4,3},{5,2},{6,1},{7,0},{8,15},{9,14},{10,... | collective-permute-start | bytes 98312 | tf_op jit(solution)/shard_map/ppermute | solution.py:152
  36.4 5.8 %collective-permute-start.15 = (bf16[128,128]{1,0:T(8,128)(2,1)S(1)}, bf16[128,128]{1,0:T(8,128)(2,1)S(1)}, u32[]{:S(2)}, u32[]{:S(2)}) collective-permute-start(bf16[128,128]{1,0:T(8,128)(2,1)S(1)} %fusion.35), channel_id=1, source_target_pairs={{0,25},{1,24},{2,27},{3,26},{4,29},{5,28},{6,31},{7,30},{8,17},{9,... | collective-permute-start | bytes 98312 | tf_op jit(solution)/shard_map/ppermute | solution.py:152
  36.7 5.5 %collective-permute-start.16 = (bf16[128,128]{1,0:T(8,128)(2,1)S(1)}, bf16[128,128]{1,0:T(8,128)(2,1)S(1)}, u32[]{:S(2)}, u32[]{:S(2)}) collective-permute-start(bf16[128,128]{1,0:T(8,128)(2,1)S(1)} %fusion.35), channel_id=1, source_target_pairs={{0,16},{1,17},{2,18},{3,19},{4,20},{5,21},{6,22},{7,23},{8,24},{9,... | collective-permute-start | bytes 98312 | tf_op jit(solution)/shard_map/ppermute | solution.py:152
  38.1 5.5 %collective-permute-start.17 = (bf16[128,128]{1,0:T(8,128)(2,1)S(1)}, bf16[128,128]{1,0:T(8,128)(2,1)S(1)}, u32[]{:S(2)}, u32[]{:S(2)}) collective-permute-start(bf16[128,128]{1,0:T(8,128)(2,1)S(1)} %fusion.35), channel_id=1, source_target_pairs={{0,9},{1,8},{2,11},{3,10},{4,13},{5,12},{6,15},{7,14},{8,1},{9,0},... | collective-permute-start | bytes 98312 | tf_op jit(solution)/shard_map/ppermute | solution.py:152
  43.6 4.0 %collective-permute-start.19 = (bf16[128,128]{1,0:T(8,128)(2,1)S(1)}, bf16[128,128]{1,0:T(8,128)(2,1)S(1)}, u32[]{:S(2)}, u32[]{:S(2)}) collective-permute-start(bf16[128,128]{1,0:T(8,128)(2,1)S(1)} %get-tuple-element.95), channel_id=1, source_target_pairs={{0,4},{1,5},{2,6},{3,7},{4,0},{5,1},{6,2},{7,3},{8,12},{9,13},{10,... | collective-permute-start | bytes 98312 | tf_op jit(solution)/shard_map/ppermute | solution.py:152
  43.7 3.9 %collective-permute-start.18 = (bf16[128,128]{1,0:T(8,128)(2,1)S(1)}, bf16[128,128]{1,0:T(8,128)(2,1)S(1)}, u32[]{:S(2)}, u32[]{:S(2)}) collective-permute-start(bf16[128,128]{1,0:T(8,128)(2,1)S(1)} %get-tuple-element.94), channel_id=1, source_target_pairs={{0,3},{1,2},{2,1},{3,0},{4,7},{5,6},{6,5},{7,4},{8,11},{9,10},{10,... | collective-permute-start | bytes 98312 | tf_op jit(solution)/shard_map/ppermute | solution.py:152
  44.4 4.3 %collective-permute-start.20 = (bf16[128,128]{1,0:T(8,128)(2,1)S(1)}, bf16[128,128]{1,0:T(8,128)(2,1)S(1)}, u32[]{:S(2)}, u32[]{:S(2)}) collective-permute-start(bf16[128,128]{1,0:T(8,128)(2,1)S(1)} %get-tuple-element.107), channel_id=1, source_target_pairs={{0,7},{1,6},{2,5},{3,4},{4,3},{5,2},{6,1},{7,0},{8,15},{9,14},{10,... | collective-permute-start | bytes 98312 | tf_op jit(solution)/shard_map/ppermute | solution.py:152
  48.8 1.5 %collective-permute-start.21 = (bf16[4,128,128]{2,1,0:T(8,128)(2,1)S(1)}, bf16[4,128,128]{2,1,0:T(8,128)(2,1)S(1)}, u32[]{:S(2)}, u32[]{:S(2)}) collective-permute-start(bf16[4,128,128]{2,1,0:T(8,128)(2,1)S(1)} %get-tuple-element.99), channel_id=1, source_target_pairs={{0,1},{1,0},{2,3},{3,2},{4,5},{5,4},{6,7},{7,6},{8,9},{9,8},{10,11... | collective-permute-start | bytes 393224 | tf_op jit(solution)/shard_map/ppermute | solution.py:152

commit v4 on v3

v4 whole, which is shorter than its diff:
```python
import functools
import math

import jax
import jax.numpy as jnp
from jax import lax
from jax.experimental import pallas as pl
from jax.experimental.pallas import tpu as pltpu
from jax.sharding import PartitionSpec as P

HD = 128
COST = 3
AXES = ("grp", "shard")
F32 = jnp.float32
BF16 = jnp.bfloat16


def dot(a, b, a_dim, b_dim):
    return lax.dot_general(a, b, (((a_dim,), (b_dim,)), ((), ())), preferred_element_type=F32)


def columns(slot, key):
    return pl.ds(pl.multiple_of((slot ^ key) * HD, HD), HD)


def triangle(rows, keep_lower):
    at_row = lax.broadcasted_iota(jnp.int32, (rows, rows), 0)
    at_col = lax.broadcasted_iota(jnp.int32, (rows, rows), 1)
    return at_row >= at_col if keep_lower else at_row <= at_col


def call(kernel, outs, args, flops, out_hbm=0, in_hbm=(), scratch=(), aliases=None):
    smem = pl.BlockSpec(memory_space=pltpu.SMEM)
    vmem = pl.BlockSpec(memory_space=pltpu.VMEM)
    hbm = pl.BlockSpec(memory_space=pltpu.HBM)
    shapes = [
        jax.ShapeDtypeStruct(shape, dtype) if i < out_hbm else pltpu.VMEM(shape, dtype)
        for i, (shape, dtype) in enumerate(outs)
    ]
    size = sum(math.prod(a.shape) * jnp.dtype(a.dtype).itemsize for a in (*args, *shapes))
    args = [pltpu.with_memory_space_constraint(a, pltpu.HBM) if i in in_hbm else a for i, a in enumerate(args)]
    specs = [smem if a.dtype == jnp.int32 else hbm if i in in_hbm else vmem for i, a in enumerate(args)]
    return pl.pallas_call(
        kernel,
        out_shape=shapes,
        in_specs=specs,
        out_specs=[hbm if i < out_hbm else vmem for i in range(len(shapes))],
        scratch_shapes=list(scratch),
        input_output_aliases=aliases or {},
        compiler_params=pltpu.CompilerParams(vmem_limit_bytes=12 * 1024 * 1024),
        cost_estimate=pl.CostEstimate(flops=int(flops * COST), bytes_accessed=int(size * COST), transcendentals=0),
    )(*args)


def send_kernel(key_ref, k_hbm, v_hbm, out_ref, theirs_ref, mine_ref, sems):
    key = key_ref[0]
    half = out_ref.shape[0]
    copies = []
    for part, ref in enumerate((theirs_ref, mine_ref)):
        for at, hbm in enumerate((k_hbm, v_hbm)):
            copies.append(pltpu.make_async_copy(hbm.at[:, half_of(key, half, part)], ref.at[at], sems.at[part, at]))
            copies[-1].start()
    for copy in copies[:2]:
        copy.wait()
    for j in range(half):
        cols = half_columns(j, key, half)
        out_ref[j] = dot(theirs_ref[0, :, cols], theirs_ref[1, :, cols], 0, 0).astype(BF16)
    for copy in copies[2:]:
        copy.wait()


def own_kernel(key_ref, kv_ref, out_ref):
    key = key_ref[0]
    half = out_ref.shape[0]
    for j in range(half):
        cols = half_columns(j, key, half)
        out_ref[j] = dot(kv_ref[0, :, cols], kv_ref[1, :, cols], 0, 0).astype(BF16)


def fetch_kernel(half, key_ref, q_hbm, g_hbm, theirs_ref, mine_ref, sems):
    key = key_ref[0]
    copies = []
    for part, ref in enumerate((theirs_ref, mine_ref)):
        for at, hbm in enumerate((q_hbm, g_hbm)):
            copies.append(pltpu.make_async_copy(hbm.at[:, half_of(key, half, part)], ref.at[at], sems.at[part, at]))
            copies[-1].start()
    for copy in copies:
        copy.wait()


def half_of(key, half, mine):
    first = key & half
    if not mine:
        first = half ^ first
    return pl.ds(pl.multiple_of(first * HD, half * HD), half * HD)


def half_columns(slot, key, half):
    return pl.ds(pl.multiple_of(((slot ^ key) & (half - 1)) * HD, HD), HD)


def local_kernel(key_ref, kv_ref, qg_ref, their_kv_ref, their_qg_ref, mixed_ref):
    key = key_ref[0]
    half = mixed_ref.shape[1]
    low = triangle(mixed_ref.shape[2], True)
    for j in range(half):
        cols = half_columns(j, key, half)
        for at, (kv, qg) in enumerate(((kv_ref, qg_ref), (their_kv_ref, their_qg_ref))):
            scores = jnp.where(low, dot(qg[0, :, cols], kv[0, :, cols], 1, 1), 0.0).astype(BF16)
            mixed_ref[at, j] = dot(scores, kv[1, :, cols], 1, 0)


def norm_kernel(base, key_ref, qg_ref, their_qg_ref, mixed_ref, mine_ref, theirs_ref, att_ref, gm_ref, state_ref, pair_ref, their_state_ref):
    key = key_ref[0]
    half = mixed_ref.shape[1]
    for j in range(mine_ref.shape[0]):
        cols = half_columns(base + j, key, half)
        for at, (qg, e) in enumerate(((qg_ref, mine_ref), (their_qg_ref, theirs_ref))):
            q = qg[0, :, cols]
            mixed = mixed_ref[at, base + j] + dot(q, e[j], 1, 0)
            inv_rms = lax.rsqrt(jnp.mean(mixed * mixed, axis=-1, keepdims=True) + 1.0)
            normed = mixed * inv_rms
            g = qg[1, :, cols].astype(F32)
            gm = ((g - normed * jnp.mean(g * normed, axis=-1, keepdims=True)) * inv_rms).astype(BF16)
            state = dot(q, gm, 0, 0).astype(BF16)
            if at:
                pair_ref[0, j] = normed.astype(BF16)
                pair_ref[1, j] = gm
                their_state_ref[j] = state
            else:
                att_ref[j] = normed.astype(BF16)
                gm_ref[j] = gm
                state_ref[j] = state


def grads_kernel(base, pieces, key_ref, q_ref, k_ref, v_ref, *refs):
    att_refs, gm_refs, e_refs = (refs[i * pieces : (i + 1) * pieces] for i in range(3))
    att_hbm, gq_hbm, kl_ref, vl_ref, gq_buf, sems = refs[-6:]
    key = key_ref[0]
    rows = q_ref.shape[0]
    low = triangle(rows, True)
    high = triangle(rows, False)
    copies = []
    for j in range(gq_buf.shape[0]):
        piece, i = divmod(j, gq_buf.shape[0] // pieces)
        cols = columns(base + j, key)
        copies.append(pltpu.make_async_copy(att_refs[piece].at[i], att_hbm.at[:, cols], sems.at[0, j]))
        copies[-1].start()
        q = q_ref[:, cols]
        k = k_ref[:, cols]
        v = v_ref[:, cols]
        gm = gm_refs[piece][i]
        gs = jnp.where(low, dot(gm, v, 1, 1), 0.0).astype(BF16)
        gq_buf[j] = (dot(gs, k, 1, 0) + dot(gm, e_refs[piece][i], 1, 1)).astype(BF16)
        copies.append(pltpu.make_async_copy(gq_buf.at[j], gq_hbm.at[:, cols], sems.at[1, j]))
        copies[-1].start()
        gs_turned = jnp.where(high, dot(v, gm, 1, 1), 0.0).astype(BF16)
        kl_ref[j] = dot(gs_turned, q, 1, 0).astype(BF16)
        scores = jnp.where(high, dot(k, q, 1, 1), 0.0).astype(BF16)
        vl_ref[j] = dot(scores, gm, 1, 0).astype(BF16)
    for copy in copies:
        copy.wait()


def last_kernel(base, key_ref, k_ref, v_ref, kl_ref, vl_ref, l_ref, *refs):
    gk_hbm, gv_hbm, gk_buf, gv_buf, sems = refs[-5:]
    key = key_ref[0]
    copies = []
    for j in range(l_ref.shape[0]):
        cols = columns(base + j, key)
        later = l_ref[j]
        gk_buf[j] = (kl_ref[j] + dot(v_ref[:, cols], later, 1, 1)).astype(BF16)
        copies.append(pltpu.make_async_copy(gk_buf.at[j], gk_hbm.at[:, cols], sems.at[0, j]))
        copies[-1].start()
        gv_buf[j] = (vl_ref[j] + dot(k_ref[:, cols], later, 1, 0)).astype(BF16)
        copies.append(pltpu.make_async_copy(gv_buf.at[j], gv_hbm.at[:, cols], sems.at[1, j]))
        copies[-1].start()
    for copy in copies:
        copy.wait()


def swap(array, mask, count):
    return lax.ppermute(array, AXES, [(i, i ^ mask) for i in range(count)])


def exchange_levels(count):
    bits = count.bit_length() - 1
    levels = []
    bit = 3
    while bit < bits:
        first = (1 << bit) | 1
        if bit + 1 < bits:
            second = 1 << (bit + 1)
            levels.append(((3 << bit), (1 << bit) | 1, (2 << bit) | 1))
        else:
            levels.append((first,))
        bit += 2
    return levels


ORDER = (1, 3, 2)
SCATTER = (3, 4, 7)


GROUPS = ((0, 1), (2, 3))


def slot_key(place, count):
    bits = count.bit_length() - 1
    half = (place ^ (place >> 1)) & 1
    for bit in range(3, bits, 2):
        half = half ^ ((place >> (bit + 0)) ^ (place >> (bit + 1))) & 1
    return (half << 2) | ((place >> 1) & 3)


def beside(arrays, work, tie):
    if work is None:
        return arrays, None
    done = work(tie)
    return lax.optimization_barrier((arrays, done))


def pick(condition, array):
    return jnp.where(condition, array, 0.0)


def tie_to(array, other):
    return lax.optimization_barrier((array, other))[0]


def merge(own, from_core, place, count, backward, works):
    def before(a, b):
        return (a > b) if backward else (a < b)

    chip = place >> 1
    total = [a.astype(F32) + b.astype(F32) for a, b in zip(own, from_core)]
    rounded = [t.astype(BF16) for t in total]
    arrived = {j: swap(rounded[j], SCATTER[j - 1], count) for j in ORDER}
    arrived = [arrived[j] for j in (1, 2, 3)]
    if works[0] is not None and works[0][1]:
        first = works[0][0](arrived[ORDER[0] - 1])
    else:
        arrived, first = beside(arrived, works[0] and works[0][0], rounded[ORDER[0]])
    parts = [total[0], *(a.astype(F32) for a in arrived)]
    cluster = parts[0] + parts[1] + parts[2] + parts[3]
    entering = jnp.zeros_like(cluster)
    second = None
    for at, masks in enumerate(exchange_levels(count)):
        rounded = cluster.astype(BF16)
        arrived = [swap(rounded, mask, count) for mask in masks]
        if at == 0:
            arrived, second = beside(arrived, works[1], rounded)
        for mask, array in zip(masks, arrived):
            array = array.astype(F32)
            entering = entering + pick(before(chip ^ (mask >> 1), chip), array)
            cluster = cluster + array
    low = chip & 3
    sums = []
    for j in range(4):
        value = entering
        for i in range(4):
            if i != j:
                value = value + pick(before(low ^ i, low ^ j), parts[i])
        sums.append(value)
    rounded = [value.astype(BF16) for value in sums]
    arrived = {j: swap(rounded[j], SCATTER[j - 1], count) for j in ORDER}
    arrived = [arrived[j] for j in (1, 2, 3)]
    arrived, third = beside(arrived, works[2], rounded[1])
    return [sums[0], *arrived], (first, second, third)


def share(slots, entering, own, from_core, place, backward):
    first = (place & 1) == (1 if backward else 0)
    entering = jnp.stack([e.astype(F32) for e in entering])
    mine = entering + pick(~first, jnp.stack([from_core[j].astype(F32) for j in slots]))
    theirs = entering + pick(first, jnp.stack([own[j].astype(F32) for j in slots]))
    return mine.astype(BF16), theirs.astype(BF16)


def body(query_rows, key_rows, value_rows, grad_out):
    rows, width = query_rows.shape
    heads = width // HD
    half = heads // 2
    count = lax.axis_size("grp") * lax.axis_size("shard")
    place = lax.axis_index(AXES)
    key = slot_key(place, count).astype(jnp.int32).reshape(1)
    work = rows * width * HD
    scores = rows * width * rows
    block = (half, rows, HD)
    flat = (rows, width)
    dma = pltpu.SemaphoreType.DMA((2, half))
    buffer = pltpu.VMEM(block, BF16)

    def tied(tie):
        return lax.optimization_barrier((key, tie))[0]

    wide = (2, rows, width // 2)
    pairs = pltpu.SemaphoreType.DMA((2, 2))
    send, kv_send, kv_own = call(
        send_kernel, [((half, HD, HD), BF16), (wide, BF16), (wide, BF16)], (key, key_rows, value_rows),
        work, in_hbm=(1, 2), scratch=(pairs,),
    )
    (own,) = call(own_kernel, [((half, HD, HD), BF16)], (tied(send), kv_own), work)
    from_core = swap(send, 1, count)
    brought = []

    def fetch(tie):
        brought.extend(call(
            functools.partial(fetch_kernel, half), [(wide, BF16), (wide, BF16)],
            (tied(tie), query_rows, grad_out), 0, in_hbm=(1, 2), scratch=(pairs,),
        ))
        return brought

    def local(tie):
        qg_send, qg_own = brought
        kv = swap(tie_to(kv_send, tie), 1, count)
        qg = swap(tie_to(qg_send, tie), 1, count)
        brought.append(qg)
        return call(
            local_kernel, [((2, half, rows, HD), F32)], (tied(tie), kv_own, qg_own, kv, qg), 4 * scores,
        )[0]

    entering, ((_, qg_own), mixed, _) = merge(own, from_core, place, count, False, ((fetch, False), local, None))

    qg = brought[2]

    def norm(slot, mine, theirs):
        n = mine.shape[0]
        rows_of = (n, rows, HD)
        states = (n, HD, HD)
        return call(
            functools.partial(norm_kernel, slot),
            [(rows_of, BF16), (rows_of, BF16), (states, BF16), ((2, *rows_of), BF16), (states, BF16)],
            (key, qg_own, qg, mixed, mine, theirs), n * work // 2,
        )

    inner, outer = [], []
    own_back, core_back = [], []
    for at, group in enumerate(GROUPS):
        come = [entering[j] for j in group]
        if at:
            come = tie_to(come, state)
        mine, theirs = share(group, come, own, from_core, place, False)
        att, gm, state, pair, their_state = norm(group[0], mine, theirs)
        inner.append((att, gm, mine))
        outer.append((pair, theirs))
        own_back += [state[i] for i in range(len(group))]
        core_back += [their_state[i] for i in range(len(group))]

    late_q, late_k, late_v = tie_to((query_rows, key_rows, value_rows), mixed)

    def grads(base, key, parts, outs):
        att, gm, e = ([p[i] for p in parts] for i in range(3))
        n = 4 + 3 * len(parts)
        return call(
            functools.partial(grads_kernel, base, len(parts)),
            [(flat, BF16), (flat, BF16), (block, BF16), (block, BF16)],
            (key, late_q, late_k, late_v, *att, *gm, *e, *outs),
            4 * scores + work, out_hbm=2, in_hbm=(n, n + 1), scratch=(buffer, dma),
            aliases={n: 0, n + 1: 1} if outs else None,
        )

    made = []

    def grads_first(tie):
        made.append(grads(0, tied(tie), inner, ()))
        return made[0]

    def grads_second(tie):
        parts = []
        for pair, theirs in outer:
            pair = swap(pair, 1, count)
            parts.append((pair[0], pair[1], swap(theirs, 1, count)))
        return grads(half, tied(tie), parts, made[0][:2])

    entering, ((_, _, kl_mine, vl_mine), (attended, grad_query, kl_other, vl_other), _) = merge(
        own_back, core_back, place, count, True, ((grads_first, False), grads_second, None)
    )
    l_mine, theirs = share(range(half), entering, own_back, core_back, place, True)
    l_other = swap(theirs, 1, count)

    def last(base, key, kl, vl, later, outs):
        n = 6
        return call(
            functools.partial(last_kernel, base),
            [(flat, BF16), (flat, BF16)],
            (key, late_k, late_v, kl, vl, later, *outs),
            2 * work, out_hbm=2, in_hbm=(n, n + 1), scratch=(buffer, buffer, dma),
            aliases={n: 0, n + 1: 1} if outs else None,
        )

    outs = last(0, key, kl_mine, vl_mine, l_mine, ())
    grad_key, grad_value = last(half, key, kl_other, vl_other, l_other, outs)
    return attended, grad_query, grad_key, grad_value


def solution(mesh):
    spec = P(AXES, None)
    return jax.shard_map(
        body, mesh=mesh, in_specs=(spec,) * 4, out_specs=(spec,) * 4, check_vma=False
    )
```

time: 51.6 us -> 49.3 us (0.955)
  waiting for transfers between devices: 16.7 us -> 12 us
  Pallas kernels: 9.81 us -> 11.1 us
  starting transfers between devices: 23.5 us -> 24.6 us
    ppermute x22 -> x26, waiting for transfers between devices: 16.7 us -> 12 us  [swap(): return lax.ppermute(array, AXES, [(i, i ^ mask) for i in range(count)])]
    pallas_call x9 -> x10, Pallas kernels: 9.81 us -> 11.1 us  [call(): pl.pallas_call(kernel, out_shape=shapes, in_specs=specs, out_specs=[hbm i...]
    ppermute x22 -> x26, starting transfers between devices: 23.5 us -> 24.6 us  [swap(): return lax.ppermute(array, AXES, [(i, i ^ mask) for i in range(count)])]
  transfers between devices with their start and end apart: 22 -> 26, of which waited for: 15 -> 11; matrix products, arithmetic and copies ran while one was open for 0% -> 1% of each run, Pallas kernels for 14% -> 18%
where the time goes in v4:
time: 49.3 us; the launch traced here: 49.2 us
  starting transfers between devices  24.6 us (50%)
  waiting for transfers between devices  12 us (24%)
  Pallas kernels  11.1 us (23%)
  between operations  0.86 us (2%)
  other arithmetic  0.57 us (1%)
    ppermute x26, starting transfers between devices, swap(): return lax.ppermute(array, AXES, [(i, i ^ mask) for i in range(count)])  24.6 us
    ppermute x26, waiting for transfers between devices, swap(): return lax.ppermute(array, AXES, [(i, i ^ mask) for i in range(count)])  12 us
    pallas_call x10, Pallas kernels, call(): pl.pallas_call(kernel, out_shape=shapes, in_specs=specs, out_specs=[hbm i...  11.1 us
  transfers between devices with their start and end apart: 26, of which 11 were waited for; matrix products, arithmetic and copies ran while one was open for 1% of the time, Pallas kernels for 18%

profile of v4, /device:TPU:0, one launch (start us, length us, event | category | flops | bytes accessed | tf_op | source)
XLA Modules:
  0.0 49.2 jit_solution(13937721514039467603)
XLA Ops:
  0.6 1.3 %shard_map.75 = (bf16[4,128,128]{2,1,0:T(8,128)(2,1)S(1)}, bf16[2,256,512]{2,1,0:T(8,128)(2,1)S(1)}, bf16[2,256,512]{2,1,0:T(8,128)(2,1)S(1)}) custom-call(s32[1]{0:T(128)} %bitcast.key_ref, bf16[256,1024]{1,0:T(8,128)(2,1)} %k_ref.3, bf16[256,1024]{1,0:T(8,128)(2,1)} %v_ref.3), custom_call_target="tpu_custom_call" | custom-call | flops 100663296 | bytes 6684684 | tf_op jit(solution)/shard_map/pallas_call | solution.py:43
  2.0 0.5 %collective-permute-start = (bf16[4,128,128]{2,1,0:T(8,128)(2,1)S(1)}, bf16[4,128,128]{2,1,0:T(8,128)(2,1)S(1)}, u32[]{:S(2)}, u32[]{:S(2)}) collective-permute-start(bf16[4,128,128]{2,1,0:T(8,128)(2,1)S(1)} %get-tuple-element.63), channel_id=1, source_target_pairs={{0,1},{1,0},{2,3},{3,2},{4,5},{5,4},{6,7},{7,6},{8,9},{9,8},{10,11... | collective-permute-start | bytes 393224 | tf_op jit(solution)/shard_map/ppermute | solution.py:183
  2.5 0.3 shard_map.76
  2.8 0.7 %collective-permute-done = bf16[4,128,128]{2,1,0:T(8,128)(2,1)S(1)} collective-permute-done((bf16[4,128,128]{2,1,0:T(8,128)(2,1)S(1)}, bf16[4,128,128]{2,1,0:T(8,128)(2,1)S(1)}, u32[]{:S(2)}, u32[]{:S(2)}) %collective-permute-start) | collective-permute-done | bytes 131104 | tf_op jit(solution)/shard_map/ppermute | solution.py:183
  3.5 2.7 %collective-permute-start.1 = (bf16[128,128]{1,0:T(8,128)(2,1)S(1)}, bf16[128,128]{1,0:T(8,128)(2,1)S(1)}, u32[]{:S(2)}, u32[]{:S(2)}) collective-permute-start(bf16[128,128]{1,0:T(8,128)(2,1)S(1)} %get-tuple-element.134), channel_id=1, source_target_pairs={{0,3},{1,2},{2,1},{3,0},{4,7},{5,6},{6,5},{7,4},{8,11},{9,10},{10,... | collective-permute-start | bytes 98312 | tf_op jit(solution)/shard_map/ppermute | solution.py:183
  6.2 1.6 %collective-permute-start.2 = (bf16[128,128]{1,0:T(8,128)(2,1)S(1)}, bf16[128,128]{1,0:T(8,128)(2,1)S(1)}, u32[]{:S(2)}, u32[]{:S(2)}) collective-permute-start(bf16[128,128]{1,0:T(8,128)(2,1)S(1)} %get-tuple-element.133), channel_id=1, source_target_pairs={{0,4},{1,5},{2,6},{3,7},{4,0},{5,1},{6,2},{7,3},{8,12},{9,13},{10,... | collective-permute-start | bytes 98312 | tf_op jit(solution)/shard_map/ppermute | solution.py:183
  7.8 0.0 collective-permute-start.3
  7.8 1.2 %shard_map.77 = (bf16[2,256,512]{2,1,0:T(8,128)(2,1)S(1)}, bf16[2,256,512]{2,1,0:T(8,128)(2,1)S(1)}) custom-call(s32[1]{0:T(128)} %bitcast.key_ref, bf16[256,1024]{1,0:T(8,128)(2,1)} %q_ref.1, bf16[256,1024]{1,0:T(8,128)(2,1)} %g_hbm.1), custom_call_target="tpu_custom_call" | custom-call | bytes 6291468 | tf_op jit(solution)/shard_map/pallas_call | solution.py:43
  9.0 0.0 collective-permute-done.1
  9.0 1.1 %collective-permute-done.2 = bf16[128,128]{1,0:T(8,128)(2,1)S(1)} collective-permute-done((bf16[128,128]{1,0:T(8,128)(2,1)S(1)}, bf16[128,128]{1,0:T(8,128)(2,1)S(1)}, u32[]{:S(2)}, u32[]{:S(2)}) %collective-permute-start.2) | collective-permute-done | bytes 32800 | tf_op jit(solution)/shard_map/ppermute | solution.py:183
  10.1 2.0 %collective-permute-done.3 = bf16[128,128]{1,0:T(8,128)(2,1)S(1)} collective-permute-done((bf16[128,128]{1,0:T(8,128)(2,1)S(1)}, bf16[128,128]{1,0:T(8,128)(2,1)S(1)}, u32[]{:S(2)}, u32[]{:S(2)}) %collective-permute-start.3) | collective-permute-done | bytes 32800 | tf_op jit(solution)/shard_map/ppermute | solution.py:183
  12.2 0.2 collective-permute-start.8
  12.3 0.4 collective-permute-start.4
  12.7 3.5 %collective-permute-start.5 = (bf16[128,128]{1,0:T(8,128)(2,1)S(1)}, bf16[128,128]{1,0:T(8,128)(2,1)S(1)}, u32[]{:S(2)}, u32[]{:S(2)}) collective-permute-start(bf16[128,128]{1,0:T(8,128)(2,1)S(1)} %fusion.15), channel_id=1, source_target_pairs={{0,24},{1,25},{2,26},{3,27},{4,28},{5,29},{6,30},{7,31},{8,16},{9,... | collective-permute-start | bytes 98312 | tf_op jit(solution)/shard_map/ppermute | solution.py:183
  16.3 0.0 collective-permute-start.6
  16.3 0.6 %collective-permute-start.7 = (bf16[128,128]{1,0:T(8,128)(2,1)S(1)}, bf16[128,128]{1,0:T(8,128)(2,1)S(1)}, u32[]{:S(2)}, u32[]{:S(2)}) collective-permute-start(bf16[128,128]{1,0:T(8,128)(2,1)S(1)} %fusion.15), channel_id=1, source_target_pairs={{0,17},{1,16},{2,19},{3,18},{4,21},{5,20},{6,23},{7,22},{8,25},{9,... | collective-permute-start | bytes 98312 | tf_op jit(solution)/shard_map/ppermute | solution.py:183
  16.8 0.0 collective-permute-done.8.their_kv_ref
  16.9 0.0 collective-permute-done.4.their_qg_ref
  16.9 0.9 %shard_map.78.mixed_ref = f32[2,4,256,128]{3,2,1,0:T(8,128)S(1)} custom-call(s32[1]{0:T(128)} %bitcast.key_ref, bf16[2,256,512]{2,1,0:T(8,128)(2,1)S(1)} %get-tuple-element.65.kv_ref, bf16[2,256,512]{2,1,0:T(8,128)(2,1)S(1)} %get-tuple-element.69.qg_ref, bf16[2,256,512]{2,1,0:T(8,128)(2,1)S(1)} %collective-permute-done.8.their_kv_ref, ...), custom_call_target="tpu_custom_call" | custom-call | flops 805306368 | bytes 9437196 | tf_op jit(solution)/shard_map/pallas_call | solution.py:43
  17.8 0.9 %collective-permute-done.5 = bf16[128,128]{1,0:T(8,128)(2,1)S(1)} collective-permute-done((bf16[128,128]{1,0:T(8,128)(2,1)S(1)}, bf16[128,128]{1,0:T(8,128)(2,1)S(1)}, u32[]{:S(2)}, u32[]{:S(2)}) %collective-permute-start.5) | collective-permute-done | bytes 32800 | tf_op jit(solution)/shard_map/ppermute | solution.py:183
  18.7 2.8 %collective-permute-done.6 = bf16[128,128]{1,0:T(8,128)(2,1)S(1)} collective-permute-done((bf16[128,128]{1,0:T(8,128)(2,1)S(1)}, bf16[128,128]{1,0:T(8,128)(2,1)S(1)}, u32[]{:S(2)}, u32[]{:S(2)}) %collective-permute-start.6) | collective-permute-done | bytes 32800 | tf_op jit(solution)/shard_map/ppermute | solution.py:183
  21.5 0.0 collective-permute-done.7
  21.5 0.1 fusion.11
  21.5 0.4 collective-permute-start.9
  21.9 0.1 fusion.8
  22.0 0.1 collective-permute-start.11
  22.1 2.6 %collective-permute-start.12 = (bf16[128,128]{1,0:T(8,128)(2,1)S(1)}, bf16[128,128]{1,0:T(8,128)(2,1)S(1)}, u32[]{:S(2)}, u32[]{:S(2)}) collective-permute-start(bf16[128,128]{1,0:T(8,128)(2,1)S(1)} %get-tuple-element.122), channel_id=1, source_target_pairs={{0,7},{1,6},{2,5},{3,4},{4,3},{5,2},{6,1},{7,0},{8,15},{9,14},{10,... | collective-permute-start | bytes 98312 | tf_op jit(solution)/shard_map/ppermute | solution.py:183
  24.7 0.3 collective-permute-done.9
  25.1 0.7 %shard_map.79 = (bf16[2,256,128]{2,1,0:T(8,128)(2,1)S(1)}, bf16[2,256,128]{2,1,0:T(8,128)(2,1)S(1)}, bf16[2,128,128]{2,1,0:T(8,128)(2,1)S(1)}, bf16[2,2,256,128]...) custom-call(s32[1]{0:T(128)} %bitcast.key_ref, bf16[2,256,512]{2,1,0:T(8,128)(2,1)S(1)} %get-tuple-element.69.qg_ref, ...), custom_call_target="tpu_custom_call" | custom-call | flops 100663296 | bytes 8650764 | tf_op jit(solution)/shard_map/pallas_call | solution.py:43
  25.8 0.4 collective-permute-start.10
  26.2 0.0 collective-permute-done.11
  26.2 0.6 %collective-permute-done.12 = bf16[128,128]{1,0:T(8,128)(2,1)S(1)} collective-permute-done((bf16[128,128]{1,0:T(8,128)(2,1)S(1)}, bf16[128,128]{1,0:T(8,128)(2,1)S(1)}, u32[]{:S(2)}, u32[]{:S(2)}) %collective-permute-start.12) | collective-permute-done | bytes 32800 | tf_op jit(solution)/shard_map/ppermute | solution.py:183
  26.9 0.4 collective-permute-start.21
  27.3 0.7 %shard_map.80 = (bf16[2,256,128]{2,1,0:T(8,128)(2,1)S(1)}, bf16[2,256,128]{2,1,0:T(8,128)(2,1)S(1)}, bf16[2,128,128]{2,1,0:T(8,128)(2,1)S(1)}, bf16[2,2,256,128]...) custom-call(s32[1]{0:T(128)} %bitcast.key_ref, bf16[2,256,512]{2,1,0:T(8,128)(2,1)S(1)} %get-tuple-element.69.qg_ref, ...), custom_call_target="tpu_custom_call" | custom-call | flops 100663296 | bytes 8650764 | tf_op jit(solution)/shard_map/pallas_call | solution.py:43
  28.0 1.4 %collective-permute-start.13 = (bf16[128,128]{1,0:T(8,128)(2,1)S(1)}, bf16[128,128]{1,0:T(8,128)(2,1)S(1)}, u32[]{:S(2)}, u32[]{:S(2)}) collective-permute-start(bf16[128,128]{1,0:T(8,128)(2,1)S(1)} %get-tuple-element.140), channel_id=1, source_target_pairs={{0,4},{1,5},{2,6},{3,7},{4,0},{5,1},{6,2},{7,3},{8,12},{9,13},{10,... | collective-permute-start | bytes 98312 | tf_op jit(solution)/shard_map/ppermute | solution.py:183
  29.5 0.9 %collective-permute-start.14 = (bf16[128,128]{1,0:T(8,128)(2,1)S(1)}, bf16[128,128]{1,0:T(8,128)(2,1)S(1)}, u32[]{:S(2)}, u32[]{:S(2)}) collective-permute-start(bf16[128,128]{1,0:T(8,128)(2,1)S(1)} %get-tuple-element.139), channel_id=1, source_target_pairs={{0,7},{1,6},{2,5},{3,4},{4,3},{5,2},{6,1},{7,0},{8,15},{9,14},{10,... | collective-permute-start | bytes 98312 | tf_op jit(solution)/shard_map/ppermute | solution.py:183
  30.3 0.4 collective-permute-start.19
  30.8 1.9 %shard_map.81 = (bf16[256,1024]{1,0:T(8,128)(2,1)}, bf16[256,1024]{1,0:T(8,128)(2,1)}, bf16[4,256,128]{2,1,0:T(8,128)(2,1)S(1)}, bf16[4,256,128]{2,1,0:T(8,128)(2,1)S(1)}) custom-call(s32[1]{0:T(128)} %bitcast.key_ref, bf16[256,1024]{1,0:T(8,128)(2,1)S(1)} %copy-done.2, bf16[256,1024]{1,0:T(8,128)(2,1)S(1)} %copy-done, bf16[256,1024]{1,0:T(8,128)(2,1)S(1)} %copy-done.1, ...), custom_call_target="tpu_custom_call" | custom-call | flops 905969664 | bytes 11403276 | tf_op jit(solution)/shard_map/pallas_call | solution.py:43
  32.6 0.0 collective-permute-done.13
  32.7 0.2 collective-permute-start.20
  32.8 1.0 %collective-permute-done.14 = bf16[128,128]{1,0:T(8,128)(2,1)S(1)} collective-permute-done((bf16[128,128]{1,0:T(8,128)(2,1)S(1)}, bf16[128,128]{1,0:T(8,128)(2,1)S(1)}, u32[]{:S(2)}, u32[]{:S(2)}) %collective-permute-start.14) | collective-permute-done | bytes 32800 | tf_op jit(solution)/shard_map/ppermute | solution.py:183
  33.8 0.1 collective-permute-start.18
  33.9 0.0 collective-permute-done.10
  34.0 1.5 %collective-permute-start.15 = (bf16[128,128]{1,0:T(8,128)(2,1)S(1)}, bf16[128,128]{1,0:T(8,128)(2,1)S(1)}, u32[]{:S(2)}, u32[]{:S(2)}) collective-permute-start(bf16[128,128]{1,0:T(8,128)(2,1)S(1)} %fusion.29), channel_id=1, source_target_pairs={{0,24},{1,25},{2,26},{3,27},{4,28},{5,29},{6,30},{7,31},{8,16},{9,... | collective-permute-start | bytes 98312 | tf_op jit(solution)/shard_map/ppermute | solution.py:183
  35.5 0.0 collective-permute-done.19
  35.5 1.1 %collective-permute-start.16 = (bf16[128,128]{1,0:T(8,128)(2,1)S(1)}, bf16[128,128]{1,0:T(8,128)(2,1)S(1)}, u32[]{:S(2)}, u32[]{:S(2)}) collective-permute-start(bf16[128,128]{1,0:T(8,128)(2,1)S(1)} %fusion.29), channel_id=1, source_target_pairs={{0,9},{1,8},{2,11},{3,10},{4,13},{5,12},{6,15},{7,14},{8,1},{9,0},... | collective-permute-start | bytes 98312 | tf_op jit(solution)/shard_map/ppermute | solution.py:183
  36.6 0.0 collective-permute-done.18
  36.6 1.6 %collective-permute-start.17 = (bf16[128,128]{1,0:T(8,128)(2,1)S(1)}, bf16[128,128]{1,0:T(8,128)(2,1)S(1)}, u32[]{:S(2)}, u32[]{:S(2)}) collective-permute-start(bf16[128,128]{1,0:T(8,128)(2,1)S(1)} %fusion.29), channel_id=1, source_target_pairs={{0,17},{1,16},{2,19},{3,18},{4,21},{5,20},{6,23},{7,22},{8,25},{9,... | collective-permute-start | bytes 98312 | tf_op jit(solution)/shard_map/ppermute | solution.py:183
  38.3 0.0 collective-permute-done.21.refs_5_
  38.3 0.0 collective-permute-done.20.refs_4_
  38.3 1.9 %shard_map.82 = (bf16[256,1024]{1,0:T(8,128)(2,1)}, bf16[256,1024]{1,0:T(8,128)(2,1)}, bf16[4,256,128]{2,1,0:T(8,128)(2,1)S(1)}, bf16[4,256,128]{2,1,0:T(8,128)(2,1)S(1)}) custom-call(s32[1]{0:T(128)} %bitcast.key_ref, bf16[256,1024]{1,0:T(8,128)(2,1)S(1)} %copy-done.2, ...), custom_call_target="tpu_custom_call", output_to_operand_aliasing={{0}: (10, {}), {1}: (11, {})} | custom-call | flops 905969664 | bytes 14549004 | tf_op jit(solution)/shard_map/pallas_call | solution.py:43
  40.2 0.8 %collective-permute-done.15 = bf16[128,128]{1,0:T(8,128)(2,1)S(1)} collective-permute-done((bf16[128,128]{1,0:T(8,128)(2,1)S(1)}, bf16[128,128]{1,0:T(8,128)(2,1)S(1)}, u32[]{:S(2)}, u32[]{:S(2)}) %collective-permute-start.15) | collective-permute-done | bytes 32800 | tf_op jit(solution)/shard_map/ppermute | solution.py:183
  41.0 0.1 fusion.28
  41.1 0.3 collective-permute-start.23
  41.4 0.6 %collective-permute-start.22 = (bf16[128,128]{1,0:T(8,128)(2,1)S(1)}, bf16[128,128]{1,0:T(8,128)(2,1)S(1)}, u32[]{:S(2)}, u32[]{:S(2)}) collective-permute-start(bf16[128,128]{1,0:T(8,128)(2,1)S(1)} %get-tuple-element.126), channel_id=1, source_target_pairs={{0,3},{1,2},{2,1},{3,0},{4,7},{5,6},{6,5},{7,4},{8,11},{9,10},{10,... | collective-permute-start | bytes 98312 | tf_op jit(solution)/shard_map/ppermute | solution.py:183
  41.9 0.1 fusion.19
  42.0 2.5 %collective-permute-start.24 = (bf16[128,128]{1,0:T(8,128)(2,1)S(1)}, bf16[128,128]{1,0:T(8,128)(2,1)S(1)}, u32[]{:S(2)}, u32[]{:S(2)}) collective-permute-start(bf16[128,128]{1,0:T(8,128)(2,1)S(1)} %get-tuple-element.136), channel_id=1, source_target_pairs={{0,7},{1,6},{2,5},{3,4},{4,3},{5,2},{6,1},{7,0},{8,15},{9,14},{10,... | collective-permute-start | bytes 98312 | tf_op jit(solution)/shard_map/ppermute | solution.py:183
  44.5 0.6 %collective-permute-done.23 = bf16[128,128]{1,0:T(8,128)(2,1)S(1)} collective-permute-done((bf16[128,128]{1,0:T(8,128)(2,1)S(1)}, bf16[128,128]{1,0:T(8,128)(2,1)S(1)}, u32[]{:S(2)}, u32[]{:S(2)}) %collective-permute-start.23) | collective-permute-done | bytes 32800 | tf_op jit(solution)/shard_map/ppermute | solution.py:183
  45.1 0.0 collective-permute-done.22
  45.1 1.2 %collective-permute-done.24 = bf16[128,128]{1,0:T(8,128)(2,1)S(1)} collective-permute-done((bf16[128,128]{1,0:T(8,128)(2,1)S(1)}, bf16[128,128]{1,0:T(8,128)(2,1)S(1)}, u32[]{:S(2)}, u32[]{:S(2)}) %collective-permute-start.24) | collective-permute-done | bytes 32800 | tf_op jit(solution)/shard_map/ppermute | solution.py:183
  46.3 0.1 add_convert_fusion
  46.4 0.7 %collective-permute-start.25 = (bf16[4,128,128]{2,1,0:T(8,128)(2,1)S(1)}, bf16[4,128,128]{2,1,0:T(8,128)(2,1)S(1)}, u32[]{:S(2)}, u32[]{:S(2)}) collective-permute-start(bf16[4,128,128]{2,1,0:T(8,128)(2,1)S(1)} %get-tuple-element.125), channel_id=1, source_target_pairs={{0,1},{1,0},{2,3},{3,2},{4,5},{5,4},{6,7},{7,6},{8,9},{9,8},{10,11... | collective-permute-start | bytes 393224 | tf_op jit(solution)/shard_map/ppermute | solution.py:183
  47.1 1.0 %shard_map.83 = (bf16[256,1024]{1,0:T(8,128)(2,1)}, bf16[256,1024]{1,0:T(8,128)(2,1)}) custom-call(s32[1]{0:T(128)} %bitcast.key_ref, bf16[256,1024]{1,0:T(8,128)(2,1)S(1)} %copy-done, bf16[256,1024]{1,0:T(8,128)(2,1)S(1)} %copy-done.1, bf16[4,256,128]{2,1,0:T(8,128)(2,1)S(1)} %get-tuple-element.116.kl_ref, ...), custom_call_target="tpu_custom_call" | custom-call | flops 201326592 | bytes 8257548 | tf_op jit(solution)/shard_map/pallas_call | solution.py:43
  48.1 1.0 %shard_map.84 = (bf16[256,1024]{1,0:T(8,128)(2,1)}, bf16[256,1024]{1,0:T(8,128)(2,1)}) custom-call(s32[1]{0:T(128)} %bitcast.key_ref, bf16[256,1024]{1,0:T(8,128)(2,1)S(1)} %copy-done, bf16[256,1024]{1,0:T(8,128)(2,1)S(1)} %copy-done.1, bf16[4,256,128]{2,1,0:T(8,128)(2,1)S(1)} %get-tuple-element.111.kl_ref, ...), custom_call_target="tpu_custom_call", output_to_operand_aliasing={{0}: (6, {}), {1}: (7, {})} | custom-call | flops 201326592 | bytes 11403276 | tf_op jit(solution)/shard_map/pallas_call | solution.py:43
  (22 shorter events, 0.3 us)
Async XLA Ops:
  2.0 1.5 %collective-permute-start = (bf16[4,128,128]{2,1,0:T(8,128)(2,1)S(1)}, bf16[4,128,128]{2,1,0:T(8,128)(2,1)S(1)}, u32[]{:S(2)}, u32[]{:S(2)}) collective-permute-start(bf16[4,128,128]{2,1,0:T(8,128)(2,1)S(1)} %get-tuple-element.63), channel_id=1, source_target_pairs={{0,1},{1,0},{2,3},{3,2},{4,5},{5,4},{6,7},{7,6},{8,9},{9,8},{10,11... | collective-permute-start | bytes 393224 | tf_op jit(solution)/shard_map/ppermute | solution.py:183
  3.5 5.5 %collective-permute-start.1 = (bf16[128,128]{1,0:T(8,128)(2,1)S(1)}, bf16[128,128]{1,0:T(8,128)(2,1)S(1)}, u32[]{:S(2)}, u32[]{:S(2)}) collective-permute-start(bf16[128,128]{1,0:T(8,128)(2,1)S(1)} %get-tuple-element.134), channel_id=1, source_target_pairs={{0,3},{1,2},{2,1},{3,0},{4,7},{5,6},{6,5},{7,4},{8,11},{9,10},{10,... | collective-permute-start | bytes 98312 | tf_op jit(solution)/shard_map/ppermute | solution.py:183
  6.2 3.9 %collective-permute-start.2 = (bf16[128,128]{1,0:T(8,128)(2,1)S(1)}, bf16[128,128]{1,0:T(8,128)(2,1)S(1)}, u32[]{:S(2)}, u32[]{:S(2)}) collective-permute-start(bf16[128,128]{1,0:T(8,128)(2,1)S(1)} %get-tuple-element.133), channel_id=1, source_target_pairs={{0,4},{1,5},{2,6},{3,7},{4,0},{5,1},{6,2},{7,3},{8,12},{9,13},{10,... | collective-permute-start | bytes 98312 | tf_op jit(solution)/shard_map/ppermute | solution.py:183
  7.8 4.3 %collective-permute-start.3 = (bf16[128,128]{1,0:T(8,128)(2,1)S(1)}, bf16[128,128]{1,0:T(8,128)(2,1)S(1)}, u32[]{:S(2)}, u32[]{:S(2)}) collective-permute-start(bf16[128,128]{1,0:T(8,128)(2,1)S(1)} %get-tuple-element.132), channel_id=1, source_target_pairs={{0,7},{1,6},{2,5},{3,4},{4,3},{5,2},{6,1},{7,0},{8,15},{9,14},{10,... | collective-permute-start | bytes 98312 | tf_op jit(solution)/shard_map/ppermute | solution.py:183
  12.2 4.7 %collective-permute-start.8 = (bf16[2,256,512]{2,1,0:T(8,128)(2,1)S(1)}, bf16[2,256,512]{2,1,0:T(8,128)(2,1)S(1)}, u32[]{:S(2)}, u32[]{:S(2)}) collective-permute-start(bf16[2,256,512]{2,1,0:T(8,128)(2,1)S(1)} %get-tuple-element.76), channel_id=1, source_target_pairs={{0,1},{1,0},{2,3},{3,2},{4,5},{5,4},{6,7},{7,6},{8,9},{9,8},{10,11... | collective-permute-start | bytes 1572872 | tf_op jit(solution)/shard_map/ppermute | solution.py:183
  12.3 4.5 %collective-permute-start.4 = (bf16[2,256,512]{2,1,0:T(8,128)(2,1)S(1)}, bf16[2,256,512]{2,1,0:T(8,128)(2,1)S(1)}, u32[]{:S(2)}, u32[]{:S(2)}) collective-permute-start(bf16[2,256,512]{2,1,0:T(8,128)(2,1)S(1)} %get-tuple-element.73), channel_id=1, source_target_pairs={{0,1},{1,0},{2,3},{3,2},{4,5},{5,4},{6,7},{7,6},{8,9},{9,8},{10,11... | collective-permute-start | bytes 1572872 | tf_op jit(solution)/shard_map/ppermute | solution.py:183
  12.7 5.9 %collective-permute-start.5 = (bf16[128,128]{1,0:T(8,128)(2,1)S(1)}, bf16[128,128]{1,0:T(8,128)(2,1)S(1)}, u32[]{:S(2)}, u32[]{:S(2)}) collective-permute-start(bf16[128,128]{1,0:T(8,128)(2,1)S(1)} %fusion.15), channel_id=1, source_target_pairs={{0,24},{1,25},{2,26},{3,27},{4,28},{5,29},{6,30},{7,31},{8,16},{9,... | collective-permute-start | bytes 98312 | tf_op jit(solution)/shard_map/ppermute | solution.py:183
  16.3 5.2 %collective-permute-start.6 = (bf16[128,128]{1,0:T(8,128)(2,1)S(1)}, bf16[128,128]{1,0:T(8,128)(2,1)S(1)}, u32[]{:S(2)}, u32[]{:S(2)}) collective-permute-start(bf16[128,128]{1,0:T(8,128)(2,1)S(1)} %fusion.15), channel_id=1, source_target_pairs={{0,9},{1,8},{2,11},{3,10},{4,13},{5,12},{6,15},{7,14},{8,1},{9,0},... | collective-permute-start | bytes 98312 | tf_op jit(solution)/shard_map/ppermute | solution.py:183
  16.3 5.2 %collective-permute-start.7 = (bf16[128,128]{1,0:T(8,128)(2,1)S(1)}, bf16[128,128]{1,0:T(8,128)(2,1)S(1)}, u32[]{:S(2)}, u32[]{:S(2)}) collective-permute-start(bf16[128,128]{1,0:T(8,128)(2,1)S(1)} %fusion.15), channel_id=1, source_target_pairs={{0,17},{1,16},{2,19},{3,18},{4,21},{5,20},{6,23},{7,22},{8,25},{9,... | collective-permute-start | bytes 98312 | tf_op jit(solution)/shard_map/ppermute | solution.py:183
  21.5 3.5 %collective-permute-start.9 = (bf16[128,128]{1,0:T(8,128)(2,1)S(1)}, bf16[128,128]{1,0:T(8,128)(2,1)S(1)}, u32[]{:S(2)}, u32[]{:S(2)}) collective-permute-start(bf16[128,128]{1,0:T(8,128)(2,1)S(1)} %get-tuple-element.123), channel_id=1, source_target_pairs={{0,3},{1,2},{2,1},{3,0},{4,7},{5,6},{6,5},{7,4},{8,11},{9,10},{10,... | collective-permute-start | bytes 98312 | tf_op jit(solution)/shard_map/ppermute | solution.py:183
  22.0 4.2 %collective-permute-start.11 = (bf16[128,128]{1,0:T(8,128)(2,1)S(1)}, bf16[128,128]{1,0:T(8,128)(2,1)S(1)}, u32[]{:S(2)}, u32[]{:S(2)}) collective-permute-start(bf16[128,128]{1,0:T(8,128)(2,1)S(1)} %get-tuple-element.137), channel_id=1, source_target_pairs={{0,4},{1,5},{2,6},{3,7},{4,0},{5,1},{6,2},{7,3},{8,12},{9,13},{10,... | collective-permute-start | bytes 98312 | tf_op jit(solution)/shard_map/ppermute | solution.py:183
  22.1 4.8 %collective-permute-start.12 = (bf16[128,128]{1,0:T(8,128)(2,1)S(1)}, bf16[128,128]{1,0:T(8,128)(2,1)S(1)}, u32[]{:S(2)}, u32[]{:S(2)}) collective-permute-start(bf16[128,128]{1,0:T(8,128)(2,1)S(1)} %get-tuple-element.122), channel_id=1, source_target_pairs={{0,7},{1,6},{2,5},{3,4},{4,3},{5,2},{6,1},{7,0},{8,15},{9,14},{10,... | collective-permute-start | bytes 98312 | tf_op jit(solution)/shard_map/ppermute | solution.py:183
  25.8 8.1 %collective-permute-start.10 = (bf16[128,128]{1,0:T(8,128)(2,1)S(1)}, bf16[128,128]{1,0:T(8,128)(2,1)S(1)}, u32[]{:S(2)}, u32[]{:S(2)}) collective-permute-start(bf16[128,128]{1,0:T(8,128)(2,1)S(1)} %fusion.39), channel_id=1, source_target_pairs={{0,3},{1,2},{2,1},{3,0},{4,7},{5,6},{6,5},{7,4},{8,11},{9,10},{10,... | collective-permute-start | bytes 98312 | tf_op jit(solution)/shard_map/ppermute | solution.py:183
  26.9 11.4 %collective-permute-start.21 = (bf16[2,128,128]{2,1,0:T(8,128)(2,1)S(1)}, bf16[2,128,128]{2,1,0:T(8,128)(2,1)S(1)}, u32[]{:S(2)}, u32[]{:S(2)}) collective-permute-start(bf16[2,128,128]{2,1,0:T(8,128)(2,1)S(1)} %get-tuple-element.143.theirs_ref), channel_id=1, source_target_pairs={{0,1},{1,0},{2,3},{3,2},{4,5},{5,4},{6,7},{7,6},{8,9},{9,8},{10,11... | collective-permute-start | bytes 196616 | tf_op jit(solution)/shard_map/ppermute | solution.py:183
  27.3 3.5 %copy-start = (bf16[256,1024]{1,0:T(8,128)(2,1)S(1)}, bf16[256,1024]{1,0:T(8,128)(2,1)}, u32[]{:S(2)}) copy-start(bf16[256,1024]{1,0:T(8,128)(2,1)} %k_ref.3) | copy-start | bytes 1572868
  27.3 3.5 %copy-start.1 = (bf16[256,1024]{1,0:T(8,128)(2,1)S(1)}, bf16[256,1024]{1,0:T(8,128)(2,1)}, u32[]{:S(2)}) copy-start(bf16[256,1024]{1,0:T(8,128)(2,1)} %v_ref.3) | copy-start | bytes 1572868
  27.3 3.5 %copy-start.2 = (bf16[256,1024]{1,0:T(8,128)(2,1)S(1)}, bf16[256,1024]{1,0:T(8,128)(2,1)}, u32[]{:S(2)}) copy-start(bf16[256,1024]{1,0:T(8,128)(2,1)} %q_ref.1) | copy-start | bytes 1572868
  28.0 4.6 %collective-permute-start.13 = (bf16[128,128]{1,0:T(8,128)(2,1)S(1)}, bf16[128,128]{1,0:T(8,128)(2,1)S(1)}, u32[]{:S(2)}, u32[]{:S(2)}) collective-permute-start(bf16[128,128]{1,0:T(8,128)(2,1)S(1)} %get-tuple-element.140), channel_id=1, source_target_pairs={{0,4},{1,5},{2,6},{3,7},{4,0},{5,1},{6,2},{7,3},{8,12},{9,13},{10,... | collective-permute-start | bytes 98312 | tf_op jit(solution)/shard_map/ppermute | solution.py:183
  29.5 4.3 %collective-permute-start.14 = (bf16[128,128]{1,0:T(8,128)(2,1)S(1)}, bf16[128,128]{1,0:T(8,128)(2,1)S(1)}, u32[]{:S(2)}, u32[]{:S(2)}) collective-permute-start(bf16[128,128]{1,0:T(8,128)(2,1)S(1)} %get-tuple-element.139), channel_id=1, source_target_pairs={{0,7},{1,6},{2,5},{3,4},{4,3},{5,2},{6,1},{7,0},{8,15},{9,14},{10,... | collective-permute-start | bytes 98312 | tf_op jit(solution)/shard_map/ppermute | solution.py:183
  30.3 5.1 %collective-permute-start.19 = (bf16[2,2,256,128]{3,2,1,0:T(8,128)(2,1)S(1)}, bf16[2,2,256,128]{3,2,1,0:T(8,128)(2,1)S(1)}, u32[]{:S(2)}, u32[]{:S(2)}) collective-permute-start(bf16[2,2,256,128]{3,2,1,0:T(8,128)(2,1)S(1)} %get-tuple-element.104), channel_id=1, source_target_pairs={{0,1},{1,0},{2,3},{3,2},{4,5},{5,4},{6,7},{7,6},{8,9},{9,8},{10,11... | collective-permute-start | bytes 786440 | tf_op jit(solution)/shard_map/ppermute | solution.py:183
  32.7 5.7 %collective-permute-start.20 = (bf16[2,128,128]{2,1,0:T(8,128)(2,1)S(1)}, bf16[2,128,128]{2,1,0:T(8,128)(2,1)S(1)}, u32[]{:S(2)}, u32[]{:S(2)}) collective-permute-start(bf16[2,128,128]{2,1,0:T(8,128)(2,1)S(1)} %get-tuple-element.141.theirs_ref), channel_id=1, source_target_pairs={{0,1},{1,0},{2,3},{3,2},{4,5},{5,4},{6,7},{7,6},{8,9},{9,8},{10,11... | collective-permute-start | bytes 196616 | tf_op jit(solution)/shard_map/ppermute | solution.py:183
  33.8 2.8 %collective-permute-start.18 = (bf16[2,2,256,128]{3,2,1,0:T(8,128)(2,1)S(1)}, bf16[2,2,256,128]{3,2,1,0:T(8,128)(2,1)S(1)}, u32[]{:S(2)}, u32[]{:S(2)}) collective-permute-start(bf16[2,2,256,128]{3,2,1,0:T(8,128)(2,1)S(1)} %get-tuple-element.103), channel_id=1, source_target_pairs={{0,1},{1,0},{2,3},{3,2},{4,5},{5,4},{6,7},{7,6},{8,9},{9,8},{10,11... | collective-permute-start | bytes 786440 | tf_op jit(solution)/shard_map/ppermute | solution.py:183
  34.0 7.1 %collective-permute-start.15 = (bf16[128,128]{1,0:T(8,128)(2,1)S(1)}, bf16[128,128]{1,0:T(8,128)(2,1)S(1)}, u32[]{:S(2)}, u32[]{:S(2)}) collective-permute-start(bf16[128,128]{1,0:T(8,128)(2,1)S(1)} %fusion.29), channel_id=1, source_target_pairs={{0,24},{1,25},{2,26},{3,27},{4,28},{5,29},{6,30},{7,31},{8,16},{9,... | collective-permute-start | bytes 98312 | tf_op jit(solution)/shard_map/ppermute | solution.py:183
  35.5 5.5 %collective-permute-start.16 = (bf16[128,128]{1,0:T(8,128)(2,1)S(1)}, bf16[128,128]{1,0:T(8,128)(2,1)S(1)}, u32[]{:S(2)}, u32[]{:S(2)}) collective-permute-start(bf16[128,128]{1,0:T(8,128)(2,1)S(1)} %fusion.29), channel_id=1, source_target_pairs={{0,9},{1,8},{2,11},{3,10},{4,13},{5,12},{6,15},{7,14},{8,1},{9,0},... | collective-permute-start | bytes 98312 | tf_op jit(solution)/shard_map/ppermute | solution.py:183
  36.6 4.4 %collective-permute-start.17 = (bf16[128,128]{1,0:T(8,128)(2,1)S(1)}, bf16[128,128]{1,0:T(8,128)(2,1)S(1)}, u32[]{:S(2)}, u32[]{:S(2)}) collective-permute-start(bf16[128,128]{1,0:T(8,128)(2,1)S(1)} %fusion.29), channel_id=1, source_target_pairs={{0,17},{1,16},{2,19},{3,18},{4,21},{5,20},{6,23},{7,22},{8,25},{9,... | collective-permute-start | bytes 98312 | tf_op jit(solution)/shard_map/ppermute | solution.py:183
  41.1 4.0 %collective-permute-start.23 = (bf16[128,128]{1,0:T(8,128)(2,1)S(1)}, bf16[128,128]{1,0:T(8,128)(2,1)S(1)}, u32[]{:S(2)}, u32[]{:S(2)}) collective-permute-start(bf16[128,128]{1,0:T(8,128)(2,1)S(1)} %get-tuple-element.127), channel_id=1, source_target_pairs={{0,4},{1,5},{2,6},{3,7},{4,0},{5,1},{6,2},{7,3},{8,12},{9,13},{10,... | collective-permute-start | bytes 98312 | tf_op jit(solution)/shard_map/ppermute | solution.py:183
  41.4 3.7 %collective-permute-start.22 = (bf16[128,128]{1,0:T(8,128)(2,1)S(1)}, bf16[128,128]{1,0:T(8,128)(2,1)S(1)}, u32[]{:S(2)}, u32[]{:S(2)}) collective-permute-start(bf16[128,128]{1,0:T(8,128)(2,1)S(1)} %get-tuple-element.126), channel_id=1, source_target_pairs={{0,3},{1,2},{2,1},{3,0},{4,7},{5,6},{6,5},{7,4},{8,11},{9,10},{10,... | collective-permute-start | bytes 98312 | tf_op jit(solution)/shard_map/ppermute | solution.py:183
  42.0 4.3 %collective-permute-start.24 = (bf16[128,128]{1,0:T(8,128)(2,1)S(1)}, bf16[128,128]{1,0:T(8,128)(2,1)S(1)}, u32[]{:S(2)}, u32[]{:S(2)}) collective-permute-start(bf16[128,128]{1,0:T(8,128)(2,1)S(1)} %get-tuple-element.136), channel_id=1, source_target_pairs={{0,7},{1,6},{2,5},{3,4},{4,3},{5,2},{6,1},{7,0},{8,15},{9,14},{10,... | collective-permute-start | bytes 98312 | tf_op jit(solution)/shard_map/ppermute | solution.py:183
  46.4 1.7 %collective-permute-start.25 = (bf16[4,128,128]{2,1,0:T(8,128)(2,1)S(1)}, bf16[4,128,128]{2,1,0:T(8,128)(2,1)S(1)}, u32[]{:S(2)}, u32[]{:S(2)}) collective-permute-start(bf16[4,128,128]{2,1,0:T(8,128)(2,1)S(1)} %get-tuple-element.125), channel_id=1, source_target_pairs={{0,1},{1,0},{2,3},{3,2},{4,5},{5,4},{6,7},{7,6},{8,9},{9,8},{10,11... | collective-permute-start | bytes 393224 | tf_op jit(solution)/shard_map/ppermute | solution.py:183

commit v5 on v4

--- a/solution.py
+++ b/solution.py
@@ -1,4 +1,5 @@
 import functools
+import itertools
 import math
 
 import jax
@@ -110,9 +111,9 @@
             mixed_ref[at, j] = dot(scores, kv[1, :, cols], 1, 0)
 
 
-def norm_kernel(base, key_ref, qg_ref, their_qg_ref, mixed_ref, mine_ref, theirs_ref, att_ref, gm_ref, state_ref, pair_ref, their_state_ref):
-    key = key_ref[0]
-    half = mixed_ref.shape[1]
+def norm_kernel(base, key_ref, qg_ref, their_qg_ref, mixed_ref, mine_ref, theirs_ref, att_ref, gm_ref, state_ref, pack_ref, their_state_ref):
+    key = key_ref[0]
+    half, rows = mixed_ref.shape[1:3]
     for j in range(mine_ref.shape[0]):
         cols = half_columns(base + j, key, half)
         for at, (qg, e) in enumerate(((qg_ref, mine_ref), (their_qg_ref, theirs_ref))):
@@ -124,8 +125,9 @@
             gm = ((g - normed * jnp.mean(g * normed, axis=-1, keepdims=True)) * inv_rms).astype(BF16)
             state = dot(q, gm, 0, 0).astype(BF16)
             if at:
-                pair_ref[0, j] = normed.astype(BF16)
-                pair_ref[1, j] = gm
+                pack_ref[j, :rows] = normed.astype(BF16)
+                pack_ref[j, rows : 2 * rows] = gm
+                pack_ref[j, 2 * rows :] = e[j]
                 their_state_ref[j] = state
             else:
                 att_ref[j] = normed.astype(BF16)
@@ -133,25 +135,31 @@
                 state_ref[j] = state
 
 
-def grads_kernel(base, pieces, key_ref, q_ref, k_ref, v_ref, *refs):
-    att_refs, gm_refs, e_refs = (refs[i * pieces : (i + 1) * pieces] for i in range(3))
+def grads_kernel(base, per_group, key_ref, q_ref, k_ref, v_ref, *refs):
     att_hbm, gq_hbm, kl_ref, vl_ref, gq_buf, sems = refs[-6:]
     key = key_ref[0]
     rows = q_ref.shape[0]
     low = triangle(rows, True)
     high = triangle(rows, False)
+    slots = []
+    for at in range(0, per_group * len(GROUPS), per_group):
+        group = refs[at : at + per_group]
+        for i in range(group[0].shape[0]):
+            if per_group == 1:
+                slots.append([group[0].at[i, pl.ds(start, n)] for start, n in ((0, rows), (rows, rows), (2 * rows, HD))])
+            else:
+                slots.append([ref.at[i] for ref in group])
     copies = []
-    for j in range(gq_buf.shape[0]):
-        piece, i = divmod(j, gq_buf.shape[0] // pieces)
+    for j, (att, gm_ref, e_ref) in enumerate(slots):
         cols = columns(base + j, key)
-        copies.append(pltpu.make_async_copy(att_refs[piece].at[i], att_hbm.at[:, cols], sems.at[0, j]))
+        copies.append(pltpu.make_async_copy(att, att_hbm.at[:, cols], sems.at[0, j]))
         copies[-1].start()
         q = q_ref[:, cols]
         k = k_ref[:, cols]
         v = v_ref[:, cols]
-        gm = gm_refs[piece][i]
+        gm = gm_ref[...]
         gs = jnp.where(low, dot(gm, v, 1, 1), 0.0).astype(BF16)
-        gq_buf[j] = (dot(gs, k, 1, 0) + dot(gm, e_refs[piece][i], 1, 1)).astype(BF16)
+        gq_buf[j] = (dot(gs, k, 1, 0) + dot(gm, e_ref[...], 1, 1)).astype(BF16)
         copies.append(pltpu.make_async_copy(gq_buf.at[j], gq_hbm.at[:, cols], sems.at[1, j]))
         copies[-1].start()
         gs_turned = jnp.where(high, dot(v, gm, 1, 1), 0.0).astype(BF16)
@@ -198,7 +206,7 @@
     return levels
 
 
-ORDER = (1, 3, 2)
+ORDER = (1, 2, 3)
 SCATTER = (3, 4, 7)
 
 
@@ -330,7 +338,7 @@
         states = (n, HD, HD)
         return call(
             functools.partial(norm_kernel, slot),
-            [(rows_of, BF16), (rows_of, BF16), (states, BF16), ((2, *rows_of), BF16), (states, BF16)],
+            [(rows_of, BF16), (rows_of, BF16), (states, BF16), ((n, 2 * rows + HD, HD), BF16), (states, BF16)],
             (key, qg_own, qg, mixed, mine, theirs), n * work // 2,
         )
 
@@ -341,21 +349,21 @@
         if at:
             come = tie_to(come, state)
         mine, theirs = share(group, come, own, from_core, place, False)
-        att, gm, state, pair, their_state = norm(group[0], mine, theirs)
+        att, gm, state, pack, their_state = norm(group[0], mine, theirs)
         inner.append((att, gm, mine))
-        outer.append((pair, theirs))
+        outer.append(pack)
         own_back += [state[i] for i in range(len(group))]
         core_back += [their_state[i] for i in range(len(group))]
 
     late_q, late_k, late_v = tie_to((query_rows, key_rows, value_rows), mixed)
 
     def grads(base, key, parts, outs):
-        att, gm, e = ([p[i] for p in parts] for i in range(3))
-        n = 4 + 3 * len(parts)
+        per_group = len(parts[0])
+        n = 4 + per_group * len(parts)
         return call(
-            functools.partial(grads_kernel, base, len(parts)),
+            functools.partial(grads_kernel, base, per_group),
             [(flat, BF16), (flat, BF16), (block, BF16), (block, BF16)],
-            (key, late_q, late_k, late_v, *att, *gm, *e, *outs),
+            (key, late_q, late_k, late_v, *itertools.chain(*parts), *outs),
             4 * scores + work, out_hbm=2, in_hbm=(n, n + 1), scratch=(buffer, dma),
             aliases={n: 0, n + 1: 1} if outs else None,
         )
@@ -366,15 +374,17 @@
         made.append(grads(0, tied(tie), inner, ()))
         return made[0]
 
+    came = []
+
+    def trade(tie):
+        came.extend((swap(tie_to(pack, tie), 1, count),) for pack in outer)
+        return ()
+
     def grads_second(tie):
-        parts = []
-        for pair, theirs in outer:
-            pair = swap(pair, 1, count)
-            parts.append((pair[0], pair[1], swap(theirs, 1, count)))
-        return grads(half, tied(tie), parts, made[0][:2])
-
-    entering, ((_, _, kl_mine, vl_mine), (attended, grad_query, kl_other, vl_other), _) = merge(
-        own_back, core_back, place, count, True, ((grads_first, False), grads_second, None)
+        return grads(half, tied(tie), came, made[0][:2])
+
+    entering, ((_, _, kl_mine, vl_mine), _, (attended, grad_query, kl_other, vl_other)) = merge(
+        own_back, core_back, place, count, True, ((grads_first, False), trade, grads_second)
     )
     l_mine, theirs = share(range(half), entering, own_back, core_back, place, True)
     l_other = swap(theirs, 1, count)

time: 49.3 us -> 49 us (level)
  starting transfers between devices: 24.6 us -> 23.2 us
  waiting for transfers between devices: 12 us -> 13.1 us
    ppermute x26 -> x24, starting transfers between devices: 24.6 us -> 23.2 us  [swap(): return lax.ppermute(array, AXES, [(i, i ^ mask) for i in range(count)])]
    ppermute x26 -> x24, waiting for transfers between devices: 12 us -> 13.1 us  [swap(): return lax.ppermute(array, AXES, [(i, i ^ mask) for i in range(count)])]
  transfers between devices with their start and end apart: 26 -> 24, of which waited for: 11 -> 13; matrix products, arithmetic and copies ran while one was open for 1% -> 1% of each run, Pallas kernels for 18% -> 18%
where the time goes in v5:
time: 49 us; the launch traced here: 48.8 us
  starting transfers between devices  23.2 us (47%)
  waiting for transfers between devices  13.1 us (27%)
  Pallas kernels  11.1 us (23%)
  between operations  0.88 us (2%)
  other arithmetic  0.57 us (1%)
    ppermute x24, starting transfers between devices, swap(): return lax.ppermute(array, AXES, [(i, i ^ mask) for i in range(count)])  23.2 us
    ppermute x24, waiting for transfers between devices, swap(): return lax.ppermute(array, AXES, [(i, i ^ mask) for i in range(count)])  13.1 us
    pallas_call x10, Pallas kernels, call(): pl.pallas_call(kernel, out_shape=shapes, in_specs=specs, out_specs=[hbm i...  11.1 us
  transfers between devices with their start and end apart: 24, of which 13 were waited for; matrix products, arithmetic and copies ran while one was open for 1% of the time, Pallas kernels for 18%

profile of v5, /device:TPU:0, one launch (start us, length us, event | category | flops | bytes accessed | tf_op | source)
XLA Modules:
  0.0 48.8 jit_solution(2668763067913822429)
XLA Ops:
  0.6 1.3 %shard_map.75 = (bf16[4,128,128]{2,1,0:T(8,128)(2,1)S(1)}, bf16[2,256,512]{2,1,0:T(8,128)(2,1)S(1)}, bf16[2,256,512]{2,1,0:T(8,128)(2,1)S(1)}) custom-call(s32[1]{0:T(128)} %bitcast.key_ref, bf16[256,1024]{1,0:T(8,128)(2,1)} %k_ref.3, bf16[256,1024]{1,0:T(8,128)(2,1)} %v_ref.3), custom_call_target="tpu_custom_call" | custom-call | flops 100663296 | bytes 6684684 | tf_op jit(solution)/shard_map/pallas_call | solution.py:44
  2.0 0.5 %collective-permute-start = (bf16[4,128,128]{2,1,0:T(8,128)(2,1)S(1)}, bf16[4,128,128]{2,1,0:T(8,128)(2,1)S(1)}, u32[]{:S(2)}, u32[]{:S(2)}) collective-permute-start(bf16[4,128,128]{2,1,0:T(8,128)(2,1)S(1)} %get-tuple-element.68), channel_id=1, source_target_pairs={{0,1},{1,0},{2,3},{3,2},{4,5},{5,4},{6,7},{7,6},{8,9},{9,8},{10,11... | collective-permute-start | bytes 393224 | tf_op jit(solution)/shard_map/ppermute | solution.py:191
  2.5 0.3 shard_map.76
  2.8 0.7 %collective-permute-done = bf16[4,128,128]{2,1,0:T(8,128)(2,1)S(1)} collective-permute-done((bf16[4,128,128]{2,1,0:T(8,128)(2,1)S(1)}, bf16[4,128,128]{2,1,0:T(8,128)(2,1)S(1)}, u32[]{:S(2)}, u32[]{:S(2)}) %collective-permute-start) | collective-permute-done | bytes 131104 | tf_op jit(solution)/shard_map/ppermute | solution.py:191
  3.5 2.7 %collective-permute-start.1 = (bf16[128,128]{1,0:T(8,128)(2,1)S(1)}, bf16[128,128]{1,0:T(8,128)(2,1)S(1)}, u32[]{:S(2)}, u32[]{:S(2)}) collective-permute-start(bf16[128,128]{1,0:T(8,128)(2,1)S(1)} %get-tuple-element.140), channel_id=1, source_target_pairs={{0,3},{1,2},{2,1},{3,0},{4,7},{5,6},{6,5},{7,4},{8,11},{9,10},{10,... | collective-permute-start | bytes 98312 | tf_op jit(solution)/shard_map/ppermute | solution.py:191
  6.2 1.6 %collective-permute-start.2 = (bf16[128,128]{1,0:T(8,128)(2,1)S(1)}, bf16[128,128]{1,0:T(8,128)(2,1)S(1)}, u32[]{:S(2)}, u32[]{:S(2)}) collective-permute-start(bf16[128,128]{1,0:T(8,128)(2,1)S(1)} %get-tuple-element.139), channel_id=1, source_target_pairs={{0,4},{1,5},{2,6},{3,7},{4,0},{5,1},{6,2},{7,3},{8,12},{9,13},{10,... | collective-permute-start | bytes 98312 | tf_op jit(solution)/shard_map/ppermute | solution.py:191
  7.8 0.0 collective-permute-start.3
  7.8 1.2 %shard_map.77 = (bf16[2,256,512]{2,1,0:T(8,128)(2,1)S(1)}, bf16[2,256,512]{2,1,0:T(8,128)(2,1)S(1)}) custom-call(s32[1]{0:T(128)} %bitcast.key_ref, bf16[256,1024]{1,0:T(8,128)(2,1)} %q_ref.1, bf16[256,1024]{1,0:T(8,128)(2,1)} %g_hbm.1), custom_call_target="tpu_custom_call" | custom-call | bytes 6291468 | tf_op jit(solution)/shard_map/pallas_call | solution.py:44
  9.0 0.0 collective-permute-done.1
  9.0 1.1 %collective-permute-done.2 = bf16[128,128]{1,0:T(8,128)(2,1)S(1)} collective-permute-done((bf16[128,128]{1,0:T(8,128)(2,1)S(1)}, bf16[128,128]{1,0:T(8,128)(2,1)S(1)}, u32[]{:S(2)}, u32[]{:S(2)}) %collective-permute-start.2) | collective-permute-done | bytes 32800 | tf_op jit(solution)/shard_map/ppermute | solution.py:191
  10.1 2.0 %collective-permute-done.3 = bf16[128,128]{1,0:T(8,128)(2,1)S(1)} collective-permute-done((bf16[128,128]{1,0:T(8,128)(2,1)S(1)}, bf16[128,128]{1,0:T(8,128)(2,1)S(1)}, u32[]{:S(2)}, u32[]{:S(2)}) %collective-permute-start.3) | collective-permute-done | bytes 32800 | tf_op jit(solution)/shard_map/ppermute | solution.py:191
  12.2 0.2 collective-permute-start.4
  12.3 0.4 collective-permute-start.8
  12.7 3.5 %collective-permute-start.5 = (bf16[128,128]{1,0:T(8,128)(2,1)S(1)}, bf16[128,128]{1,0:T(8,128)(2,1)S(1)}, u32[]{:S(2)}, u32[]{:S(2)}) collective-permute-start(bf16[128,128]{1,0:T(8,128)(2,1)S(1)} %fusion.15), channel_id=1, source_target_pairs={{0,24},{1,25},{2,26},{3,27},{4,28},{5,29},{6,30},{7,31},{8,16},{9,... | collective-permute-start | bytes 98312 | tf_op jit(solution)/shard_map/ppermute | solution.py:191
  16.3 0.0 collective-permute-start.6
  16.3 0.6 %collective-permute-start.7 = (bf16[128,128]{1,0:T(8,128)(2,1)S(1)}, bf16[128,128]{1,0:T(8,128)(2,1)S(1)}, u32[]{:S(2)}, u32[]{:S(2)}) collective-permute-start(bf16[128,128]{1,0:T(8,128)(2,1)S(1)} %fusion.15), channel_id=1, source_target_pairs={{0,17},{1,16},{2,19},{3,18},{4,21},{5,20},{6,23},{7,22},{8,25},{9,... | collective-permute-start | bytes 98312 | tf_op jit(solution)/shard_map/ppermute | solution.py:191
  16.8 0.0 collective-permute-done.4.their_qg_ref
  16.9 0.0 collective-permute-done.8.their_kv_ref
  16.9 0.9 %shard_map.78.mixed_ref = f32[2,4,256,128]{3,2,1,0:T(8,128)S(1)} custom-call(s32[1]{0:T(128)} %bitcast.key_ref, bf16[2,256,512]{2,1,0:T(8,128)(2,1)S(1)} %get-tuple-element.70.kv_ref, bf16[2,256,512]{2,1,0:T(8,128)(2,1)S(1)} %get-tuple-element.74.qg_ref, bf16[2,256,512]{2,1,0:T(8,128)(2,1)S(1)} %collective-permute-done.8.their_kv_ref, ...), custom_call_target="tpu_custom_call" | custom-call | flops 805306368 | bytes 9437196 | tf_op jit(solution)/shard_map/pallas_call | solution.py:44
  17.8 0.9 %collective-permute-done.5 = bf16[128,128]{1,0:T(8,128)(2,1)S(1)} collective-permute-done((bf16[128,128]{1,0:T(8,128)(2,1)S(1)}, bf16[128,128]{1,0:T(8,128)(2,1)S(1)}, u32[]{:S(2)}, u32[]{:S(2)}) %collective-permute-start.5) | collective-permute-done | bytes 32800 | tf_op jit(solution)/shard_map/ppermute | solution.py:191
  18.7 2.8 %collective-permute-done.6 = bf16[128,128]{1,0:T(8,128)(2,1)S(1)} collective-permute-done((bf16[128,128]{1,0:T(8,128)(2,1)S(1)}, bf16[128,128]{1,0:T(8,128)(2,1)S(1)}, u32[]{:S(2)}, u32[]{:S(2)}) %collective-permute-start.6) | collective-permute-done | bytes 32800 | tf_op jit(solution)/shard_map/ppermute | solution.py:191
  21.5 0.0 collective-permute-done.7
  21.5 0.1 fusion.11
  21.5 0.4 collective-permute-start.9
  21.9 0.1 fusion.8
  22.0 0.1 collective-permute-start.11
  22.1 2.6 %collective-permute-start.12 = (bf16[128,128]{1,0:T(8,128)(2,1)S(1)}, bf16[128,128]{1,0:T(8,128)(2,1)S(1)}, u32[]{:S(2)}, u32[]{:S(2)}) collective-permute-start(bf16[128,128]{1,0:T(8,128)(2,1)S(1)} %get-tuple-element.132), channel_id=1, source_target_pairs={{0,7},{1,6},{2,5},{3,4},{4,3},{5,2},{6,1},{7,0},{8,15},{9,14},{10,... | collective-permute-start | bytes 98312 | tf_op jit(solution)/shard_map/ppermute | solution.py:191
  24.7 0.3 collective-permute-done.9
  25.1 0.7 %shard_map.79 = (bf16[2,256,128]{2,1,0:T(8,128)(2,1)S(1)}, bf16[2,256,128]{2,1,0:T(8,128)(2,1)S(1)}, bf16[2,128,128]{2,1,0:T(8,128)(2,1)S(1)}, bf16[2,640,128]{2,1,0:T(8,128)(2,1)S(1)}, bf16[2,128,128]{2,1,0:T(8,128)(2,1)S(1)}) custom-call(s32[1]{0:T(128)} %bitcast.key_ref, bf16[2,256,512]{2,1,0:T(8,128)(2,1)S(1)} %get-tuple-element.74.qg_ref, ...), custom_call_target="tpu_custom_call" | custom-call | flops 100663296 | bytes 8847372 | tf_op jit(solution)/shard_map/pallas_call | solution.py:44
  25.8 0.4 collective-permute-start.10
  26.2 0.0 collective-permute-done.11
  26.2 0.6 %collective-permute-done.12 = bf16[128,128]{1,0:T(8,128)(2,1)S(1)} collective-permute-done((bf16[128,128]{1,0:T(8,128)(2,1)S(1)}, bf16[128,128]{1,0:T(8,128)(2,1)S(1)}, u32[]{:S(2)}, u32[]{:S(2)}) %collective-permute-start.12) | collective-permute-done | bytes 32800 | tf_op jit(solution)/shard_map/ppermute | solution.py:191
  26.9 0.0 copy-start
  26.9 0.0 copy-start.1
  26.9 0.0 copy-start.2
  26.9 0.7 %shard_map.80 = (bf16[2,256,128]{2,1,0:T(8,128)(2,1)S(1)}, bf16[2,256,128]{2,1,0:T(8,128)(2,1)S(1)}, bf16[2,128,128]{2,1,0:T(8,128)(2,1)S(1)}, bf16[2,640,128]{2,1,0:T(8,128)(2,1)S(1)}, bf16[2,128,128]{2,1,0:T(8,128)(2,1)S(1)}) custom-call(s32[1]{0:T(128)} %bitcast.key_ref, bf16[2,256,512]{2,1,0:T(8,128)(2,1)S(1)} %get-tuple-element.74.qg_ref, ...), custom_call_target="tpu_custom_call" | custom-call | flops 100663296 | bytes 8847372 | tf_op jit(solution)/shard_map/pallas_call | solution.py:44
  27.7 1.6 %collective-permute-start.13 = (bf16[128,128]{1,0:T(8,128)(2,1)S(1)}, bf16[128,128]{1,0:T(8,128)(2,1)S(1)}, u32[]{:S(2)}, u32[]{:S(2)}) collective-permute-start(bf16[128,128]{1,0:T(8,128)(2,1)S(1)} %get-tuple-element.146), channel_id=1, source_target_pairs={{0,4},{1,5},{2,6},{3,7},{4,0},{5,1},{6,2},{7,3},{8,12},{9,13},{10,... | collective-permute-start | bytes 98312 | tf_op jit(solution)/shard_map/ppermute | solution.py:191
  29.3 0.7 %collective-permute-start.14 = (bf16[128,128]{1,0:T(8,128)(2,1)S(1)}, bf16[128,128]{1,0:T(8,128)(2,1)S(1)}, u32[]{:S(2)}, u32[]{:S(2)}) collective-permute-start(bf16[128,128]{1,0:T(8,128)(2,1)S(1)} %get-tuple-element.145), channel_id=1, source_target_pairs={{0,7},{1,6},{2,5},{3,4},{4,3},{5,2},{6,1},{7,0},{8,15},{9,14},{10,... | collective-permute-start | bytes 98312 | tf_op jit(solution)/shard_map/ppermute | solution.py:191
  30.0 1.9 %shard_map.81 = (bf16[256,1024]{1,0:T(8,128)(2,1)}, bf16[256,1024]{1,0:T(8,128)(2,1)}, bf16[4,256,128]{2,1,0:T(8,128)(2,1)S(1)}, bf16[4,256,128]{2,1,0:T(8,128)(2,1)S(1)}) custom-call(s32[1]{0:T(128)} %bitcast.key_ref, bf16[256,1024]{1,0:T(8,128)(2,1)S(1)} %copy-done.2, bf16[256,1024]{1,0:T(8,128)(2,1)S(1)} %copy-done, bf16[256,1024]{1,0:T(8,128)(2,1)S(1)} %copy-done.1, ...), custom_call_target="tpu_custom_call" | custom-call | flops 905969664 | bytes 11403276 | tf_op jit(solution)/shard_map/pallas_call | solution.py:44
  31.9 0.0 collective-permute-done.10
  31.9 0.0 copy-start.3
  31.9 1.9 %collective-permute-done.14 = bf16[128,128]{1,0:T(8,128)(2,1)S(1)} collective-permute-done((bf16[128,128]{1,0:T(8,128)(2,1)S(1)}, bf16[128,128]{1,0:T(8,128)(2,1)S(1)}, u32[]{:S(2)}, u32[]{:S(2)}) %collective-permute-start.14) | collective-permute-done | bytes 32800 | tf_op jit(solution)/shard_map/ppermute | solution.py:191
  33.9 1.5 %collective-permute-start.15 = (bf16[128,128]{1,0:T(8,128)(2,1)S(1)}, bf16[128,128]{1,0:T(8,128)(2,1)S(1)}, u32[]{:S(2)}, u32[]{:S(2)}) collective-permute-start(bf16[128,128]{1,0:T(8,128)(2,1)S(1)} %fusion.29), channel_id=1, source_target_pairs={{0,24},{1,25},{2,26},{3,27},{4,28},{5,29},{6,30},{7,31},{8,16},{9,... | collective-permute-start | bytes 98312 | tf_op jit(solution)/shard_map/ppermute | solution.py:191
  35.4 0.9 %collective-permute-start.16 = (bf16[128,128]{1,0:T(8,128)(2,1)S(1)}, bf16[128,128]{1,0:T(8,128)(2,1)S(1)}, u32[]{:S(2)}, u32[]{:S(2)}) collective-permute-start(bf16[128,128]{1,0:T(8,128)(2,1)S(1)} %fusion.29), channel_id=1, source_target_pairs={{0,9},{1,8},{2,11},{3,10},{4,13},{5,12},{6,15},{7,14},{8,1},{9,0},... | collective-permute-start | bytes 98312 | tf_op jit(solution)/shard_map/ppermute | solution.py:191
  36.2 1.8 %collective-permute-start.17 = (bf16[128,128]{1,0:T(8,128)(2,1)S(1)}, bf16[128,128]{1,0:T(8,128)(2,1)S(1)}, u32[]{:S(2)}, u32[]{:S(2)}) collective-permute-start(bf16[128,128]{1,0:T(8,128)(2,1)S(1)} %fusion.29), channel_id=1, source_target_pairs={{0,17},{1,16},{2,19},{3,18},{4,21},{5,20},{6,23},{7,22},{8,25},{9,... | collective-permute-start | bytes 98312 | tf_op jit(solution)/shard_map/ppermute | solution.py:191
  38.0 0.0 collective-permute-start.21
  38.0 0.5 %collective-permute-start.22 = (bf16[2,640,128]{2,1,0:T(8,128)(2,1)S(1)}, bf16[2,640,128]{2,1,0:T(8,128)(2,1)S(1)}, u32[]{:S(2)}, u32[]{:S(2)}) collective-permute-start(bf16[2,640,128]{2,1,0:T(8,128)(2,1)S(1)} %get-tuple-element.114), channel_id=1, source_target_pairs={{0,1},{1,0},{2,3},{3,2},{4,5},{5,4},{6,7},{7,6},{8,9},{9,8},{10,11... | collective-permute-start | bytes 983048 | tf_op jit(solution)/shard_map/ppermute | solution.py:191
  38.5 1.8 %collective-permute-done.15 = bf16[128,128]{1,0:T(8,128)(2,1)S(1)} collective-permute-done((bf16[128,128]{1,0:T(8,128)(2,1)S(1)}, bf16[128,128]{1,0:T(8,128)(2,1)S(1)}, u32[]{:S(2)}, u32[]{:S(2)}) %collective-permute-start.15) | collective-permute-done | bytes 32800 | tf_op jit(solution)/shard_map/ppermute | solution.py:191
  40.3 0.2 collective-permute-done.16
  40.5 0.1 fusion.21
  40.6 0.9 %collective-permute-start.18 = (bf16[128,128]{1,0:T(8,128)(2,1)S(1)}, bf16[128,128]{1,0:T(8,128)(2,1)S(1)}, u32[]{:S(2)}, u32[]{:S(2)}) collective-permute-start(bf16[128,128]{1,0:T(8,128)(2,1)S(1)} %get-tuple-element.137), channel_id=1, source_target_pairs={{0,3},{1,2},{2,1},{3,0},{4,7},{5,6},{6,5},{7,4},{8,11},{9,10},{10,... | collective-permute-start | bytes 98312 | tf_op jit(solution)/shard_map/ppermute | solution.py:191
  41.5 0.1 fusion.25
  41.6 0.1 collective-permute-start.19
  41.6 2.1 %collective-permute-start.20 = (bf16[128,128]{1,0:T(8,128)(2,1)S(1)}, bf16[128,128]{1,0:T(8,128)(2,1)S(1)}, u32[]{:S(2)}, u32[]{:S(2)}) collective-permute-start(bf16[128,128]{1,0:T(8,128)(2,1)S(1)} %get-tuple-element.136), channel_id=1, source_target_pairs={{0,7},{1,6},{2,5},{3,4},{4,3},{5,2},{6,1},{7,0},{8,15},{9,14},{10,... | collective-permute-start | bytes 98312 | tf_op jit(solution)/shard_map/ppermute | solution.py:191
  43.8 0.0 collective-permute-done.21.refs_0_
  43.8 0.0 collective-permute-done.22.refs_1_
  43.8 1.9 %shard_map.82 = (bf16[256,1024]{1,0:T(8,128)(2,1)}, bf16[256,1024]{1,0:T(8,128)(2,1)}, bf16[4,256,128]{2,1,0:T(8,128)(2,1)S(1)}, bf16[4,256,128]{2,1,0:T(8,128)(2,1)S(1)}) custom-call(s32[1]{0:T(128)} %bitcast.key_ref, bf16[256,1024]{1,0:T(8,128)(2,1)S(1)} %copy-done.2, bf16[256,1024]{1,0:T(8,128)(2,1)S(1)} %copy-done, ...), custom_call_target="tpu_custom_call", output_to_operand_aliasing={{0}: (6, {}), {1}: (7, {})} | custom-call | flops 905969664 | bytes 14549004 | tf_op jit(solution)/shard_map/pallas_call | solution.py:44
  45.6 0.2 collective-permute-done.19
  45.9 0.4 collective-permute-done.20
  46.3 0.1 add_convert_fusion
  46.4 0.2 collective-permute-start.23
  46.6 1.0 %shard_map.83 = (bf16[256,1024]{1,0:T(8,128)(2,1)}, bf16[256,1024]{1,0:T(8,128)(2,1)}) custom-call(s32[1]{0:T(128)} %bitcast.key_ref, bf16[256,1024]{1,0:T(8,128)(2,1)S(1)} %copy-done, bf16[256,1024]{1,0:T(8,128)(2,1)S(1)} %copy-done.1, bf16[4,256,128]{2,1,0:T(8,128)(2,1)S(1)} %get-tuple-element.126.kl_ref, ...), custom_call_target="tpu_custom_call" | custom-call | flops 201326592 | bytes 8257548 | tf_op jit(solution)/shard_map/pallas_call | solution.py:44
  47.6 0.2 collective-permute-done.23.l_ref
  47.8 1.0 %shard_map.84 = (bf16[256,1024]{1,0:T(8,128)(2,1)}, bf16[256,1024]{1,0:T(8,128)(2,1)}) custom-call(s32[1]{0:T(128)} %bitcast.key_ref, bf16[256,1024]{1,0:T(8,128)(2,1)S(1)} %copy-done, bf16[256,1024]{1,0:T(8,128)(2,1)S(1)} %copy-done.1, bf16[4,256,128]{2,1,0:T(8,128)(2,1)S(1)} %get-tuple-element.121.kl_ref, ...), custom_call_target="tpu_custom_call", output_to_operand_aliasing={{0}: (6, {}), {1}: (7, {})} | custom-call | flops 201326592 | bytes 11403276 | tf_op jit(solution)/shard_map/pallas_call | solution.py:44
  (19 shorter events, 0.2 us)
Async XLA Ops:
  2.0 1.5 %collective-permute-start = (bf16[4,128,128]{2,1,0:T(8,128)(2,1)S(1)}, bf16[4,128,128]{2,1,0:T(8,128)(2,1)S(1)}, u32[]{:S(2)}, u32[]{:S(2)}) collective-permute-start(bf16[4,128,128]{2,1,0:T(8,128)(2,1)S(1)} %get-tuple-element.68), channel_id=1, source_target_pairs={{0,1},{1,0},{2,3},{3,2},{4,5},{5,4},{6,7},{7,6},{8,9},{9,8},{10,11... | collective-permute-start | bytes 393224 | tf_op jit(solution)/shard_map/ppermute | solution.py:191
  3.5 5.5 %collective-permute-start.1 = (bf16[128,128]{1,0:T(8,128)(2,1)S(1)}, bf16[128,128]{1,0:T(8,128)(2,1)S(1)}, u32[]{:S(2)}, u32[]{:S(2)}) collective-permute-start(bf16[128,128]{1,0:T(8,128)(2,1)S(1)} %get-tuple-element.140), channel_id=1, source_target_pairs={{0,3},{1,2},{2,1},{3,0},{4,7},{5,6},{6,5},{7,4},{8,11},{9,10},{10,... | collective-permute-start | bytes 98312 | tf_op jit(solution)/shard_map/ppermute | solution.py:191
  6.2 3.9 %collective-permute-start.2 = (bf16[128,128]{1,0:T(8,128)(2,1)S(1)}, bf16[128,128]{1,0:T(8,128)(2,1)S(1)}, u32[]{:S(2)}, u32[]{:S(2)}) collective-permute-start(bf16[128,128]{1,0:T(8,128)(2,1)S(1)} %get-tuple-element.139), channel_id=1, source_target_pairs={{0,4},{1,5},{2,6},{3,7},{4,0},{5,1},{6,2},{7,3},{8,12},{9,13},{10,... | collective-permute-start | bytes 98312 | tf_op jit(solution)/shard_map/ppermute | solution.py:191
  7.8 4.3 %collective-permute-start.3 = (bf16[128,128]{1,0:T(8,128)(2,1)S(1)}, bf16[128,128]{1,0:T(8,128)(2,1)S(1)}, u32[]{:S(2)}, u32[]{:S(2)}) collective-permute-start(bf16[128,128]{1,0:T(8,128)(2,1)S(1)} %get-tuple-element.138), channel_id=1, source_target_pairs={{0,7},{1,6},{2,5},{3,4},{4,3},{5,2},{6,1},{7,0},{8,15},{9,14},{10,... | collective-permute-start | bytes 98312 | tf_op jit(solution)/shard_map/ppermute | solution.py:191
  12.2 4.7 %collective-permute-start.4 = (bf16[2,256,512]{2,1,0:T(8,128)(2,1)S(1)}, bf16[2,256,512]{2,1,0:T(8,128)(2,1)S(1)}, u32[]{:S(2)}, u32[]{:S(2)}) collective-permute-start(bf16[2,256,512]{2,1,0:T(8,128)(2,1)S(1)} %get-tuple-element.78), channel_id=1, source_target_pairs={{0,1},{1,0},{2,3},{3,2},{4,5},{5,4},{6,7},{7,6},{8,9},{9,8},{10,11... | collective-permute-start | bytes 1572872 | tf_op jit(solution)/shard_map/ppermute | solution.py:191
  12.3 4.5 %collective-permute-start.8 = (bf16[2,256,512]{2,1,0:T(8,128)(2,1)S(1)}, bf16[2,256,512]{2,1,0:T(8,128)(2,1)S(1)}, u32[]{:S(2)}, u32[]{:S(2)}) collective-permute-start(bf16[2,256,512]{2,1,0:T(8,128)(2,1)S(1)} %get-tuple-element.81), channel_id=1, source_target_pairs={{0,1},{1,0},{2,3},{3,2},{4,5},{5,4},{6,7},{7,6},{8,9},{9,8},{10,11... | collective-permute-start | bytes 1572872 | tf_op jit(solution)/shard_map/ppermute | solution.py:191
  12.7 5.9 %collective-permute-start.5 = (bf16[128,128]{1,0:T(8,128)(2,1)S(1)}, bf16[128,128]{1,0:T(8,128)(2,1)S(1)}, u32[]{:S(2)}, u32[]{:S(2)}) collective-permute-start(bf16[128,128]{1,0:T(8,128)(2,1)S(1)} %fusion.15), channel_id=1, source_target_pairs={{0,24},{1,25},{2,26},{3,27},{4,28},{5,29},{6,30},{7,31},{8,16},{9,... | collective-permute-start | bytes 98312 | tf_op jit(solution)/shard_map/ppermute | solution.py:191
  16.3 5.2 %collective-permute-start.6 = (bf16[128,128]{1,0:T(8,128)(2,1)S(1)}, bf16[128,128]{1,0:T(8,128)(2,1)S(1)}, u32[]{:S(2)}, u32[]{:S(2)}) collective-permute-start(bf16[128,128]{1,0:T(8,128)(2,1)S(1)} %fusion.15), channel_id=1, source_target_pairs={{0,9},{1,8},{2,11},{3,10},{4,13},{5,12},{6,15},{7,14},{8,1},{9,0},... | collective-permute-start | bytes 98312 | tf_op jit(solution)/shard_map/ppermute | solution.py:191
  16.3 5.2 %collective-permute-start.7 = (bf16[128,128]{1,0:T(8,128)(2,1)S(1)}, bf16[128,128]{1,0:T(8,128)(2,1)S(1)}, u32[]{:S(2)}, u32[]{:S(2)}) collective-permute-start(bf16[128,128]{1,0:T(8,128)(2,1)S(1)} %fusion.15), channel_id=1, source_target_pairs={{0,17},{1,16},{2,19},{3,18},{4,21},{5,20},{6,23},{7,22},{8,25},{9,... | collective-permute-start | bytes 98312 | tf_op jit(solution)/shard_map/ppermute | solution.py:191
  21.5 3.5 %collective-permute-start.9 = (bf16[128,128]{1,0:T(8,128)(2,1)S(1)}, bf16[128,128]{1,0:T(8,128)(2,1)S(1)}, u32[]{:S(2)}, u32[]{:S(2)}) collective-permute-start(bf16[128,128]{1,0:T(8,128)(2,1)S(1)} %get-tuple-element.133), channel_id=1, source_target_pairs={{0,3},{1,2},{2,1},{3,0},{4,7},{5,6},{6,5},{7,4},{8,11},{9,10},{10,... | collective-permute-start | bytes 98312 | tf_op jit(solution)/shard_map/ppermute | solution.py:191
  22.0 4.2 %collective-permute-start.11 = (bf16[128,128]{1,0:T(8,128)(2,1)S(1)}, bf16[128,128]{1,0:T(8,128)(2,1)S(1)}, u32[]{:S(2)}, u32[]{:S(2)}) collective-permute-start(bf16[128,128]{1,0:T(8,128)(2,1)S(1)} %get-tuple-element.143), channel_id=1, source_target_pairs={{0,4},{1,5},{2,6},{3,7},{4,0},{5,1},{6,2},{7,3},{8,12},{9,13},{10,... | collective-permute-start | bytes 98312 | tf_op jit(solution)/shard_map/ppermute | solution.py:191
  22.1 4.8 %collective-permute-start.12 = (bf16[128,128]{1,0:T(8,128)(2,1)S(1)}, bf16[128,128]{1,0:T(8,128)(2,1)S(1)}, u32[]{:S(2)}, u32[]{:S(2)}) collective-permute-start(bf16[128,128]{1,0:T(8,128)(2,1)S(1)} %get-tuple-element.132), channel_id=1, source_target_pairs={{0,7},{1,6},{2,5},{3,4},{4,3},{5,2},{6,1},{7,0},{8,15},{9,14},{10,... | collective-permute-start | bytes 98312 | tf_op jit(solution)/shard_map/ppermute | solution.py:191
  25.8 6.1 %collective-permute-start.10 = (bf16[128,128]{1,0:T(8,128)(2,1)S(1)}, bf16[128,128]{1,0:T(8,128)(2,1)S(1)}, u32[]{:S(2)}, u32[]{:S(2)}) collective-permute-start(bf16[128,128]{1,0:T(8,128)(2,1)S(1)} %fusion.39), channel_id=1, source_target_pairs={{0,3},{1,2},{2,1},{3,0},{4,7},{5,6},{6,5},{7,4},{8,11},{9,10},{10,... | collective-permute-start | bytes 98312 | tf_op jit(solution)/shard_map/ppermute | solution.py:191
  26.9 3.1 %copy-start = (bf16[256,1024]{1,0:T(8,128)(2,1)S(1)}, bf16[256,1024]{1,0:T(8,128)(2,1)}, u32[]{:S(2)}) copy-start(bf16[256,1024]{1,0:T(8,128)(2,1)} %k_ref.3) | copy-start | bytes 1572868
  26.9 3.1 %copy-start.1 = (bf16[256,1024]{1,0:T(8,128)(2,1)S(1)}, bf16[256,1024]{1,0:T(8,128)(2,1)}, u32[]{:S(2)}) copy-start(bf16[256,1024]{1,0:T(8,128)(2,1)} %v_ref.3) | copy-start | bytes 1572868
  26.9 3.1 %copy-start.2 = (bf16[256,1024]{1,0:T(8,128)(2,1)S(1)}, bf16[256,1024]{1,0:T(8,128)(2,1)}, u32[]{:S(2)}) copy-start(bf16[256,1024]{1,0:T(8,128)(2,1)} %q_ref.1) | copy-start | bytes 1572868
  27.7 4.2 %collective-permute-start.13 = (bf16[128,128]{1,0:T(8,128)(2,1)S(1)}, bf16[128,128]{1,0:T(8,128)(2,1)S(1)}, u32[]{:S(2)}, u32[]{:S(2)}) collective-permute-start(bf16[128,128]{1,0:T(8,128)(2,1)S(1)} %get-tuple-element.146), channel_id=1, source_target_pairs={{0,4},{1,5},{2,6},{3,7},{4,0},{5,1},{6,2},{7,3},{8,12},{9,13},{10,... | collective-permute-start | bytes 98312 | tf_op jit(solution)/shard_map/ppermute | solution.py:191
  29.3 4.5 %collective-permute-start.14 = (bf16[128,128]{1,0:T(8,128)(2,1)S(1)}, bf16[128,128]{1,0:T(8,128)(2,1)S(1)}, u32[]{:S(2)}, u32[]{:S(2)}) collective-permute-start(bf16[128,128]{1,0:T(8,128)(2,1)S(1)} %get-tuple-element.145), channel_id=1, source_target_pairs={{0,7},{1,6},{2,5},{3,4},{4,3},{5,2},{6,1},{7,0},{8,15},{9,14},{10,... | collective-permute-start | bytes 98312 | tf_op jit(solution)/shard_map/ppermute | solution.py:191
  31.9 1.9 %copy-start.3 = (bf16[128,128]{1,0:T(8,128)(2,1)}, bf16[128,128]{1,0:T(8,128)(2,1)S(1)}, u32[]{:S(2)}) copy-start(bf16[128,128]{1,0:T(8,128)(2,1)S(1)} %collective-permute-done.10) | copy-start | bytes 98308
  33.9 6.5 %collective-permute-start.15 = (bf16[128,128]{1,0:T(8,128)(2,1)S(1)}, bf16[128,128]{1,0:T(8,128)(2,1)S(1)}, u32[]{:S(2)}, u32[]{:S(2)}) collective-permute-start(bf16[128,128]{1,0:T(8,128)(2,1)S(1)} %fusion.29), channel_id=1, source_target_pairs={{0,24},{1,25},{2,26},{3,27},{4,28},{5,29},{6,30},{7,31},{8,16},{9,... | collective-permute-start | bytes 98312 | tf_op jit(solution)/shard_map/ppermute | solution.py:191
  35.4 5.2 %copy-start.4 = (bf16[128,128]{1,0:T(8,128)(2,1)S(1)}, bf16[128,128]{1,0:T(8,128)(2,1)}, u32[]{:S(2)}) copy-start(bf16[128,128]{1,0:T(8,128)(2,1)} %copy-done.3) | copy-start | bytes 98308
  35.4 5.2 %collective-permute-start.16 = (bf16[128,128]{1,0:T(8,128)(2,1)S(1)}, bf16[128,128]{1,0:T(8,128)(2,1)S(1)}, u32[]{:S(2)}, u32[]{:S(2)}) collective-permute-start(bf16[128,128]{1,0:T(8,128)(2,1)S(1)} %fusion.29), channel_id=1, source_target_pairs={{0,9},{1,8},{2,11},{3,10},{4,13},{5,12},{6,15},{7,14},{8,1},{9,0},... | collective-permute-start | bytes 98312 | tf_op jit(solution)/shard_map/ppermute | solution.py:191
  36.2 4.3 %collective-permute-start.17 = (bf16[128,128]{1,0:T(8,128)(2,1)S(1)}, bf16[128,128]{1,0:T(8,128)(2,1)S(1)}, u32[]{:S(2)}, u32[]{:S(2)}) collective-permute-start(bf16[128,128]{1,0:T(8,128)(2,1)S(1)} %fusion.29), channel_id=1, source_target_pairs={{0,17},{1,16},{2,19},{3,18},{4,21},{5,20},{6,23},{7,22},{8,25},{9,... | collective-permute-start | bytes 98312 | tf_op jit(solution)/shard_map/ppermute | solution.py:191
  38.0 5.7 %collective-permute-start.21 = (bf16[2,640,128]{2,1,0:T(8,128)(2,1)S(1)}, bf16[2,640,128]{2,1,0:T(8,128)(2,1)S(1)}, u32[]{:S(2)}, u32[]{:S(2)}) collective-permute-start(bf16[2,640,128]{2,1,0:T(8,128)(2,1)S(1)} %get-tuple-element.112), channel_id=1, source_target_pairs={{0,1},{1,0},{2,3},{3,2},{4,5},{5,4},{6,7},{7,6},{8,9},{9,8},{10,11... | collective-permute-start | bytes 983048 | tf_op jit(solution)/shard_map/ppermute | solution.py:191
  38.0 5.7 %collective-permute-start.22 = (bf16[2,640,128]{2,1,0:T(8,128)(2,1)S(1)}, bf16[2,640,128]{2,1,0:T(8,128)(2,1)S(1)}, u32[]{:S(2)}, u32[]{:S(2)}) collective-permute-start(bf16[2,640,128]{2,1,0:T(8,128)(2,1)S(1)} %get-tuple-element.114), channel_id=1, source_target_pairs={{0,1},{1,0},{2,3},{3,2},{4,5},{5,4},{6,7},{7,6},{8,9},{9,8},{10,11... | collective-permute-start | bytes 983048 | tf_op jit(solution)/shard_map/ppermute | solution.py:191
  40.6 5.0 %collective-permute-start.18 = (bf16[128,128]{1,0:T(8,128)(2,1)S(1)}, bf16[128,128]{1,0:T(8,128)(2,1)S(1)}, u32[]{:S(2)}, u32[]{:S(2)}) collective-permute-start(bf16[128,128]{1,0:T(8,128)(2,1)S(1)} %get-tuple-element.137), channel_id=1, source_target_pairs={{0,3},{1,2},{2,1},{3,0},{4,7},{5,6},{6,5},{7,4},{8,11},{9,10},{10,... | collective-permute-start | bytes 98312 | tf_op jit(solution)/shard_map/ppermute | solution.py:191
  41.6 4.3 %collective-permute-start.19 = (bf16[128,128]{1,0:T(8,128)(2,1)S(1)}, bf16[128,128]{1,0:T(8,128)(2,1)S(1)}, u32[]{:S(2)}, u32[]{:S(2)}) collective-permute-start(bf16[128,128]{1,0:T(8,128)(2,1)S(1)} %get-tuple-element.142), channel_id=1, source_target_pairs={{0,4},{1,5},{2,6},{3,7},{4,0},{5,1},{6,2},{7,3},{8,12},{9,13},{10,... | collective-permute-start | bytes 98312 | tf_op jit(solution)/shard_map/ppermute | solution.py:191
  41.6 4.6 %collective-permute-start.20 = (bf16[128,128]{1,0:T(8,128)(2,1)S(1)}, bf16[128,128]{1,0:T(8,128)(2,1)S(1)}, u32[]{:S(2)}, u32[]{:S(2)}) collective-permute-start(bf16[128,128]{1,0:T(8,128)(2,1)S(1)} %get-tuple-element.136), channel_id=1, source_target_pairs={{0,7},{1,6},{2,5},{3,4},{4,3},{5,2},{6,1},{7,0},{8,15},{9,14},{10,... | collective-permute-start | bytes 98312 | tf_op jit(solution)/shard_map/ppermute | solution.py:191
  46.4 1.4 %collective-permute-start.23 = (bf16[4,128,128]{2,1,0:T(8,128)(2,1)S(1)}, bf16[4,128,128]{2,1,0:T(8,128)(2,1)S(1)}, u32[]{:S(2)}, u32[]{:S(2)}) collective-permute-start(bf16[4,128,128]{2,1,0:T(8,128)(2,1)S(1)} %get-tuple-element.135), channel_id=1, source_target_pairs={{0,1},{1,0},{2,3},{3,2},{4,5},{5,4},{6,7},{7,6},{8,9},{9,8},{10,11... | collective-permute-start | bytes 393224 | tf_op jit(solution)/shard_map/ppermute | solution.py:191

commit v6 on v5

--- a/solution.py
+++ b/solution.py
@@ -100,25 +100,25 @@
     return pl.ds(pl.multiple_of(((slot ^ key) & (half - 1)) * HD, HD), HD)
 
 
-def local_kernel(key_ref, kv_ref, qg_ref, their_kv_ref, their_qg_ref, mixed_ref):
-    key = key_ref[0]
-    half = mixed_ref.shape[1]
-    low = triangle(mixed_ref.shape[2], True)
+def local_kernel(key_ref, kv_ref, qg_ref, their_kv_ref, their_qg_ref, mixed_ref, their_mixed_ref):
+    key = key_ref[0]
+    half = mixed_ref.shape[0]
+    low = triangle(mixed_ref.shape[1], True)
     for j in range(half):
         cols = half_columns(j, key, half)
-        for at, (kv, qg) in enumerate(((kv_ref, qg_ref), (their_kv_ref, their_qg_ref))):
+        for kv, qg, out in ((their_kv_ref, their_qg_ref, their_mixed_ref), (kv_ref, qg_ref, mixed_ref)):
             scores = jnp.where(low, dot(qg[0, :, cols], kv[0, :, cols], 1, 1), 0.0).astype(BF16)
-            mixed_ref[at, j] = dot(scores, kv[1, :, cols], 1, 0)
-
-
-def norm_kernel(base, key_ref, qg_ref, their_qg_ref, mixed_ref, mine_ref, theirs_ref, att_ref, gm_ref, state_ref, pack_ref, their_state_ref):
-    key = key_ref[0]
-    half, rows = mixed_ref.shape[1:3]
+            out[j] = dot(scores, kv[1, :, cols], 1, 0).astype(out.dtype)
+
+
+def norm_kernel(base, key_ref, qg_ref, their_qg_ref, mixed_ref, their_mixed_ref, mine_ref, theirs_ref, att_ref, gm_ref, state_ref, pack_ref, their_state_ref):
+    key = key_ref[0]
+    half, rows = mixed_ref.shape[:2]
     for j in range(mine_ref.shape[0]):
         cols = half_columns(base + j, key, half)
-        for at, (qg, e) in enumerate(((qg_ref, mine_ref), (their_qg_ref, theirs_ref))):
+        for at, (qg, own_part, e) in enumerate(((qg_ref, mixed_ref, mine_ref), (their_qg_ref, their_mixed_ref, theirs_ref))):
             q = qg[0, :, cols]
-            mixed = mixed_ref[at, base + j] + dot(q, e[j], 1, 0)
+            mixed = own_part[base + j] + dot(q, e[j], 1, 0)
             inv_rms = lax.rsqrt(jnp.mean(mixed * mixed, axis=-1, keepdims=True) + 1.0)
             normed = mixed * inv_rms
             g = qg[1, :, cols].astype(F32)
@@ -207,6 +207,7 @@
 
 
 ORDER = (1, 2, 3)
+FORWARD = (2, 1, 0)
 SCATTER = (3, 4, 7)
 
 
@@ -255,6 +256,8 @@
     second = None
     for at, masks in enumerate(exchange_levels(count)):
         rounded = cluster.astype(BF16)
+        if not backward and len(masks) == 3:
+            masks = [masks[i] for i in FORWARD]
         arrived = [swap(rounded, mask, count) for mask in masks]
         if at == 0:
             arrived, second = beside(arrived, works[1], rounded)
@@ -310,27 +313,21 @@
     )
     (own,) = call(own_kernel, [((half, HD, HD), BF16)], (tied(send), kv_own), work)
     from_core = swap(send, 1, count)
-    brought = []
-
-    def fetch(tie):
-        brought.extend(call(
+    def ready(tie):
+        qg_send, qg_own = call(
             functools.partial(fetch_kernel, half), [(wide, BF16), (wide, BF16)],
             (tied(tie), query_rows, grad_out), 0, in_hbm=(1, 2), scratch=(pairs,),
-        ))
-        return brought
-
-    def local(tie):
-        qg_send, qg_own = brought
-        kv = swap(tie_to(kv_send, tie), 1, count)
-        qg = swap(tie_to(qg_send, tie), 1, count)
-        brought.append(qg)
-        return call(
-            local_kernel, [((2, half, rows, HD), F32)], (tied(tie), kv_own, qg_own, kv, qg), 4 * scores,
-        )[0]
-
-    entering, ((_, qg_own), mixed, _) = merge(own, from_core, place, count, False, ((fetch, False), local, None))
-
-    qg = brought[2]
+        )
+        mixed, mixed_send = call(
+            local_kernel, [(block, F32), (block, F32)], (key, kv_own, qg_own, kv_send, qg_send), 4 * scores,
+        )
+        return qg_own, mixed, qg_send, mixed_send
+
+    entering, ((qg_own, mixed, qg_send, mixed_send), _, _) = merge(
+        own, from_core, place, count, False, ((ready, False), None, None)
+    )
+    qg = swap(qg_send, 1, count)
+    their_mixed = swap(mixed_send, 1, count)
 
     def norm(slot, mine, theirs):
         n = mine.shape[0]
@@ -339,7 +336,7 @@
         return call(
             functools.partial(norm_kernel, slot),
             [(rows_of, BF16), (rows_of, BF16), (states, BF16), ((n, 2 * rows + HD, HD), BF16), (states, BF16)],
-            (key, qg_own, qg, mixed, mine, theirs), n * work // 2,
+            (key, qg_own, qg, mixed, their_mixed, mine, theirs), n * work // 2,
         )
 
     inner, outer = [], []

time: 49 us -> 48.5 us (0.990)
  waiting for transfers between devices: 13.1 us -> 12.6 us
    ppermute x24, waiting for transfers between devices: 13.1 us -> 12.6 us  [swap(): return lax.ppermute(array, AXES, [(i, i ^ mask) for i in range(count)])]
where the time goes in v6:
time: 48.5 us; the launch traced here: 48.3 us
  starting transfers between devices  23.2 us (48%)
  waiting for transfers between devices  12.6 us (26%)
  Pallas kernels  11 us (23%)
  between operations  0.89 us (2%)
  other arithmetic  0.57 us (1%)
    ppermute x24, starting transfers between devices, swap(): return lax.ppermute(array, AXES, [(i, i ^ mask) for i in range(count)])  23.2 us
    ppermute x24, waiting for transfers between devices, swap(): return lax.ppermute(array, AXES, [(i, i ^ mask) for i in range(count)])  12.6 us
    pallas_call x10, Pallas kernels, call(): pl.pallas_call(kernel, out_shape=shapes, in_specs=specs, out_specs=[hbm i...  11 us
  transfers between devices with their start and end apart: 24, of which 13 were waited for; matrix products, arithmetic and copies ran while one was open for 1% of the time, Pallas kernels for 18%

profile of v6, /device:TPU:0, one launch (start us, length us, event | category | flops | bytes accessed | tf_op | source)
XLA Modules:
  0.0 48.3 jit_solution(13846562050163304412)
XLA Ops:
  0.6 1.3 %shard_map.75 = (bf16[4,128,128]{2,1,0:T(8,128)(2,1)S(1)}, bf16[2,256,512]{2,1,0:T(8,128)(2,1)S(1)}, bf16[2,256,512]{2,1,0:T(8,128)(2,1)S(1)}) custom-call(s32[1]{0:T(128)} %bitcast.key_ref, bf16[256,1024]{1,0:T(8,128)(2,1)} %k_ref.3, bf16[256,1024]{1,0:T(8,128)(2,1)} %v_ref.3), custom_call_target="tpu_custom_call" | custom-call | flops 100663296 | bytes 6684684 | tf_op jit(solution)/shard_map/pallas_call | solution.py:44
  2.0 0.5 %collective-permute-start = (bf16[4,128,128]{2,1,0:T(8,128)(2,1)S(1)}, bf16[4,128,128]{2,1,0:T(8,128)(2,1)S(1)}, u32[]{:S(2)}, u32[]{:S(2)}) collective-permute-start(bf16[4,128,128]{2,1,0:T(8,128)(2,1)S(1)} %get-tuple-element.66), channel_id=1, source_target_pairs={{0,1},{1,0},{2,3},{3,2},{4,5},{5,4},{6,7},{7,6},{8,9},{9,8},{10,11... | collective-permute-start | bytes 393224 | tf_op jit(solution)/shard_map/ppermute | solution.py:191
  2.5 0.3 shard_map.76
  2.8 0.7 %collective-permute-done = bf16[4,128,128]{2,1,0:T(8,128)(2,1)S(1)} collective-permute-done((bf16[4,128,128]{2,1,0:T(8,128)(2,1)S(1)}, bf16[4,128,128]{2,1,0:T(8,128)(2,1)S(1)}, u32[]{:S(2)}, u32[]{:S(2)}) %collective-permute-start) | collective-permute-done | bytes 131104 | tf_op jit(solution)/shard_map/ppermute | solution.py:191
  3.5 2.7 %collective-permute-start.1 = (bf16[128,128]{1,0:T(8,128)(2,1)S(1)}, bf16[128,128]{1,0:T(8,128)(2,1)S(1)}, u32[]{:S(2)}, u32[]{:S(2)}) collective-permute-start(bf16[128,128]{1,0:T(8,128)(2,1)S(1)} %get-tuple-element.136), channel_id=1, source_target_pairs={{0,3},{1,2},{2,1},{3,0},{4,7},{5,6},{6,5},{7,4},{8,11},{9,10},{10,... | collective-permute-start | bytes 98312 | tf_op jit(solution)/shard_map/ppermute | solution.py:191
  6.2 1.6 %collective-permute-start.2 = (bf16[128,128]{1,0:T(8,128)(2,1)S(1)}, bf16[128,128]{1,0:T(8,128)(2,1)S(1)}, u32[]{:S(2)}, u32[]{:S(2)}) collective-permute-start(bf16[128,128]{1,0:T(8,128)(2,1)S(1)} %get-tuple-element.135), channel_id=1, source_target_pairs={{0,4},{1,5},{2,6},{3,7},{4,0},{5,1},{6,2},{7,3},{8,12},{9,13},{10,... | collective-permute-start | bytes 98312 | tf_op jit(solution)/shard_map/ppermute | solution.py:191
  7.8 0.0 collective-permute-start.3
  7.8 1.2 %shard_map.77 = (bf16[2,256,512]{2,1,0:T(8,128)(2,1)S(1)}, bf16[2,256,512]{2,1,0:T(8,128)(2,1)S(1)}) custom-call(s32[1]{0:T(128)} %bitcast.key_ref, bf16[256,1024]{1,0:T(8,128)(2,1)} %q_ref.1, bf16[256,1024]{1,0:T(8,128)(2,1)} %g_hbm.1), custom_call_target="tpu_custom_call" | custom-call | bytes 6291468 | tf_op jit(solution)/shard_map/pallas_call | solution.py:44
  9.0 0.9 %shard_map.78 = (f32[4,256,128]{2,1,0:T(8,128)S(1)}, f32[4,256,128]{2,1,0:T(8,128)S(1)}) custom-call(s32[1]{0:T(128)} %bitcast.key_ref, bf16[2,256,512]{2,1,0:T(8,128)(2,1)S(1)} %get-tuple-element.68.kv_ref, bf16[2,256,512]{2,1,0:T(8,128)(2,1)S(1)} %get-tuple-element.75.qg_ref, bf16[2,256,512]{2,1,0:T(8,128)(2,1)S(1)} %get-tuple-element.71.their_kv_ref, ...), custom_call_target="tpu_custom_call" | custom-call | flops 805306368 | bytes 9437196 | tf_op jit(solution)/shard_map/pallas_call | solution.py:44
  10.0 0.0 collective-permute-done.1
  10.0 0.2 collective-permute-done.2
  10.1 2.0 %collective-permute-done.3 = bf16[128,128]{1,0:T(8,128)(2,1)S(1)} collective-permute-done((bf16[128,128]{1,0:T(8,128)(2,1)S(1)}, bf16[128,128]{1,0:T(8,128)(2,1)S(1)}, u32[]{:S(2)}, u32[]{:S(2)}) %collective-permute-start.3) | collective-permute-done | bytes 32800 | tf_op jit(solution)/shard_map/ppermute | solution.py:191
  12.2 3.6 %collective-permute-start.8 = (bf16[128,128]{1,0:T(8,128)(2,1)S(1)}, bf16[128,128]{1,0:T(8,128)(2,1)S(1)}, u32[]{:S(2)}, u32[]{:S(2)}) collective-permute-start(bf16[128,128]{1,0:T(8,128)(2,1)S(1)} %fusion.15), channel_id=1, source_target_pairs={{0,24},{1,25},{2,26},{3,27},{4,28},{5,29},{6,30},{7,31},{8,16},{9,... | collective-permute-start | bytes 98312 | tf_op jit(solution)/shard_map/ppermute | solution.py:191
  15.8 0.0 collective-permute-start.7
  15.8 0.6 %collective-permute-start.6 = (bf16[128,128]{1,0:T(8,128)(2,1)S(1)}, bf16[128,128]{1,0:T(8,128)(2,1)S(1)}, u32[]{:S(2)}, u32[]{:S(2)}) collective-permute-start(bf16[128,128]{1,0:T(8,128)(2,1)S(1)} %fusion.15), channel_id=1, source_target_pairs={{0,17},{1,16},{2,19},{3,18},{4,21},{5,20},{6,23},{7,22},{8,25},{9,... | collective-permute-start | bytes 98312 | tf_op jit(solution)/shard_map/ppermute | solution.py:191
  16.3 0.1 collective-permute-start.4
  16.4 0.4 collective-permute-start.5
  16.8 1.3 %collective-permute-done.8 = bf16[128,128]{1,0:T(8,128)(2,1)S(1)} collective-permute-done((bf16[128,128]{1,0:T(8,128)(2,1)S(1)}, bf16[128,128]{1,0:T(8,128)(2,1)S(1)}, u32[]{:S(2)}, u32[]{:S(2)}) %collective-permute-start.8) | collective-permute-done | bytes 32800 | tf_op jit(solution)/shard_map/ppermute | solution.py:191
  18.2 2.8 %collective-permute-done.7 = bf16[128,128]{1,0:T(8,128)(2,1)S(1)} collective-permute-done((bf16[128,128]{1,0:T(8,128)(2,1)S(1)}, bf16[128,128]{1,0:T(8,128)(2,1)S(1)}, u32[]{:S(2)}, u32[]{:S(2)}) %collective-permute-start.7) | collective-permute-done | bytes 32800 | tf_op jit(solution)/shard_map/ppermute | solution.py:191
  21.0 0.0 collective-permute-done.6
  21.0 0.1 fusion.11
  21.0 0.4 collective-permute-start.9
  21.4 0.1 fusion.8
  21.5 0.1 collective-permute-start.11
  21.6 2.6 %collective-permute-start.12 = (bf16[128,128]{1,0:T(8,128)(2,1)S(1)}, bf16[128,128]{1,0:T(8,128)(2,1)S(1)}, u32[]{:S(2)}, u32[]{:S(2)}) collective-permute-start(bf16[128,128]{1,0:T(8,128)(2,1)S(1)} %get-tuple-element.128), channel_id=1, source_target_pairs={{0,7},{1,6},{2,5},{3,4},{4,3},{5,2},{6,1},{7,0},{8,15},{9,14},{10,... | collective-permute-start | bytes 98312 | tf_op jit(solution)/shard_map/ppermute | solution.py:191
  24.2 0.3 collective-permute-done.9
  24.6 0.0 collective-permute-done.5.their_mixed_ref
  24.6 0.7 %shard_map.79 = (bf16[2,256,128]{2,1,0:T(8,128)(2,1)S(1)}, bf16[2,256,128]{2,1,0:T(8,128)(2,1)S(1)}, bf16[2,128,128]{2,1,0:T(8,128)(2,1)S(1)}, bf16[2,640,128]{2,1,0:T(8,128)(2,1)S(1)}, bf16[2,128,128]{2,1,0:T(8,128)(2,1)S(1)}) custom-call(s32[1]{0:T(128)} %bitcast.key_ref, bf16[2,256,512]{2,1,0:T(8,128)(2,1)S(1)} %get-tuple-element.75.qg_ref, ...), custom_call_target="tpu_custom_call" | custom-call | flops 100663296 | bytes 8847372 | tf_op jit(solution)/shard_map/pallas_call | solution.py:44
  25.3 0.4 collective-permute-start.10
  25.7 0.0 collective-permute-done.11
  25.7 0.6 %collective-permute-done.12 = bf16[128,128]{1,0:T(8,128)(2,1)S(1)} collective-permute-done((bf16[128,128]{1,0:T(8,128)(2,1)S(1)}, bf16[128,128]{1,0:T(8,128)(2,1)S(1)}, u32[]{:S(2)}, u32[]{:S(2)}) %collective-permute-start.12) | collective-permute-done | bytes 32800 | tf_op jit(solution)/shard_map/ppermute | solution.py:191
  26.4 0.0 copy-start
  26.4 0.0 copy-start.1
  26.4 0.0 copy-start.2
  26.4 0.7 %shard_map.80 = (bf16[2,256,128]{2,1,0:T(8,128)(2,1)S(1)}, bf16[2,256,128]{2,1,0:T(8,128)(2,1)S(1)}, bf16[2,128,128]{2,1,0:T(8,128)(2,1)S(1)}, bf16[2,640,128]{2,1,0:T(8,128)(2,1)S(1)}, bf16[2,128,128]{2,1,0:T(8,128)(2,1)S(1)}) custom-call(s32[1]{0:T(128)} %bitcast.key_ref, bf16[2,256,512]{2,1,0:T(8,128)(2,1)S(1)} %get-tuple-element.75.qg_ref, ...), custom_call_target="tpu_custom_call" | custom-call | flops 100663296 | bytes 8847372 | tf_op jit(solution)/shard_map/pallas_call | solution.py:44
  27.2 1.6 %collective-permute-start.13 = (bf16[128,128]{1,0:T(8,128)(2,1)S(1)}, bf16[128,128]{1,0:T(8,128)(2,1)S(1)}, u32[]{:S(2)}, u32[]{:S(2)}) collective-permute-start(bf16[128,128]{1,0:T(8,128)(2,1)S(1)} %get-tuple-element.142), channel_id=1, source_target_pairs={{0,4},{1,5},{2,6},{3,7},{4,0},{5,1},{6,2},{7,3},{8,12},{9,13},{10,... | collective-permute-start | bytes 98312 | tf_op jit(solution)/shard_map/ppermute | solution.py:191
  28.8 0.7 %collective-permute-start.14 = (bf16[128,128]{1,0:T(8,128)(2,1)S(1)}, bf16[128,128]{1,0:T(8,128)(2,1)S(1)}, u32[]{:S(2)}, u32[]{:S(2)}) collective-permute-start(bf16[128,128]{1,0:T(8,128)(2,1)S(1)} %get-tuple-element.141), channel_id=1, source_target_pairs={{0,7},{1,6},{2,5},{3,4},{4,3},{5,2},{6,1},{7,0},{8,15},{9,14},{10,... | collective-permute-start | bytes 98312 | tf_op jit(solution)/shard_map/ppermute | solution.py:191
  29.5 1.9 %shard_map.81 = (bf16[256,1024]{1,0:T(8,128)(2,1)}, bf16[256,1024]{1,0:T(8,128)(2,1)}, bf16[4,256,128]{2,1,0:T(8,128)(2,1)S(1)}, bf16[4,256,128]{2,1,0:T(8,128)(2,1)S(1)}) custom-call(s32[1]{0:T(128)} %bitcast.key_ref, bf16[256,1024]{1,0:T(8,128)(2,1)S(1)} %copy-done.2, bf16[256,1024]{1,0:T(8,128)(2,1)S(1)} %copy-done, bf16[256,1024]{1,0:T(8,128)(2,1)S(1)} %copy-done.1, ...), custom_call_target="tpu_custom_call" | custom-call | flops 905969664 | bytes 11403276 | tf_op jit(solution)/shard_map/pallas_call | solution.py:44
  31.4 0.0 copy-start.3
  31.4 0.0 collective-permute-done.13
  31.4 1.9 %collective-permute-done.14 = bf16[128,128]{1,0:T(8,128)(2,1)S(1)} collective-permute-done((bf16[128,128]{1,0:T(8,128)(2,1)S(1)}, bf16[128,128]{1,0:T(8,128)(2,1)S(1)}, u32[]{:S(2)}, u32[]{:S(2)}) %collective-permute-start.14) | collective-permute-done | bytes 32800 | tf_op jit(solution)/shard_map/ppermute | solution.py:191
  33.4 1.5 %collective-permute-start.15 = (bf16[128,128]{1,0:T(8,128)(2,1)S(1)}, bf16[128,128]{1,0:T(8,128)(2,1)S(1)}, u32[]{:S(2)}, u32[]{:S(2)}) collective-permute-start(bf16[128,128]{1,0:T(8,128)(2,1)S(1)} %fusion.29), channel_id=1, source_target_pairs={{0,24},{1,25},{2,26},{3,27},{4,28},{5,29},{6,30},{7,31},{8,16},{9,... | collective-permute-start | bytes 98312 | tf_op jit(solution)/shard_map/ppermute | solution.py:191
  34.8 0.9 %collective-permute-start.16 = (bf16[128,128]{1,0:T(8,128)(2,1)S(1)}, bf16[128,128]{1,0:T(8,128)(2,1)S(1)}, u32[]{:S(2)}, u32[]{:S(2)}) collective-permute-start(bf16[128,128]{1,0:T(8,128)(2,1)S(1)} %fusion.29), channel_id=1, source_target_pairs={{0,9},{1,8},{2,11},{3,10},{4,13},{5,12},{6,15},{7,14},{8,1},{9,0},... | collective-permute-start | bytes 98312 | tf_op jit(solution)/shard_map/ppermute | solution.py:191
  35.7 1.8 %collective-permute-start.17 = (bf16[128,128]{1,0:T(8,128)(2,1)S(1)}, bf16[128,128]{1,0:T(8,128)(2,1)S(1)}, u32[]{:S(2)}, u32[]{:S(2)}) collective-permute-start(bf16[128,128]{1,0:T(8,128)(2,1)S(1)} %fusion.29), channel_id=1, source_target_pairs={{0,17},{1,16},{2,19},{3,18},{4,21},{5,20},{6,23},{7,22},{8,25},{9,... | collective-permute-start | bytes 98312 | tf_op jit(solution)/shard_map/ppermute | solution.py:191
  37.5 0.5 %collective-permute-start.22 = (bf16[2,640,128]{2,1,0:T(8,128)(2,1)S(1)}, bf16[2,640,128]{2,1,0:T(8,128)(2,1)S(1)}, u32[]{:S(2)}, u32[]{:S(2)}) collective-permute-start(bf16[2,640,128]{2,1,0:T(8,128)(2,1)S(1)} %get-tuple-element.110), channel_id=1, source_target_pairs={{0,1},{1,0},{2,3},{3,2},{4,5},{5,4},{6,7},{7,6},{8,9},{9,8},{10,11... | collective-permute-start | bytes 983048 | tf_op jit(solution)/shard_map/ppermute | solution.py:191
  38.1 1.7 %collective-permute-done.15 = bf16[128,128]{1,0:T(8,128)(2,1)S(1)} collective-permute-done((bf16[128,128]{1,0:T(8,128)(2,1)S(1)}, bf16[128,128]{1,0:T(8,128)(2,1)S(1)}, u32[]{:S(2)}, u32[]{:S(2)}) %collective-permute-start.15) | collective-permute-done | bytes 32800 | tf_op jit(solution)/shard_map/ppermute | solution.py:191
  39.8 0.2 collective-permute-done.16
  40.0 0.0 collective-permute-done.17
  40.0 0.1 fusion.21
  40.1 0.9 %collective-permute-start.18 = (bf16[128,128]{1,0:T(8,128)(2,1)S(1)}, bf16[128,128]{1,0:T(8,128)(2,1)S(1)}, u32[]{:S(2)}, u32[]{:S(2)}) collective-permute-start(bf16[128,128]{1,0:T(8,128)(2,1)S(1)} %get-tuple-element.133), channel_id=1, source_target_pairs={{0,3},{1,2},{2,1},{3,0},{4,7},{5,6},{6,5},{7,4},{8,11},{9,10},{10,... | collective-permute-start | bytes 98312 | tf_op jit(solution)/shard_map/ppermute | solution.py:191
  41.0 0.1 fusion.25
  41.0 0.1 collective-permute-start.19
  41.1 2.1 %collective-permute-start.20 = (bf16[128,128]{1,0:T(8,128)(2,1)S(1)}, bf16[128,128]{1,0:T(8,128)(2,1)S(1)}, u32[]{:S(2)}, u32[]{:S(2)}) collective-permute-start(bf16[128,128]{1,0:T(8,128)(2,1)S(1)} %get-tuple-element.132), channel_id=1, source_target_pairs={{0,7},{1,6},{2,5},{3,4},{4,3},{5,2},{6,1},{7,0},{8,15},{9,14},{10,... | collective-permute-start | bytes 98312 | tf_op jit(solution)/shard_map/ppermute | solution.py:191
  43.2 0.0 collective-permute-done.21.refs_0_
  43.2 0.0 collective-permute-done.22.refs_1_
  43.2 1.9 %shard_map.82 = (bf16[256,1024]{1,0:T(8,128)(2,1)}, bf16[256,1024]{1,0:T(8,128)(2,1)}, bf16[4,256,128]{2,1,0:T(8,128)(2,1)S(1)}, bf16[4,256,128]{2,1,0:T(8,128)(2,1)S(1)}) custom-call(s32[1]{0:T(128)} %bitcast.key_ref, bf16[256,1024]{1,0:T(8,128)(2,1)S(1)} %copy-done.2, bf16[256,1024]{1,0:T(8,128)(2,1)S(1)} %copy-done, ...), custom_call_target="tpu_custom_call", output_to_operand_aliasing={{0}: (6, {}), {1}: (7, {})} | custom-call | flops 905969664 | bytes 14549004 | tf_op jit(solution)/shard_map/pallas_call | solution.py:44
  45.1 0.0 collective-permute-done.18
  45.1 0.2 collective-permute-done.19
  45.3 0.4 collective-permute-done.20
  45.8 0.1 add_convert_fusion
  45.9 0.2 collective-permute-start.23
  46.1 1.0 %shard_map.83 = (bf16[256,1024]{1,0:T(8,128)(2,1)}, bf16[256,1024]{1,0:T(8,128)(2,1)}) custom-call(s32[1]{0:T(128)} %bitcast.key_ref, bf16[256,1024]{1,0:T(8,128)(2,1)S(1)} %copy-done, bf16[256,1024]{1,0:T(8,128)(2,1)S(1)} %copy-done.1, bf16[4,256,128]{2,1,0:T(8,128)(2,1)S(1)} %get-tuple-element.122.kl_ref, ...), custom_call_target="tpu_custom_call" | custom-call | flops 201326592 | bytes 8257548 | tf_op jit(solution)/shard_map/pallas_call | solution.py:44
  47.1 0.2 collective-permute-done.23.l_ref
  47.3 1.0 %shard_map.84 = (bf16[256,1024]{1,0:T(8,128)(2,1)}, bf16[256,1024]{1,0:T(8,128)(2,1)}) custom-call(s32[1]{0:T(128)} %bitcast.key_ref, bf16[256,1024]{1,0:T(8,128)(2,1)S(1)} %copy-done, bf16[256,1024]{1,0:T(8,128)(2,1)S(1)} %copy-done.1, bf16[4,256,128]{2,1,0:T(8,128)(2,1)S(1)} %get-tuple-element.117.kl_ref, ...), custom_call_target="tpu_custom_call", output_to_operand_aliasing={{0}: (6, {}), {1}: (7, {})} | custom-call | flops 201326592 | bytes 11403276 | tf_op jit(solution)/shard_map/pallas_call | solution.py:44
  (19 shorter events, 0.2 us)
Async XLA Ops:
  2.0 1.5 %collective-permute-start = (bf16[4,128,128]{2,1,0:T(8,128)(2,1)S(1)}, bf16[4,128,128]{2,1,0:T(8,128)(2,1)S(1)}, u32[]{:S(2)}, u32[]{:S(2)}) collective-permute-start(bf16[4,128,128]{2,1,0:T(8,128)(2,1)S(1)} %get-tuple-element.66), channel_id=1, source_target_pairs={{0,1},{1,0},{2,3},{3,2},{4,5},{5,4},{6,7},{7,6},{8,9},{9,8},{10,11... | collective-permute-start | bytes 393224 | tf_op jit(solution)/shard_map/ppermute | solution.py:191
  3.5 6.4 %collective-permute-start.1 = (bf16[128,128]{1,0:T(8,128)(2,1)S(1)}, bf16[128,128]{1,0:T(8,128)(2,1)S(1)}, u32[]{:S(2)}, u32[]{:S(2)}) collective-permute-start(bf16[128,128]{1,0:T(8,128)(2,1)S(1)} %get-tuple-element.136), channel_id=1, source_target_pairs={{0,3},{1,2},{2,1},{3,0},{4,7},{5,6},{6,5},{7,4},{8,11},{9,10},{10,... | collective-permute-start | bytes 98312 | tf_op jit(solution)/shard_map/ppermute | solution.py:191
  6.2 3.9 %collective-permute-start.2 = (bf16[128,128]{1,0:T(8,128)(2,1)S(1)}, bf16[128,128]{1,0:T(8,128)(2,1)S(1)}, u32[]{:S(2)}, u32[]{:S(2)}) collective-permute-start(bf16[128,128]{1,0:T(8,128)(2,1)S(1)} %get-tuple-element.135), channel_id=1, source_target_pairs={{0,4},{1,5},{2,6},{3,7},{4,0},{5,1},{6,2},{7,3},{8,12},{9,13},{10,... | collective-permute-start | bytes 98312 | tf_op jit(solution)/shard_map/ppermute | solution.py:191
  7.8 4.3 %collective-permute-start.3 = (bf16[128,128]{1,0:T(8,128)(2,1)S(1)}, bf16[128,128]{1,0:T(8,128)(2,1)S(1)}, u32[]{:S(2)}, u32[]{:S(2)}) collective-permute-start(bf16[128,128]{1,0:T(8,128)(2,1)S(1)} %get-tuple-element.134), channel_id=1, source_target_pairs={{0,7},{1,6},{2,5},{3,4},{4,3},{5,2},{6,1},{7,0},{8,15},{9,14},{10,... | collective-permute-start | bytes 98312 | tf_op jit(solution)/shard_map/ppermute | solution.py:191
  12.2 6.0 %collective-permute-start.8 = (bf16[128,128]{1,0:T(8,128)(2,1)S(1)}, bf16[128,128]{1,0:T(8,128)(2,1)S(1)}, u32[]{:S(2)}, u32[]{:S(2)}) collective-permute-start(bf16[128,128]{1,0:T(8,128)(2,1)S(1)} %fusion.15), channel_id=1, source_target_pairs={{0,24},{1,25},{2,26},{3,27},{4,28},{5,29},{6,30},{7,31},{8,16},{9,... | collective-permute-start | bytes 98312 | tf_op jit(solution)/shard_map/ppermute | solution.py:191
  15.8 5.2 %collective-permute-start.7 = (bf16[128,128]{1,0:T(8,128)(2,1)S(1)}, bf16[128,128]{1,0:T(8,128)(2,1)S(1)}, u32[]{:S(2)}, u32[]{:S(2)}) collective-permute-start(bf16[128,128]{1,0:T(8,128)(2,1)S(1)} %fusion.15), channel_id=1, source_target_pairs={{0,9},{1,8},{2,11},{3,10},{4,13},{5,12},{6,15},{7,14},{8,1},{9,0},... | collective-permute-start | bytes 98312 | tf_op jit(solution)/shard_map/ppermute | solution.py:191
  15.8 5.2 %collective-permute-start.6 = (bf16[128,128]{1,0:T(8,128)(2,1)S(1)}, bf16[128,128]{1,0:T(8,128)(2,1)S(1)}, u32[]{:S(2)}, u32[]{:S(2)}) collective-permute-start(bf16[128,128]{1,0:T(8,128)(2,1)S(1)} %fusion.15), channel_id=1, source_target_pairs={{0,17},{1,16},{2,19},{3,18},{4,21},{5,20},{6,23},{7,22},{8,25},{9,... | collective-permute-start | bytes 98312 | tf_op jit(solution)/shard_map/ppermute | solution.py:191
  16.3 8.2 %collective-permute-start.4 = (bf16[2,256,512]{2,1,0:T(8,128)(2,1)S(1)}, bf16[2,256,512]{2,1,0:T(8,128)(2,1)S(1)}, u32[]{:S(2)}, u32[]{:S(2)}) collective-permute-start(bf16[2,256,512]{2,1,0:T(8,128)(2,1)S(1)} %get-tuple-element.76.their_qg_ref), channel_id=1, source_target_pairs={{0,1},{1,0},{2,3},{3,2},{4,5},{5,4},{6,7},{7,6},{8,9},{9,8},{10,11... | collective-permute-start | bytes 1572872 | tf_op jit(solution)/shard_map/ppermute | solution.py:191
  16.4 8.2 %collective-permute-start.5 = (f32[4,256,128]{2,1,0:T(8,128)S(1)}, f32[4,256,128]{2,1,0:T(8,128)S(1)}, u32[]{:S(2)}, u32[]{:S(2)}) collective-permute-start(f32[4,256,128]{2,1,0:T(8,128)S(1)} %get-tuple-element.78), channel_id=1, source_target_pairs={{0,1},{1,0},{2,3},{3,2},{4,5},{5,4},{6,7},{7,6},{8,9},{9,8},{10,11... | collective-permute-start | bytes 1572872 | tf_op jit(solution)/shard_map/ppermute | solution.py:191
  21.0 3.5 %collective-permute-start.9 = (bf16[128,128]{1,0:T(8,128)(2,1)S(1)}, bf16[128,128]{1,0:T(8,128)(2,1)S(1)}, u32[]{:S(2)}, u32[]{:S(2)}) collective-permute-start(bf16[128,128]{1,0:T(8,128)(2,1)S(1)} %get-tuple-element.129), channel_id=1, source_target_pairs={{0,3},{1,2},{2,1},{3,0},{4,7},{5,6},{6,5},{7,4},{8,11},{9,10},{10,... | collective-permute-start | bytes 98312 | tf_op jit(solution)/shard_map/ppermute | solution.py:191
  21.5 4.2 %collective-permute-start.11 = (bf16[128,128]{1,0:T(8,128)(2,1)S(1)}, bf16[128,128]{1,0:T(8,128)(2,1)S(1)}, u32[]{:S(2)}, u32[]{:S(2)}) collective-permute-start(bf16[128,128]{1,0:T(8,128)(2,1)S(1)} %get-tuple-element.139), channel_id=1, source_target_pairs={{0,4},{1,5},{2,6},{3,7},{4,0},{5,1},{6,2},{7,3},{8,12},{9,13},{10,... | collective-permute-start | bytes 98312 | tf_op jit(solution)/shard_map/ppermute | solution.py:191
  21.6 4.8 %collective-permute-start.12 = (bf16[128,128]{1,0:T(8,128)(2,1)S(1)}, bf16[128,128]{1,0:T(8,128)(2,1)S(1)}, u32[]{:S(2)}, u32[]{:S(2)}) collective-permute-start(bf16[128,128]{1,0:T(8,128)(2,1)S(1)} %get-tuple-element.128), channel_id=1, source_target_pairs={{0,7},{1,6},{2,5},{3,4},{4,3},{5,2},{6,1},{7,0},{8,15},{9,14},{10,... | collective-permute-start | bytes 98312 | tf_op jit(solution)/shard_map/ppermute | solution.py:191
  25.3 6.0 %collective-permute-start.10 = (bf16[128,128]{1,0:T(8,128)(2,1)S(1)}, bf16[128,128]{1,0:T(8,128)(2,1)S(1)}, u32[]{:S(2)}, u32[]{:S(2)}) collective-permute-start(bf16[128,128]{1,0:T(8,128)(2,1)S(1)} %fusion.39), channel_id=1, source_target_pairs={{0,3},{1,2},{2,1},{3,0},{4,7},{5,6},{6,5},{7,4},{8,11},{9,10},{10,... | collective-permute-start | bytes 98312 | tf_op jit(solution)/shard_map/ppermute | solution.py:191
  26.4 3.1 %copy-start = (bf16[256,1024]{1,0:T(8,128)(2,1)S(1)}, bf16[256,1024]{1,0:T(8,128)(2,1)}, u32[]{:S(2)}) copy-start(bf16[256,1024]{1,0:T(8,128)(2,1)} %k_ref.3) | copy-start | bytes 1572868
  26.4 3.1 %copy-start.1 = (bf16[256,1024]{1,0:T(8,128)(2,1)S(1)}, bf16[256,1024]{1,0:T(8,128)(2,1)}, u32[]{:S(2)}) copy-start(bf16[256,1024]{1,0:T(8,128)(2,1)} %v_ref.3) | copy-start | bytes 1572868
  26.4 3.1 %copy-start.2 = (bf16[256,1024]{1,0:T(8,128)(2,1)S(1)}, bf16[256,1024]{1,0:T(8,128)(2,1)}, u32[]{:S(2)}) copy-start(bf16[256,1024]{1,0:T(8,128)(2,1)} %q_ref.1) | copy-start | bytes 1572868
  27.2 4.2 %collective-permute-start.13 = (bf16[128,128]{1,0:T(8,128)(2,1)S(1)}, bf16[128,128]{1,0:T(8,128)(2,1)S(1)}, u32[]{:S(2)}, u32[]{:S(2)}) collective-permute-start(bf16[128,128]{1,0:T(8,128)(2,1)S(1)} %get-tuple-element.142), channel_id=1, source_target_pairs={{0,4},{1,5},{2,6},{3,7},{4,0},{5,1},{6,2},{7,3},{8,12},{9,13},{10,... | collective-permute-start | bytes 98312 | tf_op jit(solution)/shard_map/ppermute | solution.py:191
  28.8 4.5 %collective-permute-start.14 = (bf16[128,128]{1,0:T(8,128)(2,1)S(1)}, bf16[128,128]{1,0:T(8,128)(2,1)S(1)}, u32[]{:S(2)}, u32[]{:S(2)}) collective-permute-start(bf16[128,128]{1,0:T(8,128)(2,1)S(1)} %get-tuple-element.141), channel_id=1, source_target_pairs={{0,7},{1,6},{2,5},{3,4},{4,3},{5,2},{6,1},{7,0},{8,15},{9,14},{10,... | collective-permute-start | bytes 98312 | tf_op jit(solution)/shard_map/ppermute | solution.py:191
  31.4 2.0 %copy-start.3 = (bf16[128,128]{1,0:T(8,128)(2,1)}, bf16[128,128]{1,0:T(8,128)(2,1)S(1)}, u32[]{:S(2)}) copy-start(bf16[128,128]{1,0:T(8,128)(2,1)S(1)} %collective-permute-done.10) | copy-start | bytes 98308
  33.4 6.4 %collective-permute-start.15 = (bf16[128,128]{1,0:T(8,128)(2,1)S(1)}, bf16[128,128]{1,0:T(8,128)(2,1)S(1)}, u32[]{:S(2)}, u32[]{:S(2)}) collective-permute-start(bf16[128,128]{1,0:T(8,128)(2,1)S(1)} %fusion.29), channel_id=1, source_target_pairs={{0,24},{1,25},{2,26},{3,27},{4,28},{5,29},{6,30},{7,31},{8,16},{9,... | collective-permute-start | bytes 98312 | tf_op jit(solution)/shard_map/ppermute | solution.py:191
  34.8 5.2 %copy-start.4 = (bf16[128,128]{1,0:T(8,128)(2,1)S(1)}, bf16[128,128]{1,0:T(8,128)(2,1)}, u32[]{:S(2)}) copy-start(bf16[128,128]{1,0:T(8,128)(2,1)} %copy-done.3) | copy-start | bytes 98308
  34.8 5.2 %collective-permute-start.16 = (bf16[128,128]{1,0:T(8,128)(2,1)S(1)}, bf16[128,128]{1,0:T(8,128)(2,1)S(1)}, u32[]{:S(2)}, u32[]{:S(2)}) collective-permute-start(bf16[128,128]{1,0:T(8,128)(2,1)S(1)} %fusion.29), channel_id=1, source_target_pairs={{0,9},{1,8},{2,11},{3,10},{4,13},{5,12},{6,15},{7,14},{8,1},{9,0},... | collective-permute-start | bytes 98312 | tf_op jit(solution)/shard_map/ppermute | solution.py:191
  35.7 4.3 %collective-permute-start.17 = (bf16[128,128]{1,0:T(8,128)(2,1)S(1)}, bf16[128,128]{1,0:T(8,128)(2,1)S(1)}, u32[]{:S(2)}, u32[]{:S(2)}) collective-permute-start(bf16[128,128]{1,0:T(8,128)(2,1)S(1)} %fusion.29), channel_id=1, source_target_pairs={{0,17},{1,16},{2,19},{3,18},{4,21},{5,20},{6,23},{7,22},{8,25},{9,... | collective-permute-start | bytes 98312 | tf_op jit(solution)/shard_map/ppermute | solution.py:191
  37.5 5.7 %collective-permute-start.21 = (bf16[2,640,128]{2,1,0:T(8,128)(2,1)S(1)}, bf16[2,640,128]{2,1,0:T(8,128)(2,1)S(1)}, u32[]{:S(2)}, u32[]{:S(2)}) collective-permute-start(bf16[2,640,128]{2,1,0:T(8,128)(2,1)S(1)} %get-tuple-element.108), channel_id=1, source_target_pairs={{0,1},{1,0},{2,3},{3,2},{4,5},{5,4},{6,7},{7,6},{8,9},{9,8},{10,11... | collective-permute-start | bytes 983048 | tf_op jit(solution)/shard_map/ppermute | solution.py:191
  37.5 5.7 %collective-permute-start.22 = (bf16[2,640,128]{2,1,0:T(8,128)(2,1)S(1)}, bf16[2,640,128]{2,1,0:T(8,128)(2,1)S(1)}, u32[]{:S(2)}, u32[]{:S(2)}) collective-permute-start(bf16[2,640,128]{2,1,0:T(8,128)(2,1)S(1)} %get-tuple-element.110), channel_id=1, source_target_pairs={{0,1},{1,0},{2,3},{3,2},{4,5},{5,4},{6,7},{7,6},{8,9},{9,8},{10,11... | collective-permute-start | bytes 983048 | tf_op jit(solution)/shard_map/ppermute | solution.py:191
  40.1 5.0 %collective-permute-start.18 = (bf16[128,128]{1,0:T(8,128)(2,1)S(1)}, bf16[128,128]{1,0:T(8,128)(2,1)S(1)}, u32[]{:S(2)}, u32[]{:S(2)}) collective-permute-start(bf16[128,128]{1,0:T(8,128)(2,1)S(1)} %get-tuple-element.133), channel_id=1, source_target_pairs={{0,3},{1,2},{2,1},{3,0},{4,7},{5,6},{6,5},{7,4},{8,11},{9,10},{10,... | collective-permute-start | bytes 98312 | tf_op jit(solution)/shard_map/ppermute | solution.py:191
  41.0 4.3 %collective-permute-start.19 = (bf16[128,128]{1,0:T(8,128)(2,1)S(1)}, bf16[128,128]{1,0:T(8,128)(2,1)S(1)}, u32[]{:S(2)}, u32[]{:S(2)}) collective-permute-start(bf16[128,128]{1,0:T(8,128)(2,1)S(1)} %get-tuple-element.138), channel_id=1, source_target_pairs={{0,4},{1,5},{2,6},{3,7},{4,0},{5,1},{6,2},{7,3},{8,12},{9,13},{10,... | collective-permute-start | bytes 98312 | tf_op jit(solution)/shard_map/ppermute | solution.py:191
  41.1 4.6 %collective-permute-start.20 = (bf16[128,128]{1,0:T(8,128)(2,1)S(1)}, bf16[128,128]{1,0:T(8,128)(2,1)S(1)}, u32[]{:S(2)}, u32[]{:S(2)}) collective-permute-start(bf16[128,128]{1,0:T(8,128)(2,1)S(1)} %get-tuple-element.132), channel_id=1, source_target_pairs={{0,7},{1,6},{2,5},{3,4},{4,3},{5,2},{6,1},{7,0},{8,15},{9,14},{10,... | collective-permute-start | bytes 98312 | tf_op jit(solution)/shard_map/ppermute | solution.py:191
  45.9 1.4 %collective-permute-start.23 = (bf16[4,128,128]{2,1,0:T(8,128)(2,1)S(1)}, bf16[4,128,128]{2,1,0:T(8,128)(2,1)S(1)}, u32[]{:S(2)}, u32[]{:S(2)}) collective-permute-start(bf16[4,128,128]{2,1,0:T(8,128)(2,1)S(1)} %get-tuple-element.131), channel_id=1, source_target_pairs={{0,1},{1,0},{2,3},{3,2},{4,5},{5,4},{6,7},{7,6},{8,9},{9,8},{10,11... | collective-permute-start | bytes 393224 | tf_op jit(solution)/shard_map/ppermute | solution.py:191

commit v7 on v6

--- a/solution.py
+++ b/solution.py
@@ -199,7 +199,7 @@
         first = (1 << bit) | 1
         if bit + 1 < bits:
             second = 1 << (bit + 1)
-            levels.append(((3 << bit), (1 << bit) | 1, (2 << bit) | 1))
+            levels.append(((3 << bit) | 1, (1 << bit) | 1, (2 << bit)))
         else:
             levels.append((first,))
         bit += 2
@@ -218,7 +218,7 @@
     bits = count.bit_length() - 1
     half = (place ^ (place >> 1)) & 1
     for bit in range(3, bits, 2):
-        half = half ^ ((place >> (bit + 0)) ^ (place >> (bit + 1))) & 1
+        half = half ^ (place >> bit) & 1
     return (half << 2) | ((place >> 1) & 3)
 
 

time: 48.5 us -> 47.9 us (0.988)
  waiting for transfers between devices: 12.6 us -> 11.6 us
    ppermute x24, waiting for transfers between devices: 12.6 us -> 11.6 us  [swap(): return lax.ppermute(array, AXES, [(i, i ^ mask) for i in range(count)])]
  transfers between devices with their start and end apart: 24 -> 24, of which waited for: 13 -> 11; matrix products, arithmetic and copies ran while one was open for 1% -> 1% of each run, Pallas kernels for 18% -> 18%
where the time goes in v7:
time: 47.9 us; the launch traced here: 47.8 us
  starting transfers between devices  23.6 us (49%)
  waiting for transfers between devices  11.6 us (24%)
  Pallas kernels  11.1 us (23%)
  between operations  0.9 us (2%)
  other arithmetic  0.57 us (1%)
    ppermute x24, starting transfers between devices, swap(): return lax.ppermute(array, AXES, [(i, i ^ mask) for i in range(count)])  23.6 us
    ppermute x24, waiting for transfers between devices, swap(): return lax.ppermute(array, AXES, [(i, i ^ mask) for i in range(count)])  11.6 us
    pallas_call x10, Pallas kernels, call(): pl.pallas_call(kernel, out_shape=shapes, in_specs=specs, out_specs=[hbm i...  11.1 us
  transfers between devices with their start and end apart: 24, of which 11 were waited for; matrix products, arithmetic and copies ran while one was open for 1% of the time, Pallas kernels for 18%

profile of v7, /device:TPU:0, one launch (start us, length us, event | category | flops | bytes accessed | tf_op | source)
XLA Modules:
  0.0 47.8 jit_solution(8419717105212233449)
XLA Ops:
  0.6 1.3 %shard_map.75 = (bf16[4,128,128]{2,1,0:T(8,128)(2,1)S(1)}, bf16[2,256,512]{2,1,0:T(8,128)(2,1)S(1)}, bf16[2,256,512]{2,1,0:T(8,128)(2,1)S(1)}) custom-call(s32[1]{0:T(128)} %bitcast.key_ref, bf16[256,1024]{1,0:T(8,128)(2,1)} %k_ref.3, bf16[256,1024]{1,0:T(8,128)(2,1)} %v_ref.3), custom_call_target="tpu_custom_call" | custom-call | flops 100663296 | bytes 6684684 | tf_op jit(solution)/shard_map/pallas_call | solution.py:44
  2.0 0.5 %collective-permute-start = (bf16[4,128,128]{2,1,0:T(8,128)(2,1)S(1)}, bf16[4,128,128]{2,1,0:T(8,128)(2,1)S(1)}, u32[]{:S(2)}, u32[]{:S(2)}) collective-permute-start(bf16[4,128,128]{2,1,0:T(8,128)(2,1)S(1)} %get-tuple-element.66), channel_id=1, source_target_pairs={{0,1},{1,0},{2,3},{3,2},{4,5},{5,4},{6,7},{7,6},{8,9},{9,8},{10,11... | collective-permute-start | bytes 393224 | tf_op jit(solution)/shard_map/ppermute | solution.py:191
  2.5 0.3 shard_map.76
  2.8 0.7 %collective-permute-done = bf16[4,128,128]{2,1,0:T(8,128)(2,1)S(1)} collective-permute-done((bf16[4,128,128]{2,1,0:T(8,128)(2,1)S(1)}, bf16[4,128,128]{2,1,0:T(8,128)(2,1)S(1)}, u32[]{:S(2)}, u32[]{:S(2)}) %collective-permute-start) | collective-permute-done | bytes 131104 | tf_op jit(solution)/shard_map/ppermute | solution.py:191
  3.5 2.7 %collective-permute-start.1 = (bf16[128,128]{1,0:T(8,128)(2,1)S(1)}, bf16[128,128]{1,0:T(8,128)(2,1)S(1)}, u32[]{:S(2)}, u32[]{:S(2)}) collective-permute-start(bf16[128,128]{1,0:T(8,128)(2,1)S(1)} %get-tuple-element.136), channel_id=1, source_target_pairs={{0,3},{1,2},{2,1},{3,0},{4,7},{5,6},{6,5},{7,4},{8,11},{9,10},{10,... | collective-permute-start | bytes 98312 | tf_op jit(solution)/shard_map/ppermute | solution.py:191
  6.2 1.6 %collective-permute-start.2 = (bf16[128,128]{1,0:T(8,128)(2,1)S(1)}, bf16[128,128]{1,0:T(8,128)(2,1)S(1)}, u32[]{:S(2)}, u32[]{:S(2)}) collective-permute-start(bf16[128,128]{1,0:T(8,128)(2,1)S(1)} %get-tuple-element.135), channel_id=1, source_target_pairs={{0,4},{1,5},{2,6},{3,7},{4,0},{5,1},{6,2},{7,3},{8,12},{9,13},{10,... | collective-permute-start | bytes 98312 | tf_op jit(solution)/shard_map/ppermute | solution.py:191
  7.8 0.0 collective-permute-start.3
  7.8 1.2 %shard_map.77 = (bf16[2,256,512]{2,1,0:T(8,128)(2,1)S(1)}, bf16[2,256,512]{2,1,0:T(8,128)(2,1)S(1)}) custom-call(s32[1]{0:T(128)} %bitcast.key_ref, bf16[256,1024]{1,0:T(8,128)(2,1)} %q_ref.1, bf16[256,1024]{1,0:T(8,128)(2,1)} %g_hbm.1), custom_call_target="tpu_custom_call" | custom-call | bytes 6291468 | tf_op jit(solution)/shard_map/pallas_call | solution.py:44
  9.0 0.9 %shard_map.78 = (f32[4,256,128]{2,1,0:T(8,128)S(1)}, f32[4,256,128]{2,1,0:T(8,128)S(1)}) custom-call(s32[1]{0:T(128)} %bitcast.key_ref, bf16[2,256,512]{2,1,0:T(8,128)(2,1)S(1)} %get-tuple-element.68.kv_ref, bf16[2,256,512]{2,1,0:T(8,128)(2,1)S(1)} %get-tuple-element.75.qg_ref, bf16[2,256,512]{2,1,0:T(8,128)(2,1)S(1)} %get-tuple-element.71.their_kv_ref, ...), custom_call_target="tpu_custom_call" | custom-call | flops 805306368 | bytes 9437196 | tf_op jit(solution)/shard_map/pallas_call | solution.py:44
  10.0 0.0 collective-permute-done.1
  10.0 0.2 collective-permute-done.2
  10.1 2.0 %collective-permute-done.3 = bf16[128,128]{1,0:T(8,128)(2,1)S(1)} collective-permute-done((bf16[128,128]{1,0:T(8,128)(2,1)S(1)}, bf16[128,128]{1,0:T(8,128)(2,1)S(1)}, u32[]{:S(2)}, u32[]{:S(2)}) %collective-permute-start.3) | collective-permute-done | bytes 32800 | tf_op jit(solution)/shard_map/ppermute | solution.py:191
  12.2 3.3 %collective-permute-start.8 = (bf16[128,128]{1,0:T(8,128)(2,1)S(1)}, bf16[128,128]{1,0:T(8,128)(2,1)S(1)}, u32[]{:S(2)}, u32[]{:S(2)}) collective-permute-start(bf16[128,128]{1,0:T(8,128)(2,1)S(1)} %fusion.15), channel_id=1, source_target_pairs={{0,25},{1,24},{2,27},{3,26},{4,29},{5,28},{6,31},{7,30},{8,17},{9,... | collective-permute-start | bytes 98312 | tf_op jit(solution)/shard_map/ppermute | solution.py:191
  15.5 0.4 collective-permute-start.7
  15.9 0.5 collective-permute-start.6
  16.3 0.0 collective-permute-start.4
  16.3 0.5 %collective-permute-start.5 = (f32[4,256,128]{2,1,0:T(8,128)S(1)}, f32[4,256,128]{2,1,0:T(8,128)S(1)}, u32[]{:S(2)}, u32[]{:S(2)}) collective-permute-start(f32[4,256,128]{2,1,0:T(8,128)S(1)} %get-tuple-element.78), channel_id=1, source_target_pairs={{0,1},{1,0},{2,3},{3,2},{4,5},{5,4},{6,7},{7,6},{8,9},{9,8},{10,11... | collective-permute-start | bytes 1572872 | tf_op jit(solution)/shard_map/ppermute | solution.py:191
  16.8 1.4 %collective-permute-done.8 = bf16[128,128]{1,0:T(8,128)(2,1)S(1)} collective-permute-done((bf16[128,128]{1,0:T(8,128)(2,1)S(1)}, bf16[128,128]{1,0:T(8,128)(2,1)S(1)}, u32[]{:S(2)}, u32[]{:S(2)}) %collective-permute-start.8) | collective-permute-done | bytes 32800 | tf_op jit(solution)/shard_map/ppermute | solution.py:191
  18.3 2.1 %collective-permute-done.7 = bf16[128,128]{1,0:T(8,128)(2,1)S(1)} collective-permute-done((bf16[128,128]{1,0:T(8,128)(2,1)S(1)}, bf16[128,128]{1,0:T(8,128)(2,1)S(1)}, u32[]{:S(2)}, u32[]{:S(2)}) %collective-permute-start.7) | collective-permute-done | bytes 32800 | tf_op jit(solution)/shard_map/ppermute | solution.py:191
  20.4 0.0 collective-permute-done.6
  20.4 0.1 fusion.11
  20.5 0.4 collective-permute-start.9
  20.9 0.1 fusion.8
  21.0 0.3 collective-permute-start.11
  21.2 2.4 %collective-permute-start.12 = (bf16[128,128]{1,0:T(8,128)(2,1)S(1)}, bf16[128,128]{1,0:T(8,128)(2,1)S(1)}, u32[]{:S(2)}, u32[]{:S(2)}) collective-permute-start(bf16[128,128]{1,0:T(8,128)(2,1)S(1)} %get-tuple-element.128), channel_id=1, source_target_pairs={{0,7},{1,6},{2,5},{3,4},{4,3},{5,2},{6,1},{7,0},{8,15},{9,14},{10,... | collective-permute-start | bytes 98312 | tf_op jit(solution)/shard_map/ppermute | solution.py:191
  23.6 0.3 collective-permute-done.9
  24.0 0.0 collective-permute-done.4.their_qg_ref
  24.0 0.0 collective-permute-done.5.their_mixed_ref
  24.0 0.7 %shard_map.79 = (bf16[2,256,128]{2,1,0:T(8,128)(2,1)S(1)}, bf16[2,256,128]{2,1,0:T(8,128)(2,1)S(1)}, bf16[2,128,128]{2,1,0:T(8,128)(2,1)S(1)}, bf16[2,640,128]{2,1,0:T(8,128)(2,1)S(1)}, bf16[2,128,128]{2,1,0:T(8,128)(2,1)S(1)}) custom-call(s32[1]{0:T(128)} %bitcast.key_ref, bf16[2,256,512]{2,1,0:T(8,128)(2,1)S(1)} %get-tuple-element.75.qg_ref, ...), custom_call_target="tpu_custom_call" | custom-call | flops 100663296 | bytes 8847372 | tf_op jit(solution)/shard_map/pallas_call | solution.py:44
  24.8 0.4 collective-permute-start.10
  25.1 0.0 collective-permute-done.11
  25.1 0.7 %collective-permute-done.12 = bf16[128,128]{1,0:T(8,128)(2,1)S(1)} collective-permute-done((bf16[128,128]{1,0:T(8,128)(2,1)S(1)}, bf16[128,128]{1,0:T(8,128)(2,1)S(1)}, u32[]{:S(2)}, u32[]{:S(2)}) %collective-permute-start.12) | collective-permute-done | bytes 32800 | tf_op jit(solution)/shard_map/ppermute | solution.py:191
  25.9 0.0 copy-start
  25.9 0.0 copy-start.1
  25.9 0.0 copy-start.2
  25.9 0.7 %shard_map.80 = (bf16[2,256,128]{2,1,0:T(8,128)(2,1)S(1)}, bf16[2,256,128]{2,1,0:T(8,128)(2,1)S(1)}, bf16[2,128,128]{2,1,0:T(8,128)(2,1)S(1)}, bf16[2,640,128]{2,1,0:T(8,128)(2,1)S(1)}, bf16[2,128,128]{2,1,0:T(8,128)(2,1)S(1)}) custom-call(s32[1]{0:T(128)} %bitcast.key_ref, bf16[2,256,512]{2,1,0:T(8,128)(2,1)S(1)} %get-tuple-element.75.qg_ref, ...), custom_call_target="tpu_custom_call" | custom-call | flops 100663296 | bytes 8847372 | tf_op jit(solution)/shard_map/pallas_call | solution.py:44
  26.7 1.6 %collective-permute-start.13 = (bf16[128,128]{1,0:T(8,128)(2,1)S(1)}, bf16[128,128]{1,0:T(8,128)(2,1)S(1)}, u32[]{:S(2)}, u32[]{:S(2)}) collective-permute-start(bf16[128,128]{1,0:T(8,128)(2,1)S(1)} %get-tuple-element.142), channel_id=1, source_target_pairs={{0,4},{1,5},{2,6},{3,7},{4,0},{5,1},{6,2},{7,3},{8,12},{9,13},{10,... | collective-permute-start | bytes 98312 | tf_op jit(solution)/shard_map/ppermute | solution.py:191
  28.3 0.7 %collective-permute-start.14 = (bf16[128,128]{1,0:T(8,128)(2,1)S(1)}, bf16[128,128]{1,0:T(8,128)(2,1)S(1)}, u32[]{:S(2)}, u32[]{:S(2)}) collective-permute-start(bf16[128,128]{1,0:T(8,128)(2,1)S(1)} %get-tuple-element.141), channel_id=1, source_target_pairs={{0,7},{1,6},{2,5},{3,4},{4,3},{5,2},{6,1},{7,0},{8,15},{9,14},{10,... | collective-permute-start | bytes 98312 | tf_op jit(solution)/shard_map/ppermute | solution.py:191
  29.0 1.9 %shard_map.81 = (bf16[256,1024]{1,0:T(8,128)(2,1)}, bf16[256,1024]{1,0:T(8,128)(2,1)}, bf16[4,256,128]{2,1,0:T(8,128)(2,1)S(1)}, bf16[4,256,128]{2,1,0:T(8,128)(2,1)S(1)}) custom-call(s32[1]{0:T(128)} %bitcast.key_ref, bf16[256,1024]{1,0:T(8,128)(2,1)S(1)} %copy-done.2, bf16[256,1024]{1,0:T(8,128)(2,1)S(1)} %copy-done, bf16[256,1024]{1,0:T(8,128)(2,1)S(1)} %copy-done.1, ...), custom_call_target="tpu_custom_call" | custom-call | flops 905969664 | bytes 11403276 | tf_op jit(solution)/shard_map/pallas_call | solution.py:44
  30.8 0.0 collective-permute-done.10
  30.9 0.0 copy-start.3
  30.9 1.7 %collective-permute-done.14 = bf16[128,128]{1,0:T(8,128)(2,1)S(1)} collective-permute-done((bf16[128,128]{1,0:T(8,128)(2,1)S(1)}, bf16[128,128]{1,0:T(8,128)(2,1)S(1)}, u32[]{:S(2)}, u32[]{:S(2)}) %collective-permute-start.14) | collective-permute-done | bytes 32800 | tf_op jit(solution)/shard_map/ppermute | solution.py:191
  32.6 1.3 %collective-permute-start.15 = (bf16[128,128]{1,0:T(8,128)(2,1)S(1)}, bf16[128,128]{1,0:T(8,128)(2,1)S(1)}, u32[]{:S(2)}, u32[]{:S(2)}) collective-permute-start(bf16[128,128]{1,0:T(8,128)(2,1)S(1)} %fusion.29), channel_id=1, source_target_pairs={{0,25},{1,24},{2,27},{3,26},{4,29},{5,28},{6,31},{7,30},{8,17},{9,... | collective-permute-start | bytes 98312 | tf_op jit(solution)/shard_map/ppermute | solution.py:191
  34.0 1.3 %collective-permute-start.16 = (bf16[128,128]{1,0:T(8,128)(2,1)S(1)}, bf16[128,128]{1,0:T(8,128)(2,1)S(1)}, u32[]{:S(2)}, u32[]{:S(2)}) collective-permute-start(bf16[128,128]{1,0:T(8,128)(2,1)S(1)} %fusion.29), channel_id=1, source_target_pairs={{0,9},{1,8},{2,11},{3,10},{4,13},{5,12},{6,15},{7,14},{8,1},{9,0},... | collective-permute-start | bytes 98312 | tf_op jit(solution)/shard_map/ppermute | solution.py:191
  35.3 1.5 %collective-permute-start.17 = (bf16[128,128]{1,0:T(8,128)(2,1)S(1)}, bf16[128,128]{1,0:T(8,128)(2,1)S(1)}, u32[]{:S(2)}, u32[]{:S(2)}) collective-permute-start(bf16[128,128]{1,0:T(8,128)(2,1)S(1)} %fusion.29), channel_id=1, source_target_pairs={{0,16},{1,17},{2,18},{3,19},{4,20},{5,21},{6,22},{7,23},{8,24},{9,... | collective-permute-start | bytes 98312 | tf_op jit(solution)/shard_map/ppermute | solution.py:191
  36.8 0.0 collective-permute-start.21
  36.8 0.5 %collective-permute-start.22 = (bf16[2,640,128]{2,1,0:T(8,128)(2,1)S(1)}, bf16[2,640,128]{2,1,0:T(8,128)(2,1)S(1)}, u32[]{:S(2)}, u32[]{:S(2)}) collective-permute-start(bf16[2,640,128]{2,1,0:T(8,128)(2,1)S(1)} %get-tuple-element.110), channel_id=1, source_target_pairs={{0,1},{1,0},{2,3},{3,2},{4,5},{5,4},{6,7},{7,6},{8,9},{9,8},{10,11... | collective-permute-start | bytes 983048 | tf_op jit(solution)/shard_map/ppermute | solution.py:191
  37.3 1.9 %collective-permute-done.15 = bf16[128,128]{1,0:T(8,128)(2,1)S(1)} collective-permute-done((bf16[128,128]{1,0:T(8,128)(2,1)S(1)}, bf16[128,128]{1,0:T(8,128)(2,1)S(1)}, u32[]{:S(2)}, u32[]{:S(2)}) %collective-permute-start.15) | collective-permute-done | bytes 32800 | tf_op jit(solution)/shard_map/ppermute | solution.py:191
  39.2 0.1 fusion.21
  39.3 1.2 %collective-permute-start.18 = (bf16[128,128]{1,0:T(8,128)(2,1)S(1)}, bf16[128,128]{1,0:T(8,128)(2,1)S(1)}, u32[]{:S(2)}, u32[]{:S(2)}) collective-permute-start(bf16[128,128]{1,0:T(8,128)(2,1)S(1)} %get-tuple-element.133), channel_id=1, source_target_pairs={{0,3},{1,2},{2,1},{3,0},{4,7},{5,6},{6,5},{7,4},{8,11},{9,10},{10,... | collective-permute-start | bytes 98312 | tf_op jit(solution)/shard_map/ppermute | solution.py:191
  40.4 0.1 fusion.25
  40.5 0.1 collective-permute-start.19
  40.6 1.9 %collective-permute-start.20 = (bf16[128,128]{1,0:T(8,128)(2,1)S(1)}, bf16[128,128]{1,0:T(8,128)(2,1)S(1)}, u32[]{:S(2)}, u32[]{:S(2)}) collective-permute-start(bf16[128,128]{1,0:T(8,128)(2,1)S(1)} %get-tuple-element.132), channel_id=1, source_target_pairs={{0,7},{1,6},{2,5},{3,4},{4,3},{5,2},{6,1},{7,0},{8,15},{9,14},{10,... | collective-permute-start | bytes 98312 | tf_op jit(solution)/shard_map/ppermute | solution.py:191
  42.5 0.0 collective-permute-done.21.refs_0_
  42.5 0.0 collective-permute-done.22.refs_1_
  42.5 1.9 %shard_map.82 = (bf16[256,1024]{1,0:T(8,128)(2,1)}, bf16[256,1024]{1,0:T(8,128)(2,1)}, bf16[4,256,128]{2,1,0:T(8,128)(2,1)S(1)}, bf16[4,256,128]{2,1,0:T(8,128)(2,1)S(1)}) custom-call(s32[1]{0:T(128)} %bitcast.key_ref, bf16[256,1024]{1,0:T(8,128)(2,1)S(1)} %copy-done.2, bf16[256,1024]{1,0:T(8,128)(2,1)S(1)} %copy-done, ...), custom_call_target="tpu_custom_call", output_to_operand_aliasing={{0}: (6, {}), {1}: (7, {})} | custom-call | flops 905969664 | bytes 14549004 | tf_op jit(solution)/shard_map/pallas_call | solution.py:44
  44.3 0.0 collective-permute-done.18
  44.3 0.2 collective-permute-done.19
  44.5 0.4 collective-permute-done.20
  45.0 0.1 add_convert_fusion
  45.0 0.6 %collective-permute-start.23 = (bf16[4,128,128]{2,1,0:T(8,128)(2,1)S(1)}, bf16[4,128,128]{2,1,0:T(8,128)(2,1)S(1)}, u32[]{:S(2)}, u32[]{:S(2)}) collective-permute-start(bf16[4,128,128]{2,1,0:T(8,128)(2,1)S(1)} %get-tuple-element.131), channel_id=1, source_target_pairs={{0,1},{1,0},{2,3},{3,2},{4,5},{5,4},{6,7},{7,6},{8,9},{9,8},{10,11... | collective-permute-start | bytes 393224 | tf_op jit(solution)/shard_map/ppermute | solution.py:191
  45.7 1.0 %shard_map.83 = (bf16[256,1024]{1,0:T(8,128)(2,1)}, bf16[256,1024]{1,0:T(8,128)(2,1)}) custom-call(s32[1]{0:T(128)} %bitcast.key_ref, bf16[256,1024]{1,0:T(8,128)(2,1)S(1)} %copy-done, bf16[256,1024]{1,0:T(8,128)(2,1)S(1)} %copy-done.1, bf16[4,256,128]{2,1,0:T(8,128)(2,1)S(1)} %get-tuple-element.122.kl_ref, ...), custom_call_target="tpu_custom_call" | custom-call | flops 201326592 | bytes 8257548 | tf_op jit(solution)/shard_map/pallas_call | solution.py:44
  46.7 0.0 collective-permute-done.23.l_ref
  46.7 1.0 %shard_map.84 = (bf16[256,1024]{1,0:T(8,128)(2,1)}, bf16[256,1024]{1,0:T(8,128)(2,1)}) custom-call(s32[1]{0:T(128)} %bitcast.key_ref, bf16[256,1024]{1,0:T(8,128)(2,1)S(1)} %copy-done, bf16[256,1024]{1,0:T(8,128)(2,1)S(1)} %copy-done.1, bf16[4,256,128]{2,1,0:T(8,128)(2,1)S(1)} %get-tuple-element.117.kl_ref, ...), custom_call_target="tpu_custom_call", output_to_operand_aliasing={{0}: (6, {}), {1}: (7, {})} | custom-call | flops 201326592 | bytes 11403276 | tf_op jit(solution)/shard_map/pallas_call | solution.py:44
  (19 shorter events, 0.2 us)
Async XLA Ops:
  2.0 1.5 %collective-permute-start = (bf16[4,128,128]{2,1,0:T(8,128)(2,1)S(1)}, bf16[4,128,128]{2,1,0:T(8,128)(2,1)S(1)}, u32[]{:S(2)}, u32[]{:S(2)}) collective-permute-start(bf16[4,128,128]{2,1,0:T(8,128)(2,1)S(1)} %get-tuple-element.66), channel_id=1, source_target_pairs={{0,1},{1,0},{2,3},{3,2},{4,5},{5,4},{6,7},{7,6},{8,9},{9,8},{10,11... | collective-permute-start | bytes 393224 | tf_op jit(solution)/shard_map/ppermute | solution.py:191
  3.5 6.4 %collective-permute-start.1 = (bf16[128,128]{1,0:T(8,128)(2,1)S(1)}, bf16[128,128]{1,0:T(8,128)(2,1)S(1)}, u32[]{:S(2)}, u32[]{:S(2)}) collective-permute-start(bf16[128,128]{1,0:T(8,128)(2,1)S(1)} %get-tuple-element.136), channel_id=1, source_target_pairs={{0,3},{1,2},{2,1},{3,0},{4,7},{5,6},{6,5},{7,4},{8,11},{9,10},{10,... | collective-permute-start | bytes 98312 | tf_op jit(solution)/shard_map/ppermute | solution.py:191
  6.2 3.9 %collective-permute-start.2 = (bf16[128,128]{1,0:T(8,128)(2,1)S(1)}, bf16[128,128]{1,0:T(8,128)(2,1)S(1)}, u32[]{:S(2)}, u32[]{:S(2)}) collective-permute-start(bf16[128,128]{1,0:T(8,128)(2,1)S(1)} %get-tuple-element.135), channel_id=1, source_target_pairs={{0,4},{1,5},{2,6},{3,7},{4,0},{5,1},{6,2},{7,3},{8,12},{9,13},{10,... | collective-permute-start | bytes 98312 | tf_op jit(solution)/shard_map/ppermute | solution.py:191
  7.8 4.3 %collective-permute-start.3 = (bf16[128,128]{1,0:T(8,128)(2,1)S(1)}, bf16[128,128]{1,0:T(8,128)(2,1)S(1)}, u32[]{:S(2)}, u32[]{:S(2)}) collective-permute-start(bf16[128,128]{1,0:T(8,128)(2,1)S(1)} %get-tuple-element.134), channel_id=1, source_target_pairs={{0,7},{1,6},{2,5},{3,4},{4,3},{5,2},{6,1},{7,0},{8,15},{9,14},{10,... | collective-permute-start | bytes 98312 | tf_op jit(solution)/shard_map/ppermute | solution.py:191
  12.2 6.1 %collective-permute-start.8 = (bf16[128,128]{1,0:T(8,128)(2,1)S(1)}, bf16[128,128]{1,0:T(8,128)(2,1)S(1)}, u32[]{:S(2)}, u32[]{:S(2)}) collective-permute-start(bf16[128,128]{1,0:T(8,128)(2,1)S(1)} %fusion.15), channel_id=1, source_target_pairs={{0,25},{1,24},{2,27},{3,26},{4,29},{5,28},{6,31},{7,30},{8,17},{9,... | collective-permute-start | bytes 98312 | tf_op jit(solution)/shard_map/ppermute | solution.py:191
  15.5 4.9 %collective-permute-start.7 = (bf16[128,128]{1,0:T(8,128)(2,1)S(1)}, bf16[128,128]{1,0:T(8,128)(2,1)S(1)}, u32[]{:S(2)}, u32[]{:S(2)}) collective-permute-start(bf16[128,128]{1,0:T(8,128)(2,1)S(1)} %fusion.15), channel_id=1, source_target_pairs={{0,9},{1,8},{2,11},{3,10},{4,13},{5,12},{6,15},{7,14},{8,1},{9,0},... | collective-permute-start | bytes 98312 | tf_op jit(solution)/shard_map/ppermute | solution.py:191
  15.9 4.6 %collective-permute-start.6 = (bf16[128,128]{1,0:T(8,128)(2,1)S(1)}, bf16[128,128]{1,0:T(8,128)(2,1)S(1)}, u32[]{:S(2)}, u32[]{:S(2)}) collective-permute-start(bf16[128,128]{1,0:T(8,128)(2,1)S(1)} %fusion.15), channel_id=1, source_target_pairs={{0,16},{1,17},{2,18},{3,19},{4,20},{5,21},{6,22},{7,23},{8,24},{9,... | collective-permute-start | bytes 98312 | tf_op jit(solution)/shard_map/ppermute | solution.py:191
  16.3 7.7 %collective-permute-start.4 = (bf16[2,256,512]{2,1,0:T(8,128)(2,1)S(1)}, bf16[2,256,512]{2,1,0:T(8,128)(2,1)S(1)}, u32[]{:S(2)}, u32[]{:S(2)}) collective-permute-start(bf16[2,256,512]{2,1,0:T(8,128)(2,1)S(1)} %get-tuple-element.76.their_qg_ref), channel_id=1, source_target_pairs={{0,1},{1,0},{2,3},{3,2},{4,5},{5,4},{6,7},{7,6},{8,9},{9,8},{10,11... | collective-permute-start | bytes 1572872 | tf_op jit(solution)/shard_map/ppermute | solution.py:191
  16.3 7.7 %collective-permute-start.5 = (f32[4,256,128]{2,1,0:T(8,128)S(1)}, f32[4,256,128]{2,1,0:T(8,128)S(1)}, u32[]{:S(2)}, u32[]{:S(2)}) collective-permute-start(f32[4,256,128]{2,1,0:T(8,128)S(1)} %get-tuple-element.78), channel_id=1, source_target_pairs={{0,1},{1,0},{2,3},{3,2},{4,5},{5,4},{6,7},{7,6},{8,9},{9,8},{10,11... | collective-permute-start | bytes 1572872 | tf_op jit(solution)/shard_map/ppermute | solution.py:191
  20.5 3.5 %collective-permute-start.9 = (bf16[128,128]{1,0:T(8,128)(2,1)S(1)}, bf16[128,128]{1,0:T(8,128)(2,1)S(1)}, u32[]{:S(2)}, u32[]{:S(2)}) collective-permute-start(bf16[128,128]{1,0:T(8,128)(2,1)S(1)} %get-tuple-element.129), channel_id=1, source_target_pairs={{0,3},{1,2},{2,1},{3,0},{4,7},{5,6},{6,5},{7,4},{8,11},{9,10},{10,... | collective-permute-start | bytes 98312 | tf_op jit(solution)/shard_map/ppermute | solution.py:191
  21.0 4.2 %collective-permute-start.11 = (bf16[128,128]{1,0:T(8,128)(2,1)S(1)}, bf16[128,128]{1,0:T(8,128)(2,1)S(1)}, u32[]{:S(2)}, u32[]{:S(2)}) collective-permute-start(bf16[128,128]{1,0:T(8,128)(2,1)S(1)} %get-tuple-element.139), channel_id=1, source_target_pairs={{0,4},{1,5},{2,6},{3,7},{4,0},{5,1},{6,2},{7,3},{8,12},{9,13},{10,... | collective-permute-start | bytes 98312 | tf_op jit(solution)/shard_map/ppermute | solution.py:191
  21.2 4.6 %collective-permute-start.12 = (bf16[128,128]{1,0:T(8,128)(2,1)S(1)}, bf16[128,128]{1,0:T(8,128)(2,1)S(1)}, u32[]{:S(2)}, u32[]{:S(2)}) collective-permute-start(bf16[128,128]{1,0:T(8,128)(2,1)S(1)} %get-tuple-element.128), channel_id=1, source_target_pairs={{0,7},{1,6},{2,5},{3,4},{4,3},{5,2},{6,1},{7,0},{8,15},{9,14},{10,... | collective-permute-start | bytes 98312 | tf_op jit(solution)/shard_map/ppermute | solution.py:191
  24.8 6.1 %collective-permute-start.10 = (bf16[128,128]{1,0:T(8,128)(2,1)S(1)}, bf16[128,128]{1,0:T(8,128)(2,1)S(1)}, u32[]{:S(2)}, u32[]{:S(2)}) collective-permute-start(bf16[128,128]{1,0:T(8,128)(2,1)S(1)} %fusion.39), channel_id=1, source_target_pairs={{0,3},{1,2},{2,1},{3,0},{4,7},{5,6},{6,5},{7,4},{8,11},{9,10},{10,... | collective-permute-start | bytes 98312 | tf_op jit(solution)/shard_map/ppermute | solution.py:191
  25.9 3.1 %copy-start = (bf16[256,1024]{1,0:T(8,128)(2,1)S(1)}, bf16[256,1024]{1,0:T(8,128)(2,1)}, u32[]{:S(2)}) copy-start(bf16[256,1024]{1,0:T(8,128)(2,1)} %k_ref.3) | copy-start | bytes 1572868
  25.9 3.1 %copy-start.1 = (bf16[256,1024]{1,0:T(8,128)(2,1)S(1)}, bf16[256,1024]{1,0:T(8,128)(2,1)}, u32[]{:S(2)}) copy-start(bf16[256,1024]{1,0:T(8,128)(2,1)} %v_ref.3) | copy-start | bytes 1572868
  25.9 3.1 %copy-start.2 = (bf16[256,1024]{1,0:T(8,128)(2,1)S(1)}, bf16[256,1024]{1,0:T(8,128)(2,1)}, u32[]{:S(2)}) copy-start(bf16[256,1024]{1,0:T(8,128)(2,1)} %q_ref.1) | copy-start | bytes 1572868
  26.7 4.2 %collective-permute-start.13 = (bf16[128,128]{1,0:T(8,128)(2,1)S(1)}, bf16[128,128]{1,0:T(8,128)(2,1)S(1)}, u32[]{:S(2)}, u32[]{:S(2)}) collective-permute-start(bf16[128,128]{1,0:T(8,128)(2,1)S(1)} %get-tuple-element.142), channel_id=1, source_target_pairs={{0,4},{1,5},{2,6},{3,7},{4,0},{5,1},{6,2},{7,3},{8,12},{9,13},{10,... | collective-permute-start | bytes 98312 | tf_op jit(solution)/shard_map/ppermute | solution.py:191
  28.3 4.3 %collective-permute-start.14 = (bf16[128,128]{1,0:T(8,128)(2,1)S(1)}, bf16[128,128]{1,0:T(8,128)(2,1)S(1)}, u32[]{:S(2)}, u32[]{:S(2)}) collective-permute-start(bf16[128,128]{1,0:T(8,128)(2,1)S(1)} %get-tuple-element.141), channel_id=1, source_target_pairs={{0,7},{1,6},{2,5},{3,4},{4,3},{5,2},{6,1},{7,0},{8,15},{9,14},{10,... | collective-permute-start | bytes 98312 | tf_op jit(solution)/shard_map/ppermute | solution.py:191
  30.9 1.7 %copy-start.3 = (bf16[128,128]{1,0:T(8,128)(2,1)}, bf16[128,128]{1,0:T(8,128)(2,1)S(1)}, u32[]{:S(2)}) copy-start(bf16[128,128]{1,0:T(8,128)(2,1)S(1)} %collective-permute-done.10) | copy-start | bytes 98308
  32.6 6.6 %collective-permute-start.15 = (bf16[128,128]{1,0:T(8,128)(2,1)S(1)}, bf16[128,128]{1,0:T(8,128)(2,1)S(1)}, u32[]{:S(2)}, u32[]{:S(2)}) collective-permute-start(bf16[128,128]{1,0:T(8,128)(2,1)S(1)} %fusion.29), channel_id=1, source_target_pairs={{0,25},{1,24},{2,27},{3,26},{4,29},{5,28},{6,31},{7,30},{8,17},{9,... | collective-permute-start | bytes 98312 | tf_op jit(solution)/shard_map/ppermute | solution.py:191
  33.9 5.3 %copy-start.4 = (bf16[128,128]{1,0:T(8,128)(2,1)S(1)}, bf16[128,128]{1,0:T(8,128)(2,1)}, u32[]{:S(2)}) copy-start(bf16[128,128]{1,0:T(8,128)(2,1)} %copy-done.3) | copy-start | bytes 98308
  34.0 5.3 %collective-permute-start.16 = (bf16[128,128]{1,0:T(8,128)(2,1)S(1)}, bf16[128,128]{1,0:T(8,128)(2,1)S(1)}, u32[]{:S(2)}, u32[]{:S(2)}) collective-permute-start(bf16[128,128]{1,0:T(8,128)(2,1)S(1)} %fusion.29), channel_id=1, source_target_pairs={{0,9},{1,8},{2,11},{3,10},{4,13},{5,12},{6,15},{7,14},{8,1},{9,0},... | collective-permute-start | bytes 98312 | tf_op jit(solution)/shard_map/ppermute | solution.py:191
  35.3 3.9 %collective-permute-start.17 = (bf16[128,128]{1,0:T(8,128)(2,1)S(1)}, bf16[128,128]{1,0:T(8,128)(2,1)S(1)}, u32[]{:S(2)}, u32[]{:S(2)}) collective-permute-start(bf16[128,128]{1,0:T(8,128)(2,1)S(1)} %fusion.29), channel_id=1, source_target_pairs={{0,16},{1,17},{2,18},{3,19},{4,20},{5,21},{6,22},{7,23},{8,24},{9,... | collective-permute-start | bytes 98312 | tf_op jit(solution)/shard_map/ppermute | solution.py:191
  36.8 5.7 %collective-permute-start.21 = (bf16[2,640,128]{2,1,0:T(8,128)(2,1)S(1)}, bf16[2,640,128]{2,1,0:T(8,128)(2,1)S(1)}, u32[]{:S(2)}, u32[]{:S(2)}) collective-permute-start(bf16[2,640,128]{2,1,0:T(8,128)(2,1)S(1)} %get-tuple-element.108), channel_id=1, source_target_pairs={{0,1},{1,0},{2,3},{3,2},{4,5},{5,4},{6,7},{7,6},{8,9},{9,8},{10,11... | collective-permute-start | bytes 983048 | tf_op jit(solution)/shard_map/ppermute | solution.py:191
  36.8 5.7 %collective-permute-start.22 = (bf16[2,640,128]{2,1,0:T(8,128)(2,1)S(1)}, bf16[2,640,128]{2,1,0:T(8,128)(2,1)S(1)}, u32[]{:S(2)}, u32[]{:S(2)}) collective-permute-start(bf16[2,640,128]{2,1,0:T(8,128)(2,1)S(1)} %get-tuple-element.110), channel_id=1, source_target_pairs={{0,1},{1,0},{2,3},{3,2},{4,5},{5,4},{6,7},{7,6},{8,9},{9,8},{10,11... | collective-permute-start | bytes 983048 | tf_op jit(solution)/shard_map/ppermute | solution.py:191
  39.3 5.0 %collective-permute-start.18 = (bf16[128,128]{1,0:T(8,128)(2,1)S(1)}, bf16[128,128]{1,0:T(8,128)(2,1)S(1)}, u32[]{:S(2)}, u32[]{:S(2)}) collective-permute-start(bf16[128,128]{1,0:T(8,128)(2,1)S(1)} %get-tuple-element.133), channel_id=1, source_target_pairs={{0,3},{1,2},{2,1},{3,0},{4,7},{5,6},{6,5},{7,4},{8,11},{9,10},{10,... | collective-permute-start | bytes 98312 | tf_op jit(solution)/shard_map/ppermute | solution.py:191
  40.5 4.0 %collective-permute-start.19 = (bf16[128,128]{1,0:T(8,128)(2,1)S(1)}, bf16[128,128]{1,0:T(8,128)(2,1)S(1)}, u32[]{:S(2)}, u32[]{:S(2)}) collective-permute-start(bf16[128,128]{1,0:T(8,128)(2,1)S(1)} %get-tuple-element.138), channel_id=1, source_target_pairs={{0,4},{1,5},{2,6},{3,7},{4,0},{5,1},{6,2},{7,3},{8,12},{9,13},{10,... | collective-permute-start | bytes 98312 | tf_op jit(solution)/shard_map/ppermute | solution.py:191
  40.6 4.3 %collective-permute-start.20 = (bf16[128,128]{1,0:T(8,128)(2,1)S(1)}, bf16[128,128]{1,0:T(8,128)(2,1)S(1)}, u32[]{:S(2)}, u32[]{:S(2)}) collective-permute-start(bf16[128,128]{1,0:T(8,128)(2,1)S(1)} %get-tuple-element.132), channel_id=1, source_target_pairs={{0,7},{1,6},{2,5},{3,4},{4,3},{5,2},{6,1},{7,0},{8,15},{9,14},{10,... | collective-permute-start | bytes 98312 | tf_op jit(solution)/shard_map/ppermute | solution.py:191
  45.0 1.7 %collective-permute-start.23 = (bf16[4,128,128]{2,1,0:T(8,128)(2,1)S(1)}, bf16[4,128,128]{2,1,0:T(8,128)(2,1)S(1)}, u32[]{:S(2)}, u32[]{:S(2)}) collective-permute-start(bf16[4,128,128]{2,1,0:T(8,128)(2,1)S(1)} %get-tuple-element.131), channel_id=1, source_target_pairs={{0,1},{1,0},{2,3},{3,2},{4,5},{5,4},{6,7},{7,6},{8,9},{9,8},{10,11... | collective-permute-start | bytes 393224 | tf_op jit(solution)/shard_map/ppermute | solution.py:191

commit v8 on v7

--- a/solution.py
+++ b/solution.py
@@ -352,7 +352,7 @@
         own_back += [state[i] for i in range(len(group))]
         core_back += [their_state[i] for i in range(len(group))]
 
-    late_q, late_k, late_v = tie_to((query_rows, key_rows, value_rows), mixed)
+    late_q, late_k, late_v = tie_to((query_rows, key_rows, value_rows), inner[1][2])
 
     def grads(base, key, parts, outs):
         per_group = len(parts[0])

time: 47.9 us -> 47.9 us (level)
  no operation moved by 1% of the time
where the time goes in v8:
time: 47.9 us; the launch traced here: 47.8 us
  starting transfers between devices  23.6 us (49%)
  waiting for transfers between devices  11.6 us (24%)
  Pallas kernels  11.1 us (23%)
  between operations  0.9 us (2%)
  other arithmetic  0.57 us (1%)
    ppermute x24, starting transfers between devices, swap(): return lax.ppermute(array, AXES, [(i, i ^ mask) for i in range(count)])  23.6 us
    ppermute x24, waiting for transfers between devices, swap(): return lax.ppermute(array, AXES, [(i, i ^ mask) for i in range(count)])  11.6 us
    pallas_call x10, Pallas kernels, call(): pl.pallas_call(kernel, out_shape=shapes, in_specs=specs, out_specs=[hbm i...  11.1 us
  transfers between devices with their start and end apart: 24, of which 11 were waited for; matrix products, arithmetic and copies ran while one was open for 1% of the time, Pallas kernels for 18%

profile of v8, /device:TPU:0, one launch (start us, length us, event | category | flops | bytes accessed | tf_op | source)
XLA Modules:
  0.0 47.8 jit_solution(8419717105212233449)
XLA Ops:
  0.6 1.3 %shard_map.75 = (bf16[4,128,128]{2,1,0:T(8,128)(2,1)S(1)}, bf16[2,256,512]{2,1,0:T(8,128)(2,1)S(1)}, bf16[2,256,512]{2,1,0:T(8,128)(2,1)S(1)}) custom-call(s32[1]{0:T(128)} %bitcast.key_ref, bf16[256,1024]{1,0:T(8,128)(2,1)} %k_ref.3, bf16[256,1024]{1,0:T(8,128)(2,1)} %v_ref.3), custom_call_target="tpu_custom_call" | custom-call | flops 100663296 | bytes 6684684 | tf_op jit(solution)/shard_map/pallas_call | solution.py:44
  2.0 0.5 %collective-permute-start = (bf16[4,128,128]{2,1,0:T(8,128)(2,1)S(1)}, bf16[4,128,128]{2,1,0:T(8,128)(2,1)S(1)}, u32[]{:S(2)}, u32[]{:S(2)}) collective-permute-start(bf16[4,128,128]{2,1,0:T(8,128)(2,1)S(1)} %get-tuple-element.66), channel_id=1, source_target_pairs={{0,1},{1,0},{2,3},{3,2},{4,5},{5,4},{6,7},{7,6},{8,9},{9,8},{10,11... | collective-permute-start | bytes 393224 | tf_op jit(solution)/shard_map/ppermute | solution.py:191
  2.5 0.3 shard_map.76
  2.8 0.7 %collective-permute-done = bf16[4,128,128]{2,1,0:T(8,128)(2,1)S(1)} collective-permute-done((bf16[4,128,128]{2,1,0:T(8,128)(2,1)S(1)}, bf16[4,128,128]{2,1,0:T(8,128)(2,1)S(1)}, u32[]{:S(2)}, u32[]{:S(2)}) %collective-permute-start) | collective-permute-done | bytes 131104 | tf_op jit(solution)/shard_map/ppermute | solution.py:191
  3.5 2.7 %collective-permute-start.1 = (bf16[128,128]{1,0:T(8,128)(2,1)S(1)}, bf16[128,128]{1,0:T(8,128)(2,1)S(1)}, u32[]{:S(2)}, u32[]{:S(2)}) collective-permute-start(bf16[128,128]{1,0:T(8,128)(2,1)S(1)} %get-tuple-element.136), channel_id=1, source_target_pairs={{0,3},{1,2},{2,1},{3,0},{4,7},{5,6},{6,5},{7,4},{8,11},{9,10},{10,... | collective-permute-start | bytes 98312 | tf_op jit(solution)/shard_map/ppermute | solution.py:191
  6.2 1.6 %collective-permute-start.2 = (bf16[128,128]{1,0:T(8,128)(2,1)S(1)}, bf16[128,128]{1,0:T(8,128)(2,1)S(1)}, u32[]{:S(2)}, u32[]{:S(2)}) collective-permute-start(bf16[128,128]{1,0:T(8,128)(2,1)S(1)} %get-tuple-element.135), channel_id=1, source_target_pairs={{0,4},{1,5},{2,6},{3,7},{4,0},{5,1},{6,2},{7,3},{8,12},{9,13},{10,... | collective-permute-start | bytes 98312 | tf_op jit(solution)/shard_map/ppermute | solution.py:191
  7.8 0.0 collective-permute-start.3
  7.8 1.2 %shard_map.77 = (bf16[2,256,512]{2,1,0:T(8,128)(2,1)S(1)}, bf16[2,256,512]{2,1,0:T(8,128)(2,1)S(1)}) custom-call(s32[1]{0:T(128)} %bitcast.key_ref, bf16[256,1024]{1,0:T(8,128)(2,1)} %q_ref.1, bf16[256,1024]{1,0:T(8,128)(2,1)} %g_hbm.1), custom_call_target="tpu_custom_call" | custom-call | bytes 6291468 | tf_op jit(solution)/shard_map/pallas_call | solution.py:44
  9.0 0.9 %shard_map.78 = (f32[4,256,128]{2,1,0:T(8,128)S(1)}, f32[4,256,128]{2,1,0:T(8,128)S(1)}) custom-call(s32[1]{0:T(128)} %bitcast.key_ref, bf16[2,256,512]{2,1,0:T(8,128)(2,1)S(1)} %get-tuple-element.68.kv_ref, bf16[2,256,512]{2,1,0:T(8,128)(2,1)S(1)} %get-tuple-element.75.qg_ref, bf16[2,256,512]{2,1,0:T(8,128)(2,1)S(1)} %get-tuple-element.71.their_kv_ref, ...), custom_call_target="tpu_custom_call" | custom-call | flops 805306368 | bytes 9437196 | tf_op jit(solution)/shard_map/pallas_call | solution.py:44
  10.0 0.0 collective-permute-done.1
  10.0 0.2 collective-permute-done.2
  10.1 2.0 %collective-permute-done.3 = bf16[128,128]{1,0:T(8,128)(2,1)S(1)} collective-permute-done((bf16[128,128]{1,0:T(8,128)(2,1)S(1)}, bf16[128,128]{1,0:T(8,128)(2,1)S(1)}, u32[]{:S(2)}, u32[]{:S(2)}) %collective-permute-start.3) | collective-permute-done | bytes 32800 | tf_op jit(solution)/shard_map/ppermute | solution.py:191
  12.2 3.3 %collective-permute-start.8 = (bf16[128,128]{1,0:T(8,128)(2,1)S(1)}, bf16[128,128]{1,0:T(8,128)(2,1)S(1)}, u32[]{:S(2)}, u32[]{:S(2)}) collective-permute-start(bf16[128,128]{1,0:T(8,128)(2,1)S(1)} %fusion.15), channel_id=1, source_target_pairs={{0,25},{1,24},{2,27},{3,26},{4,29},{5,28},{6,31},{7,30},{8,17},{9,... | collective-permute-start | bytes 98312 | tf_op jit(solution)/shard_map/ppermute | solution.py:191
  15.5 0.4 collective-permute-start.7
  15.9 0.5 collective-permute-start.6
  16.3 0.0 collective-permute-start.4
  16.3 0.5 %collective-permute-start.5 = (f32[4,256,128]{2,1,0:T(8,128)S(1)}, f32[4,256,128]{2,1,0:T(8,128)S(1)}, u32[]{:S(2)}, u32[]{:S(2)}) collective-permute-start(f32[4,256,128]{2,1,0:T(8,128)S(1)} %get-tuple-element.78), channel_id=1, source_target_pairs={{0,1},{1,0},{2,3},{3,2},{4,5},{5,4},{6,7},{7,6},{8,9},{9,8},{10,11... | collective-permute-start | bytes 1572872 | tf_op jit(solution)/shard_map/ppermute | solution.py:191
  16.8 1.4 %collective-permute-done.8 = bf16[128,128]{1,0:T(8,128)(2,1)S(1)} collective-permute-done((bf16[128,128]{1,0:T(8,128)(2,1)S(1)}, bf16[128,128]{1,0:T(8,128)(2,1)S(1)}, u32[]{:S(2)}, u32[]{:S(2)}) %collective-permute-start.8) | collective-permute-done | bytes 32800 | tf_op jit(solution)/shard_map/ppermute | solution.py:191
  18.3 2.1 %collective-permute-done.7 = bf16[128,128]{1,0:T(8,128)(2,1)S(1)} collective-permute-done((bf16[128,128]{1,0:T(8,128)(2,1)S(1)}, bf16[128,128]{1,0:T(8,128)(2,1)S(1)}, u32[]{:S(2)}, u32[]{:S(2)}) %collective-permute-start.7) | collective-permute-done | bytes 32800 | tf_op jit(solution)/shard_map/ppermute | solution.py:191
  20.4 0.0 collective-permute-done.6
  20.4 0.1 fusion.11
  20.5 0.4 collective-permute-start.9
  20.9 0.1 fusion.8
  21.0 0.3 collective-permute-start.11
  21.2 2.4 %collective-permute-start.12 = (bf16[128,128]{1,0:T(8,128)(2,1)S(1)}, bf16[128,128]{1,0:T(8,128)(2,1)S(1)}, u32[]{:S(2)}, u32[]{:S(2)}) collective-permute-start(bf16[128,128]{1,0:T(8,128)(2,1)S(1)} %get-tuple-element.128), channel_id=1, source_target_pairs={{0,7},{1,6},{2,5},{3,4},{4,3},{5,2},{6,1},{7,0},{8,15},{9,14},{10,... | collective-permute-start | bytes 98312 | tf_op jit(solution)/shard_map/ppermute | solution.py:191
  23.6 0.3 collective-permute-done.9
  24.0 0.0 collective-permute-done.4.their_qg_ref
  24.0 0.0 collective-permute-done.5.their_mixed_ref
  24.0 0.7 %shard_map.79 = (bf16[2,256,128]{2,1,0:T(8,128)(2,1)S(1)}, bf16[2,256,128]{2,1,0:T(8,128)(2,1)S(1)}, bf16[2,128,128]{2,1,0:T(8,128)(2,1)S(1)}, bf16[2,640,128]{2,1,0:T(8,128)(2,1)S(1)}, bf16[2,128,128]{2,1,0:T(8,128)(2,1)S(1)}) custom-call(s32[1]{0:T(128)} %bitcast.key_ref, bf16[2,256,512]{2,1,0:T(8,128)(2,1)S(1)} %get-tuple-element.75.qg_ref, ...), custom_call_target="tpu_custom_call" | custom-call | flops 100663296 | bytes 8847372 | tf_op jit(solution)/shard_map/pallas_call | solution.py:44
  24.8 0.4 collective-permute-start.10
  25.1 0.0 collective-permute-done.11
  25.1 0.7 %collective-permute-done.12 = bf16[128,128]{1,0:T(8,128)(2,1)S(1)} collective-permute-done((bf16[128,128]{1,0:T(8,128)(2,1)S(1)}, bf16[128,128]{1,0:T(8,128)(2,1)S(1)}, u32[]{:S(2)}, u32[]{:S(2)}) %collective-permute-start.12) | collective-permute-done | bytes 32800 | tf_op jit(solution)/shard_map/ppermute | solution.py:191
  25.9 0.0 copy-start
  25.9 0.0 copy-start.1
  25.9 0.0 copy-start.2
  25.9 0.7 %shard_map.80 = (bf16[2,256,128]{2,1,0:T(8,128)(2,1)S(1)}, bf16[2,256,128]{2,1,0:T(8,128)(2,1)S(1)}, bf16[2,128,128]{2,1,0:T(8,128)(2,1)S(1)}, bf16[2,640,128]{2,1,0:T(8,128)(2,1)S(1)}, bf16[2,128,128]{2,1,0:T(8,128)(2,1)S(1)}) custom-call(s32[1]{0:T(128)} %bitcast.key_ref, bf16[2,256,512]{2,1,0:T(8,128)(2,1)S(1)} %get-tuple-element.75.qg_ref, ...), custom_call_target="tpu_custom_call" | custom-call | flops 100663296 | bytes 8847372 | tf_op jit(solution)/shard_map/pallas_call | solution.py:44
  26.7 1.6 %collective-permute-start.13 = (bf16[128,128]{1,0:T(8,128)(2,1)S(1)}, bf16[128,128]{1,0:T(8,128)(2,1)S(1)}, u32[]{:S(2)}, u32[]{:S(2)}) collective-permute-start(bf16[128,128]{1,0:T(8,128)(2,1)S(1)} %get-tuple-element.142), channel_id=1, source_target_pairs={{0,4},{1,5},{2,6},{3,7},{4,0},{5,1},{6,2},{7,3},{8,12},{9,13},{10,... | collective-permute-start | bytes 98312 | tf_op jit(solution)/shard_map/ppermute | solution.py:191
  28.3 0.7 %collective-permute-start.14 = (bf16[128,128]{1,0:T(8,128)(2,1)S(1)}, bf16[128,128]{1,0:T(8,128)(2,1)S(1)}, u32[]{:S(2)}, u32[]{:S(2)}) collective-permute-start(bf16[128,128]{1,0:T(8,128)(2,1)S(1)} %get-tuple-element.141), channel_id=1, source_target_pairs={{0,7},{1,6},{2,5},{3,4},{4,3},{5,2},{6,1},{7,0},{8,15},{9,14},{10,... | collective-permute-start | bytes 98312 | tf_op jit(solution)/shard_map/ppermute | solution.py:191
  29.0 1.9 %shard_map.81 = (bf16[256,1024]{1,0:T(8,128)(2,1)}, bf16[256,1024]{1,0:T(8,128)(2,1)}, bf16[4,256,128]{2,1,0:T(8,128)(2,1)S(1)}, bf16[4,256,128]{2,1,0:T(8,128)(2,1)S(1)}) custom-call(s32[1]{0:T(128)} %bitcast.key_ref, bf16[256,1024]{1,0:T(8,128)(2,1)S(1)} %copy-done.2, bf16[256,1024]{1,0:T(8,128)(2,1)S(1)} %copy-done, bf16[256,1024]{1,0:T(8,128)(2,1)S(1)} %copy-done.1, ...), custom_call_target="tpu_custom_call" | custom-call | flops 905969664 | bytes 11403276 | tf_op jit(solution)/shard_map/pallas_call | solution.py:44
  30.8 0.0 collective-permute-done.10
  30.9 0.0 copy-start.3
  30.9 1.7 %collective-permute-done.14 = bf16[128,128]{1,0:T(8,128)(2,1)S(1)} collective-permute-done((bf16[128,128]{1,0:T(8,128)(2,1)S(1)}, bf16[128,128]{1,0:T(8,128)(2,1)S(1)}, u32[]{:S(2)}, u32[]{:S(2)}) %collective-permute-start.14) | collective-permute-done | bytes 32800 | tf_op jit(solution)/shard_map/ppermute | solution.py:191
  32.6 1.3 %collective-permute-start.15 = (bf16[128,128]{1,0:T(8,128)(2,1)S(1)}, bf16[128,128]{1,0:T(8,128)(2,1)S(1)}, u32[]{:S(2)}, u32[]{:S(2)}) collective-permute-start(bf16[128,128]{1,0:T(8,128)(2,1)S(1)} %fusion.29), channel_id=1, source_target_pairs={{0,25},{1,24},{2,27},{3,26},{4,29},{5,28},{6,31},{7,30},{8,17},{9,... | collective-permute-start | bytes 98312 | tf_op jit(solution)/shard_map/ppermute | solution.py:191
  34.0 1.3 %collective-permute-start.16 = (bf16[128,128]{1,0:T(8,128)(2,1)S(1)}, bf16[128,128]{1,0:T(8,128)(2,1)S(1)}, u32[]{:S(2)}, u32[]{:S(2)}) collective-permute-start(bf16[128,128]{1,0:T(8,128)(2,1)S(1)} %fusion.29), channel_id=1, source_target_pairs={{0,9},{1,8},{2,11},{3,10},{4,13},{5,12},{6,15},{7,14},{8,1},{9,0},... | collective-permute-start | bytes 98312 | tf_op jit(solution)/shard_map/ppermute | solution.py:191
  35.3 1.5 %collective-permute-start.17 = (bf16[128,128]{1,0:T(8,128)(2,1)S(1)}, bf16[128,128]{1,0:T(8,128)(2,1)S(1)}, u32[]{:S(2)}, u32[]{:S(2)}) collective-permute-start(bf16[128,128]{1,0:T(8,128)(2,1)S(1)} %fusion.29), channel_id=1, source_target_pairs={{0,16},{1,17},{2,18},{3,19},{4,20},{5,21},{6,22},{7,23},{8,24},{9,... | collective-permute-start | bytes 98312 | tf_op jit(solution)/shard_map/ppermute | solution.py:191
  36.8 0.0 collective-permute-start.21
  36.8 0.5 %collective-permute-start.22 = (bf16[2,640,128]{2,1,0:T(8,128)(2,1)S(1)}, bf16[2,640,128]{2,1,0:T(8,128)(2,1)S(1)}, u32[]{:S(2)}, u32[]{:S(2)}) collective-permute-start(bf16[2,640,128]{2,1,0:T(8,128)(2,1)S(1)} %get-tuple-element.110), channel_id=1, source_target_pairs={{0,1},{1,0},{2,3},{3,2},{4,5},{5,4},{6,7},{7,6},{8,9},{9,8},{10,11... | collective-permute-start | bytes 983048 | tf_op jit(solution)/shard_map/ppermute | solution.py:191
  37.3 1.9 %collective-permute-done.15 = bf16[128,128]{1,0:T(8,128)(2,1)S(1)} collective-permute-done((bf16[128,128]{1,0:T(8,128)(2,1)S(1)}, bf16[128,128]{1,0:T(8,128)(2,1)S(1)}, u32[]{:S(2)}, u32[]{:S(2)}) %collective-permute-start.15) | collective-permute-done | bytes 32800 | tf_op jit(solution)/shard_map/ppermute | solution.py:191
  39.2 0.1 fusion.21
  39.3 1.2 %collective-permute-start.18 = (bf16[128,128]{1,0:T(8,128)(2,1)S(1)}, bf16[128,128]{1,0:T(8,128)(2,1)S(1)}, u32[]{:S(2)}, u32[]{:S(2)}) collective-permute-start(bf16[128,128]{1,0:T(8,128)(2,1)S(1)} %get-tuple-element.133), channel_id=1, source_target_pairs={{0,3},{1,2},{2,1},{3,0},{4,7},{5,6},{6,5},{7,4},{8,11},{9,10},{10,... | collective-permute-start | bytes 98312 | tf_op jit(solution)/shard_map/ppermute | solution.py:191
  40.4 0.1 fusion.25
  40.5 0.1 collective-permute-start.19
  40.6 1.9 %collective-permute-start.20 = (bf16[128,128]{1,0:T(8,128)(2,1)S(1)}, bf16[128,128]{1,0:T(8,128)(2,1)S(1)}, u32[]{:S(2)}, u32[]{:S(2)}) collective-permute-start(bf16[128,128]{1,0:T(8,128)(2,1)S(1)} %get-tuple-element.132), channel_id=1, source_target_pairs={{0,7},{1,6},{2,5},{3,4},{4,3},{5,2},{6,1},{7,0},{8,15},{9,14},{10,... | collective-permute-start | bytes 98312 | tf_op jit(solution)/shard_map/ppermute | solution.py:191
  42.5 0.0 collective-permute-done.21.refs_0_
  42.5 0.0 collective-permute-done.22.refs_1_
  42.5 1.9 %shard_map.82 = (bf16[256,1024]{1,0:T(8,128)(2,1)}, bf16[256,1024]{1,0:T(8,128)(2,1)}, bf16[4,256,128]{2,1,0:T(8,128)(2,1)S(1)}, bf16[4,256,128]{2,1,0:T(8,128)(2,1)S(1)}) custom-call(s32[1]{0:T(128)} %bitcast.key_ref, bf16[256,1024]{1,0:T(8,128)(2,1)S(1)} %copy-done.2, bf16[256,1024]{1,0:T(8,128)(2,1)S(1)} %copy-done, ...), custom_call_target="tpu_custom_call", output_to_operand_aliasing={{0}: (6, {}), {1}: (7, {})} | custom-call | flops 905969664 | bytes 14549004 | tf_op jit(solution)/shard_map/pallas_call | solution.py:44
  44.3 0.0 collective-permute-done.18
  44.3 0.2 collective-permute-done.19
  44.5 0.4 collective-permute-done.20
  45.0 0.1 add_convert_fusion
  45.0 0.6 %collective-permute-start.23 = (bf16[4,128,128]{2,1,0:T(8,128)(2,1)S(1)}, bf16[4,128,128]{2,1,0:T(8,128)(2,1)S(1)}, u32[]{:S(2)}, u32[]{:S(2)}) collective-permute-start(bf16[4,128,128]{2,1,0:T(8,128)(2,1)S(1)} %get-tuple-element.131), channel_id=1, source_target_pairs={{0,1},{1,0},{2,3},{3,2},{4,5},{5,4},{6,7},{7,6},{8,9},{9,8},{10,11... | collective-permute-start | bytes 393224 | tf_op jit(solution)/shard_map/ppermute | solution.py:191
  45.7 1.0 %shard_map.83 = (bf16[256,1024]{1,0:T(8,128)(2,1)}, bf16[256,1024]{1,0:T(8,128)(2,1)}) custom-call(s32[1]{0:T(128)} %bitcast.key_ref, bf16[256,1024]{1,0:T(8,128)(2,1)S(1)} %copy-done, bf16[256,1024]{1,0:T(8,128)(2,1)S(1)} %copy-done.1, bf16[4,256,128]{2,1,0:T(8,128)(2,1)S(1)} %get-tuple-element.122.kl_ref, ...), custom_call_target="tpu_custom_call" | custom-call | flops 201326592 | bytes 8257548 | tf_op jit(solution)/shard_map/pallas_call | solution.py:44
  46.7 0.0 collective-permute-done.23.l_ref
  46.7 1.0 %shard_map.84 = (bf16[256,1024]{1,0:T(8,128)(2,1)}, bf16[256,1024]{1,0:T(8,128)(2,1)}) custom-call(s32[1]{0:T(128)} %bitcast.key_ref, bf16[256,1024]{1,0:T(8,128)(2,1)S(1)} %copy-done, bf16[256,1024]{1,0:T(8,128)(2,1)S(1)} %copy-done.1, bf16[4,256,128]{2,1,0:T(8,128)(2,1)S(1)} %get-tuple-element.117.kl_ref, ...), custom_call_target="tpu_custom_call", output_to_operand_aliasing={{0}: (6, {}), {1}: (7, {})} | custom-call | flops 201326592 | bytes 11403276 | tf_op jit(solution)/shard_map/pallas_call | solution.py:44
  (19 shorter events, 0.2 us)
Async XLA Ops:
  2.0 1.5 %collective-permute-start = (bf16[4,128,128]{2,1,0:T(8,128)(2,1)S(1)}, bf16[4,128,128]{2,1,0:T(8,128)(2,1)S(1)}, u32[]{:S(2)}, u32[]{:S(2)}) collective-permute-start(bf16[4,128,128]{2,1,0:T(8,128)(2,1)S(1)} %get-tuple-element.66), channel_id=1, source_target_pairs={{0,1},{1,0},{2,3},{3,2},{4,5},{5,4},{6,7},{7,6},{8,9},{9,8},{10,11... | collective-permute-start | bytes 393224 | tf_op jit(solution)/shard_map/ppermute | solution.py:191
  3.5 6.4 %collective-permute-start.1 = (bf16[128,128]{1,0:T(8,128)(2,1)S(1)}, bf16[128,128]{1,0:T(8,128)(2,1)S(1)}, u32[]{:S(2)}, u32[]{:S(2)}) collective-permute-start(bf16[128,128]{1,0:T(8,128)(2,1)S(1)} %get-tuple-element.136), channel_id=1, source_target_pairs={{0,3},{1,2},{2,1},{3,0},{4,7},{5,6},{6,5},{7,4},{8,11},{9,10},{10,... | collective-permute-start | bytes 98312 | tf_op jit(solution)/shard_map/ppermute | solution.py:191
  6.2 3.9 %collective-permute-start.2 = (bf16[128,128]{1,0:T(8,128)(2,1)S(1)}, bf16[128,128]{1,0:T(8,128)(2,1)S(1)}, u32[]{:S(2)}, u32[]{:S(2)}) collective-permute-start(bf16[128,128]{1,0:T(8,128)(2,1)S(1)} %get-tuple-element.135), channel_id=1, source_target_pairs={{0,4},{1,5},{2,6},{3,7},{4,0},{5,1},{6,2},{7,3},{8,12},{9,13},{10,... | collective-permute-start | bytes 98312 | tf_op jit(solution)/shard_map/ppermute | solution.py:191
  7.8 4.3 %collective-permute-start.3 = (bf16[128,128]{1,0:T(8,128)(2,1)S(1)}, bf16[128,128]{1,0:T(8,128)(2,1)S(1)}, u32[]{:S(2)}, u32[]{:S(2)}) collective-permute-start(bf16[128,128]{1,0:T(8,128)(2,1)S(1)} %get-tuple-element.134), channel_id=1, source_target_pairs={{0,7},{1,6},{2,5},{3,4},{4,3},{5,2},{6,1},{7,0},{8,15},{9,14},{10,... | collective-permute-start | bytes 98312 | tf_op jit(solution)/shard_map/ppermute | solution.py:191
  12.2 6.1 %collective-permute-start.8 = (bf16[128,128]{1,0:T(8,128)(2,1)S(1)}, bf16[128,128]{1,0:T(8,128)(2,1)S(1)}, u32[]{:S(2)}, u32[]{:S(2)}) collective-permute-start(bf16[128,128]{1,0:T(8,128)(2,1)S(1)} %fusion.15), channel_id=1, source_target_pairs={{0,25},{1,24},{2,27},{3,26},{4,29},{5,28},{6,31},{7,30},{8,17},{9,... | collective-permute-start | bytes 98312 | tf_op jit(solution)/shard_map/ppermute | solution.py:191
  15.5 4.9 %collective-permute-start.7 = (bf16[128,128]{1,0:T(8,128)(2,1)S(1)}, bf16[128,128]{1,0:T(8,128)(2,1)S(1)}, u32[]{:S(2)}, u32[]{:S(2)}) collective-permute-start(bf16[128,128]{1,0:T(8,128)(2,1)S(1)} %fusion.15), channel_id=1, source_target_pairs={{0,9},{1,8},{2,11},{3,10},{4,13},{5,12},{6,15},{7,14},{8,1},{9,0},... | collective-permute-start | bytes 98312 | tf_op jit(solution)/shard_map/ppermute | solution.py:191
  15.9 4.6 %collective-permute-start.6 = (bf16[128,128]{1,0:T(8,128)(2,1)S(1)}, bf16[128,128]{1,0:T(8,128)(2,1)S(1)}, u32[]{:S(2)}, u32[]{:S(2)}) collective-permute-start(bf16[128,128]{1,0:T(8,128)(2,1)S(1)} %fusion.15), channel_id=1, source_target_pairs={{0,16},{1,17},{2,18},{3,19},{4,20},{5,21},{6,22},{7,23},{8,24},{9,... | collective-permute-start | bytes 98312 | tf_op jit(solution)/shard_map/ppermute | solution.py:191
  16.3 7.7 %collective-permute-start.4 = (bf16[2,256,512]{2,1,0:T(8,128)(2,1)S(1)}, bf16[2,256,512]{2,1,0:T(8,128)(2,1)S(1)}, u32[]{:S(2)}, u32[]{:S(2)}) collective-permute-start(bf16[2,256,512]{2,1,0:T(8,128)(2,1)S(1)} %get-tuple-element.76.their_qg_ref), channel_id=1, source_target_pairs={{0,1},{1,0},{2,3},{3,2},{4,5},{5,4},{6,7},{7,6},{8,9},{9,8},{10,11... | collective-permute-start | bytes 1572872 | tf_op jit(solution)/shard_map/ppermute | solution.py:191
  16.3 7.7 %collective-permute-start.5 = (f32[4,256,128]{2,1,0:T(8,128)S(1)}, f32[4,256,128]{2,1,0:T(8,128)S(1)}, u32[]{:S(2)}, u32[]{:S(2)}) collective-permute-start(f32[4,256,128]{2,1,0:T(8,128)S(1)} %get-tuple-element.78), channel_id=1, source_target_pairs={{0,1},{1,0},{2,3},{3,2},{4,5},{5,4},{6,7},{7,6},{8,9},{9,8},{10,11... | collective-permute-start | bytes 1572872 | tf_op jit(solution)/shard_map/ppermute | solution.py:191
  20.5 3.5 %collective-permute-start.9 = (bf16[128,128]{1,0:T(8,128)(2,1)S(1)}, bf16[128,128]{1,0:T(8,128)(2,1)S(1)}, u32[]{:S(2)}, u32[]{:S(2)}) collective-permute-start(bf16[128,128]{1,0:T(8,128)(2,1)S(1)} %get-tuple-element.129), channel_id=1, source_target_pairs={{0,3},{1,2},{2,1},{3,0},{4,7},{5,6},{6,5},{7,4},{8,11},{9,10},{10,... | collective-permute-start | bytes 98312 | tf_op jit(solution)/shard_map/ppermute | solution.py:191
  21.0 4.2 %collective-permute-start.11 = (bf16[128,128]{1,0:T(8,128)(2,1)S(1)}, bf16[128,128]{1,0:T(8,128)(2,1)S(1)}, u32[]{:S(2)}, u32[]{:S(2)}) collective-permute-start(bf16[128,128]{1,0:T(8,128)(2,1)S(1)} %get-tuple-element.139), channel_id=1, source_target_pairs={{0,4},{1,5},{2,6},{3,7},{4,0},{5,1},{6,2},{7,3},{8,12},{9,13},{10,... | collective-permute-start | bytes 98312 | tf_op jit(solution)/shard_map/ppermute | solution.py:191
  21.2 4.6 %collective-permute-start.12 = (bf16[128,128]{1,0:T(8,128)(2,1)S(1)}, bf16[128,128]{1,0:T(8,128)(2,1)S(1)}, u32[]{:S(2)}, u32[]{:S(2)}) collective-permute-start(bf16[128,128]{1,0:T(8,128)(2,1)S(1)} %get-tuple-element.128), channel_id=1, source_target_pairs={{0,7},{1,6},{2,5},{3,4},{4,3},{5,2},{6,1},{7,0},{8,15},{9,14},{10,... | collective-permute-start | bytes 98312 | tf_op jit(solution)/shard_map/ppermute | solution.py:191
  24.8 6.1 %collective-permute-start.10 = (bf16[128,128]{1,0:T(8,128)(2,1)S(1)}, bf16[128,128]{1,0:T(8,128)(2,1)S(1)}, u32[]{:S(2)}, u32[]{:S(2)}) collective-permute-start(bf16[128,128]{1,0:T(8,128)(2,1)S(1)} %fusion.39), channel_id=1, source_target_pairs={{0,3},{1,2},{2,1},{3,0},{4,7},{5,6},{6,5},{7,4},{8,11},{9,10},{10,... | collective-permute-start | bytes 98312 | tf_op jit(solution)/shard_map/ppermute | solution.py:191
  25.9 3.1 %copy-start = (bf16[256,1024]{1,0:T(8,128)(2,1)S(1)}, bf16[256,1024]{1,0:T(8,128)(2,1)}, u32[]{:S(2)}) copy-start(bf16[256,1024]{1,0:T(8,128)(2,1)} %k_ref.3) | copy-start | bytes 1572868
  25.9 3.1 %copy-start.1 = (bf16[256,1024]{1,0:T(8,128)(2,1)S(1)}, bf16[256,1024]{1,0:T(8,128)(2,1)}, u32[]{:S(2)}) copy-start(bf16[256,1024]{1,0:T(8,128)(2,1)} %v_ref.3) | copy-start | bytes 1572868
  25.9 3.1 %copy-start.2 = (bf16[256,1024]{1,0:T(8,128)(2,1)S(1)}, bf16[256,1024]{1,0:T(8,128)(2,1)}, u32[]{:S(2)}) copy-start(bf16[256,1024]{1,0:T(8,128)(2,1)} %q_ref.1) | copy-start | bytes 1572868
  26.7 4.2 %collective-permute-start.13 = (bf16[128,128]{1,0:T(8,128)(2,1)S(1)}, bf16[128,128]{1,0:T(8,128)(2,1)S(1)}, u32[]{:S(2)}, u32[]{:S(2)}) collective-permute-start(bf16[128,128]{1,0:T(8,128)(2,1)S(1)} %get-tuple-element.142), channel_id=1, source_target_pairs={{0,4},{1,5},{2,6},{3,7},{4,0},{5,1},{6,2},{7,3},{8,12},{9,13},{10,... | collective-permute-start | bytes 98312 | tf_op jit(solution)/shard_map/ppermute | solution.py:191
  28.3 4.3 %collective-permute-start.14 = (bf16[128,128]{1,0:T(8,128)(2,1)S(1)}, bf16[128,128]{1,0:T(8,128)(2,1)S(1)}, u32[]{:S(2)}, u32[]{:S(2)}) collective-permute-start(bf16[128,128]{1,0:T(8,128)(2,1)S(1)} %get-tuple-element.141), channel_id=1, source_target_pairs={{0,7},{1,6},{2,5},{3,4},{4,3},{5,2},{6,1},{7,0},{8,15},{9,14},{10,... | collective-permute-start | bytes 98312 | tf_op jit(solution)/shard_map/ppermute | solution.py:191
  30.9 1.7 %copy-start.3 = (bf16[128,128]{1,0:T(8,128)(2,1)}, bf16[128,128]{1,0:T(8,128)(2,1)S(1)}, u32[]{:S(2)}) copy-start(bf16[128,128]{1,0:T(8,128)(2,1)S(1)} %collective-permute-done.10) | copy-start | bytes 98308
  32.6 6.6 %collective-permute-start.15 = (bf16[128,128]{1,0:T(8,128)(2,1)S(1)}, bf16[128,128]{1,0:T(8,128)(2,1)S(1)}, u32[]{:S(2)}, u32[]{:S(2)}) collective-permute-start(bf16[128,128]{1,0:T(8,128)(2,1)S(1)} %fusion.29), channel_id=1, source_target_pairs={{0,25},{1,24},{2,27},{3,26},{4,29},{5,28},{6,31},{7,30},{8,17},{9,... | collective-permute-start | bytes 98312 | tf_op jit(solution)/shard_map/ppermute | solution.py:191
  33.9 5.3 %copy-start.4 = (bf16[128,128]{1,0:T(8,128)(2,1)S(1)}, bf16[128,128]{1,0:T(8,128)(2,1)}, u32[]{:S(2)}) copy-start(bf16[128,128]{1,0:T(8,128)(2,1)} %copy-done.3) | copy-start | bytes 98308
  34.0 5.3 %collective-permute-start.16 = (bf16[128,128]{1,0:T(8,128)(2,1)S(1)}, bf16[128,128]{1,0:T(8,128)(2,1)S(1)}, u32[]{:S(2)}, u32[]{:S(2)}) collective-permute-start(bf16[128,128]{1,0:T(8,128)(2,1)S(1)} %fusion.29), channel_id=1, source_target_pairs={{0,9},{1,8},{2,11},{3,10},{4,13},{5,12},{6,15},{7,14},{8,1},{9,0},... | collective-permute-start | bytes 98312 | tf_op jit(solution)/shard_map/ppermute | solution.py:191
  35.3 3.9 %collective-permute-start.17 = (bf16[128,128]{1,0:T(8,128)(2,1)S(1)}, bf16[128,128]{1,0:T(8,128)(2,1)S(1)}, u32[]{:S(2)}, u32[]{:S(2)}) collective-permute-start(bf16[128,128]{1,0:T(8,128)(2,1)S(1)} %fusion.29), channel_id=1, source_target_pairs={{0,16},{1,17},{2,18},{3,19},{4,20},{5,21},{6,22},{7,23},{8,24},{9,... | collective-permute-start | bytes 98312 | tf_op jit(solution)/shard_map/ppermute | solution.py:191
  36.8 5.7 %collective-permute-start.21 = (bf16[2,640,128]{2,1,0:T(8,128)(2,1)S(1)}, bf16[2,640,128]{2,1,0:T(8,128)(2,1)S(1)}, u32[]{:S(2)}, u32[]{:S(2)}) collective-permute-start(bf16[2,640,128]{2,1,0:T(8,128)(2,1)S(1)} %get-tuple-element.108), channel_id=1, source_target_pairs={{0,1},{1,0},{2,3},{3,2},{4,5},{5,4},{6,7},{7,6},{8,9},{9,8},{10,11... | collective-permute-start | bytes 983048 | tf_op jit(solution)/shard_map/ppermute | solution.py:191
  36.8 5.7 %collective-permute-start.22 = (bf16[2,640,128]{2,1,0:T(8,128)(2,1)S(1)}, bf16[2,640,128]{2,1,0:T(8,128)(2,1)S(1)}, u32[]{:S(2)}, u32[]{:S(2)}) collective-permute-start(bf16[2,640,128]{2,1,0:T(8,128)(2,1)S(1)} %get-tuple-element.110), channel_id=1, source_target_pairs={{0,1},{1,0},{2,3},{3,2},{4,5},{5,4},{6,7},{7,6},{8,9},{9,8},{10,11... | collective-permute-start | bytes 983048 | tf_op jit(solution)/shard_map/ppermute | solution.py:191
  39.3 5.0 %collective-permute-start.18 = (bf16[128,128]{1,0:T(8,128)(2,1)S(1)}, bf16[128,128]{1,0:T(8,128)(2,1)S(1)}, u32[]{:S(2)}, u32[]{:S(2)}) collective-permute-start(bf16[128,128]{1,0:T(8,128)(2,1)S(1)} %get-tuple-element.133), channel_id=1, source_target_pairs={{0,3},{1,2},{2,1},{3,0},{4,7},{5,6},{6,5},{7,4},{8,11},{9,10},{10,... | collective-permute-start | bytes 98312 | tf_op jit(solution)/shard_map/ppermute | solution.py:191
  40.5 4.0 %collective-permute-start.19 = (bf16[128,128]{1,0:T(8,128)(2,1)S(1)}, bf16[128,128]{1,0:T(8,128)(2,1)S(1)}, u32[]{:S(2)}, u32[]{:S(2)}) collective-permute-start(bf16[128,128]{1,0:T(8,128)(2,1)S(1)} %get-tuple-element.138), channel_id=1, source_target_pairs={{0,4},{1,5},{2,6},{3,7},{4,0},{5,1},{6,2},{7,3},{8,12},{9,13},{10,... | collective-permute-start | bytes 98312 | tf_op jit(solution)/shard_map/ppermute | solution.py:191
  40.6 4.3 %collective-permute-start.20 = (bf16[128,128]{1,0:T(8,128)(2,1)S(1)}, bf16[128,128]{1,0:T(8,128)(2,1)S(1)}, u32[]{:S(2)}, u32[]{:S(2)}) collective-permute-start(bf16[128,128]{1,0:T(8,128)(2,1)S(1)} %get-tuple-element.132), channel_id=1, source_target_pairs={{0,7},{1,6},{2,5},{3,4},{4,3},{5,2},{6,1},{7,0},{8,15},{9,14},{10,... | collective-permute-start | bytes 98312 | tf_op jit(solution)/shard_map/ppermute | solution.py:191
  45.0 1.7 %collective-permute-start.23 = (bf16[4,128,128]{2,1,0:T(8,128)(2,1)S(1)}, bf16[4,128,128]{2,1,0:T(8,128)(2,1)S(1)}, u32[]{:S(2)}, u32[]{:S(2)}) collective-permute-start(bf16[4,128,128]{2,1,0:T(8,128)(2,1)S(1)} %get-tuple-element.131), channel_id=1, source_target_pairs={{0,1},{1,0},{2,3},{3,2},{4,5},{5,4},{6,7},{7,6},{8,9},{9,8},{10,11... | collective-permute-start | bytes 393224 | tf_op jit(solution)/shard_map/ppermute | solution.py:191
